TPU v7x, 32 devices: a whole 2x2x4 slice. The times are simulated.
32 devices in a mesh: sta: 16 (over z, y, x), win: 2 (over core).
Axes of the slice: x: 2, y: 2, z: 4, core: 2. Of those that a mesh axis runs over, the one named last changes fastest.
Arguments:
- spectra: float32 [4, 64, 2, 3, 1664], P('win', 'sta')
- flags: int32 [4, 64], P('win', 'sta'), may hold values 0 or 1
- owners: int32 [4], replicated, may hold values from 0 to 15, as said below
- source_slots: int32 [4, 4], replicated, may hold values from 0 to 3, as said below
Outputs:
- correlations: float32 [4, 4, 3, 64, 3, 768], P(None, None, None, 'sta')
Inputs may be any that keep to these rules, and one draw needn't show every extreme that they name: `owners`: the index of a block of 4 stations along sta. `source_slots`: distinct within a step.
All inputs are finite; a program needn't handle non-finite values. No bound on the sum of `flags` on one device may be relied on, other than what follows from the above.
Results may differ from a plain program's by a relative error of at most 0.0037.
Values sent between devices are 32-bit elements; how exact they have to be, the bound alone decides.
No kernel may reach another device: no remote copies, remote signals or barrier semaphores. Data moves between devices by JAX's collectives and lax.ppermute only.
A program may use at most 64 MiB of HBM per device.

v0:
```python
import math

import jax
import jax.numpy as jnp
from jax import lax
from jax.sharding import PartitionSpec as P

NLAG = 768
STEPS = 4


def spread(value, axis, source):
    kept = jnp.where(lax.axis_index(axis) == source, value, 0).astype(value.dtype)
    return lax.psum(kept, axis)


def whiten(spectra):
    shape = spectra.shape
    blocks = spectra.reshape(shape[0], shape[1], 2, 3, shape[4] // 64, 64)
    power = jnp.mean(blocks * blocks, axis=(2, 3, 5), keepdims=True)
    return (blocks / jnp.sqrt(power + 1e-06)).reshape(shape)


def lag_table(bins, lags, windows):
    freq = jnp.arange(bins, dtype=jnp.int32) + 360
    shift = jnp.arange(lags, dtype=jnp.int32) - lags // 2
    phase = jnp.mod(freq[:, None] * shift[None, :], 7200).astype(jnp.float32) * (
        2.0 * math.pi / 7200.0
    )
    scale = 1.0 / math.sqrt(windows * bins)
    return jnp.concatenate([jnp.cos(phase) * scale, -jnp.sin(phase) * scale], axis=0).astype(
        jnp.bfloat16
    )


def correlate(picked, receivers, table):
    src_re = picked[:, :, 0][:, :, :, None, None, :]
    src_im = picked[:, :, 1][:, :, :, None, None, :]
    rec_re = receivers[:, :, 0][:, None, None, :, :, :]
    rec_im = receivers[:, :, 1][:, None, None, :, :, :]
    real = jnp.sum(src_re * rec_re + src_im * rec_im, axis=0)
    imag = jnp.sum(src_im * rec_re - src_re * rec_im, axis=0)
    shape = real.shape
    bins = shape[4]
    rows = jnp.concatenate([real.reshape(-1, bins), imag.reshape(-1, bins)], axis=1).astype(
        jnp.bfloat16
    )
    lagged = jnp.dot(rows, table, preferred_element_type=jnp.float32)
    return lagged.reshape(shape[0], shape[1], shape[2], shape[3], table.shape[1])


def on_device(spectra, flags, owners, source_slots):
    win_count = spectra.shape[0]
    bins = spectra.shape[4]
    weighted = whiten(spectra) * flags.astype(jnp.float32)[:, :, None, None, None]
    table = lag_table(bins, NLAG, win_count * lax.axis_size("win"))
    outputs = []
    for step in range(STEPS):
        chosen = jnp.take(weighted, source_slots[step], axis=1)
        picked = spread(chosen, "sta", owners[step])
        partial_stack = correlate(picked, weighted, table)
        partial_stack = lax.psum(partial_stack, "win")
        outputs.append(partial_stack)
    stacked = jnp.stack(outputs)
    return stacked


def solution(mesh):
    return jax.shard_map(
        on_device,
        mesh=mesh,
        in_specs=(P("win", "sta", None, None, None), P("win", "sta"), P(), P()),
        out_specs=P(None, None, None, "sta", None, None),
        check_vma=False,
    )
```

profile of v0, /device:TPU:0, one launch (start us, length us, event | category | flops | bytes accessed | tf_op | source)
XLA Modules:
  0.0 230.7 jit_solution(157746877808956636)
XLA Ops:
  7.2 1.5 fusion.30
  12.1 1.2 multiply_reduce_fusion
  18.6 1.2 bitcast_select_fusion
  19.8 1.2 bitcast_select_fusion.2
  21.5 23.4 %multiply_convert_fusion.1 = (bf16[1664,768]{1,0:T(8,128)(2,1)S(1)}, bf16[1664,768]{1,0:T(8,128)(2,1)}) fusion(s32[768]{0:T(1024)S(1)} %iota_add_fusion.1, s32[1664]{0:T(1024)S(1)} %iota_add_fusion), kind=kLoop, calls=%fused_computation.9 | loop fusion | flops 17891328 | bytes 5121536 | tf_op jit(solution)/shard_map/convert.12
  45.0 94.1 %all-reduce.5.cloned.1.call-done = (f32[2,4,2,3,1664]{4,2,3,0,1:T(2,128)}, f32[2,4,2,3,1664]{4,2,3,0,1:T(2,128)}, f32[2,4,2,3,1664]{4,2,3,0,1:T(2,128)}, f32[2,4,2,3,1664]{4,2,3,0,1:T(2,128)}) async-done(((f32[2,4,2,3,1664]{4,2,3,0,1:T(2,128)}, f32[2,4,2,3,1664]{4,2,3,0,1:T(2,128)}, f32[2,4,2,3,1664]{4,2,3,0,1:T(2,128)}, f32[2,4,2,3,1664]{4,2,3,0,1:T(2,128)}), (f32[2,4,2,3,1664]{4,2,3,0,1:T(2,128)}, ...) | async-done | bytes 1277968 | tf_op jit(solution)/shard_map/psum | solution.py:14
  139.0 1.4 fusion.28
  140.6 1.3 fusion.27
  142.9 14.1 %add_reduce_fusion.3 = (bf16[4,3,4,3,1664]{4,2,3,1,0:T(4,128)(2,1)S(1)}, bf16[4,3,4,3,1664]{4,2,3,1,0:T(4,128)(2,1)}, bf16[4,3,4,3,1664]{4,2,3,1,0:T(4,128)(2,1)...) fusion(f32[2,4,3,1664]{3,1,2,0:T(4,128)S(1)} %get-tuple-element, ...), kind=kLoop, calls=%fused_computation.22 | loop fusion | flops 13418496 | bytes 5431296 | tf_op jit(solution)/shard_map/reduce_sum | solution.py:41
  158.4 1.3 copy.45
  160.8 1.3 copy.51
  162.1 1.2 reshape.84
  163.3 1.3 copy.50
  164.6 1.2 reshape.83
  165.8 1.3 copy.57
  168.2 1.3 copy.56
  169.5 1.2 reshape.86
  170.7 1.3 copy.63
  171.9 1.2 reshape.90
  173.1 1.3 copy.62
  174.4 1.2 reshape.89
  175.6 3.8 %fusion.5 = f32[144,768]{1,0:T(8,128)} fusion(bf16[144,1664]{1,0:T(8,128)(2,1)} %reshape.81, bf16[144,1664]{1,0:T(8,128)(2,1)} %reshape.80, bf16[1664,768]{1,0:T(8,128)(2,1)} %get-tuple-element.47, bf16[1664,768]{1,0:T(8,128)(2,1)S(1)} %get-tuple-element.46), kind=kOutput, calls=%fused_computation.23 | convolution fusion | flops 748240896 | bytes 6512640 | tf_op jit(solution)/shard_map/dot_general | solution.py:48
  179.4 2.0 stack.15
  181.4 3.4 %fusion.17 = f32[144,768]{1,0:T(8,128)} fusion(bf16[144,1664]{1,0:T(8,128)(2,1)S(1)} %copy-done.2, bf16[144,1664]{1,0:T(8,128)(2,1)S(1)} %copy-done.3, bf16[1664,768]{1,0:T(8,128)(2,1)} %get-tuple-element.47, bf16[1664,768]{1,0:T(8,128)(2,1)S(1)} %get-tuple-element.46), kind=kOutput, calls=%fused_computation.35 | convolution fusion | flops 748240896 | bytes 6512640 | tf_op jit(solution)/shard_map/dot_general | solution.py:48
  184.8 2.0 stack.18
  186.9 3.8 %fusion.13 = f32[144,768]{1,0:T(8,128)} fusion(bf16[144,1664]{1,0:T(8,128)(2,1)} %reshape.87, bf16[144,1664]{1,0:T(8,128)(2,1)} %reshape.86, bf16[1664,768]{1,0:T(8,128)(2,1)} %get-tuple-element.47, bf16[1664,768]{1,0:T(8,128)(2,1)S(1)} %get-tuple-element.46), kind=kOutput, calls=%fused_computation.31 | convolution fusion | flops 748240896 | bytes 6512640 | tf_op jit(solution)/shard_map/dot_general | solution.py:48
  190.7 2.0 stack.17
  192.7 3.4 %fusion.9 = f32[144,768]{1,0:T(8,128)} fusion(bf16[144,1664]{1,0:T(8,128)(2,1)S(1)} %copy-done, bf16[144,1664]{1,0:T(8,128)(2,1)S(1)} %copy-done.1, bf16[1664,768]{1,0:T(8,128)(2,1)} %get-tuple-element.47, bf16[1664,768]{1,0:T(8,128)(2,1)S(1)} %get-tuple-element.46), kind=kOutput, calls=%fused_computation.27 | convolution fusion | flops 748240896 | bytes 6512640 | tf_op jit(solution)/shard_map/dot_general | solution.py:48
  196.1 2.0 stack.16
  198.1 21.8 %all-reduce.7.cloned.1.call-done = (f32[1,4,3,4,3,768]{5,4,3,2,1,0:T(4,128)}, f32[1,4,3,4,3,768]{5,4,3,2,1,0:T(4,128)}, f32[1,4,3,4,3,768]{5,4,3,2,1,0:T(4,128)}, f32[1,4,3,4,3,768]{5,4,3,2,1,0:T(4,128)}) async-done(((f32[1,4,3,4,3,768]{5,4,3,2,1,0:T(4,128)}, f32[1,4,3,4,3,768]{5,4,3,2,1,0:T(4,128)}, f32[1,4,3,4,3,768]{5,4,3,2,1,0:T(4,128)}, f32[1,4,3,4,3,768]{5,4,3,2,1,0:T(4,128)}), ...) | async-done | bytes 1769488 | tf_op jit(solution)/shard_map/psum | solution.py:62
  219.9 2.2 pad_maximum_fusion.1
  222.2 1.7 copy.64
  (50 shorter events, 11.9 us)
Async XLA Ops:
  6.5 132.5 %all-reduce.5.cloned.1.call-start = ((), (), s32[]{:S(2)}) async-start(), calls=%async_computation | async-start | bytes 2555904 | tf_op jit(solution)/shard_map/psum | solution.py:14
  21.1 198.8 %all-reduce.7.cloned.1.call-start = ((), (), s32[]{:S(2)}) async-start(), calls=%async_computation.1 | async-start | bytes 4718592 | tf_op jit(solution)/shard_map/psum | solution.py:62
  139.0 3.0 %copy-start.5 = (f32[2,4,2,3,1664]{4,2,3,0,1:T(2,128)S(1)}, f32[2,4,2,3,1664]{4,2,3,0,1:T(2,128)}, u32[]{:S(2)}) copy-start(f32[2,4,2,3,1664]{4,2,3,0,1:T(2,128)} %get-tuple-element.22) | copy-start | bytes 958468
  139.0 3.4 %copy-start.4 = (f32[2,4,2,3,1664]{4,2,3,0,1:T(2,128)S(1)}, f32[2,4,2,3,1664]{4,2,3,0,1:T(2,128)}, u32[]{:S(2)}) copy-start(f32[2,4,2,3,1664]{4,2,3,0,1:T(2,128)} %get-tuple-element.23) | copy-start | bytes 958468
  175.6 5.8 %copy-start.2 = (bf16[144,1664]{1,0:T(8,128)(2,1)S(1)}, bf16[144,1664]{1,0:T(8,128)(2,1)}, u32[]{:S(2)}) copy-start(bf16[144,1664]{1,0:T(8,128)(2,1)} %reshape.90) | copy-start | bytes 1437700
  175.6 5.8 %copy-start.3 = (bf16[144,1664]{1,0:T(8,128)(2,1)S(1)}, bf16[144,1664]{1,0:T(8,128)(2,1)}, u32[]{:S(2)}) copy-start(bf16[144,1664]{1,0:T(8,128)(2,1)} %reshape.89) | copy-start | bytes 1437700
  186.9 5.8 %copy-start = (bf16[144,1664]{1,0:T(8,128)(2,1)S(1)}, bf16[144,1664]{1,0:T(8,128)(2,1)}, u32[]{:S(2)}) copy-start(bf16[144,1664]{1,0:T(8,128)(2,1)} %reshape.84) | copy-start | bytes 1437700
  186.9 5.8 %copy-start.1 = (bf16[144,1664]{1,0:T(8,128)(2,1)S(1)}, bf16[144,1664]{1,0:T(8,128)(2,1)}, u32[]{:S(2)}) copy-start(bf16[144,1664]{1,0:T(8,128)(2,1)} %reshape.83) | copy-start | bytes 1437700
Sparse Core Ops, SparseCore 0:
  21.2 117.7 all-reduce.4
  198.2 21.6 all-reduce.6
where the time goes:
time: 232 us; the launch traced here: 231 us
  waiting for transfers between devices  116 us (50%)
  other arithmetic  46.3 us (20%)
  local copies, waits for them, and re-layouts  37.7 us (16%)
  between operations  16.2 us (7%)
  matrix products  14.4 us (6%)
    psum x1, waiting for transfers between devices, spread(): return lax.psum(kept, axis)  94.1 us
    another operation x1, other arithmetic  23.4 us
    psum x1, waiting for transfers between devices, on_device(): partial_stack = lax.psum(partial_stack, 'win')  21.8 us
    dot_general x4, matrix products, correlate(): lagged = jnp.dot(rows, table, preferred_element_type=jnp.float32)  14.4 us
    reduce_sum x1, other arithmetic, correlate(): real = jnp.sum(src_re * rec_re + src_im * rec_im, axis=0)  14.1 us
    another operation x5, local copies, waits for them, and re-layouts, on_device(): stacked = jnp.stack(outputs)  9.7 us
    another operation x8, local copies, waits for them, and re-layouts  9.15 us
    reshape x4, local copies, waits for them, and re-layouts, correlate(): real.reshape(-1, bins)  4.74 us
  transfers between devices with their start and end apart: 2, of which 2 were waited for; matrix products, arithmetic and copies ran while one was open for 10% of the time, Pallas kernels for 0%

commit v1 on v0

v1 whole, which is shorter than its diff:
```python
import functools
import math

import jax
import jax.numpy as jnp
import numpy as np
from jax import lax
from jax.experimental import pallas as pl
from jax.experimental.pallas import tpu as pltpu
from jax.sharding import PartitionSpec as P

NLAG = 768
LANES = 128
VMEM = 40 * 1024 * 1024


def lag_table(bins, lags, windows):
    freq = np.arange(bins, dtype=np.int64) + 360
    shift = np.arange(lags, dtype=np.int64) - lags // 2
    phase = np.mod(freq[:, None] * shift[None, :], 7200).astype(np.float32) * np.float32(
        2.0 * math.pi / 7200.0
    )
    scale = np.float32(1.0 / math.sqrt(windows * bins))
    real = (np.cos(phase) * scale).reshape(bins // LANES, 1, LANES, lags)
    imag = (-np.sin(phase) * scale).reshape(bins // LANES, 1, LANES, lags)
    return np.concatenate([real, imag], axis=1).reshape(2 * bins, lags).astype(jnp.bfloat16)


def whiten_kernel(flags, x_ref, pieces_ref, rec_ref):
    wins, stas, comps, _, bins = x_ref.shape
    tiles = bins // LANES
    lane = lax.broadcasted_iota(jnp.int32, (wins * stas, LANES), 1)
    left = lane < 64
    sums = []
    for w in range(wins):
        for s in range(stas):
            x = x_ref[w, s]
            sums.append(jnp.sum(jnp.sum(x * x, axis=0), axis=0, keepdims=True))
    power = jnp.concatenate(sums, axis=0)
    weight = jnp.concatenate(
        [
            jnp.full((1, LANES), flags[w, s].astype(jnp.float32), jnp.float32)
            for w in range(wins)
            for s in range(stas)
        ],
        axis=0,
    )
    scales = []
    for c in range(tiles):
        tile = power[:, c * LANES : (c + 1) * LANES]
        low = jnp.sum(jnp.where(left, tile, 0.0), axis=1, keepdims=True)
        high = jnp.sum(jnp.where(left, 0.0, tile), axis=1, keepdims=True)
        mean = jnp.where(left, low, high) * (1.0 / (64 * 2 * comps))
        scales.append(weight / jnp.sqrt(mean + 1e-06))
    scale = jnp.concatenate(scales, axis=1)
    for w in range(wins):
        for s in range(stas):
            k = w * stas + s
            row = scale[k : k + 1]
            for i in range(comps):
                y = x_ref[w, s, i] * row
                for part in range(2):
                    rec_ref[w, part, pl.ds(i * stas + s, 1), :] = y[part : part + 1]
                    for c in range(tiles):
                        pieces_ref[(s * wins + w) * 2 + part, pl.ds(i * tiles + c, 1), :] = y[
                            part : part + 1, c * LANES : (c + 1) * LANES
                        ]
    rest = pieces_ref.shape[1] - comps * tiles
    if rest:
        for k in range(wins * stas * 2):
            pieces_ref[k, pl.ds(comps * tiles, rest), :] = jnp.zeros((rest, LANES), jnp.float32)
    spare = rec_ref.shape[2] - comps * stas
    if spare:
        for w in range(wins):
            for part in range(2):
                rec_ref[w, part, pl.ds(comps * stas, spare), :] = jnp.zeros(
                    (spare, bins), jnp.float32
                )


def whiten(spectra, flags):
    wins, stas, _, comps, bins = spectra.shape
    rows = -(-comps * (bins // LANES) // 8) * 8
    recs = -(-comps * stas // 8) * 8
    return pl.pallas_call(
        whiten_kernel,
        out_shape=(
            jax.ShapeDtypeStruct((wins * stas * 2, rows, LANES), jnp.float32),
            jax.ShapeDtypeStruct((wins, 2, recs, bins), jnp.float32),
        ),
        in_specs=[
            pl.BlockSpec(memory_space=pltpu.SMEM),
            pl.BlockSpec(memory_space=pltpu.VMEM),
        ],
        out_specs=(
            pl.BlockSpec(memory_space=pltpu.VMEM),
            pl.BlockSpec(memory_space=pltpu.VMEM),
        ),
        compiler_params=pltpu.CompilerParams(vmem_limit_bytes=VMEM),
        name="whiten",
    )(flags, jnp.transpose(spectra, (0, 1, 3, 2, 4)))


def pick_kernel(owners, core, got_ref, keep_ref, send_ref):
    for t in range(keep_ref.shape[0]):
        keep_ref[t] = got_ref[owners[2 * t + core[0]]]
        send_ref[t] = got_ref[owners[2 * t + 1 - core[0]]]


def pick(owners, core, got):
    steps = owners.shape[0]
    shape = jax.ShapeDtypeStruct((steps // 2,) + got.shape[1:], jnp.float32)
    smem = pl.BlockSpec(memory_space=pltpu.SMEM)
    vmem = pl.BlockSpec(memory_space=pltpu.VMEM)
    return pl.pallas_call(
        pick_kernel,
        out_shape=(shape, shape),
        in_specs=[smem, smem, vmem],
        out_specs=(vmem, vmem),
        name="pick",
    )(owners, core, got)


def correlate_kernel(
    slots, where, s0, s1, s2, s3, r0, r1, table_hbm, out_ref, src, rec, table, lhs, sems, tsem
):
    _, _, groups, steps, _, _ = src.shape
    wins = groups
    bins = r0.shape[3]
    tiles = bins // LANES
    place, z, core = where[0], where[1], where[2]
    spots = (place, place ^ (1 + core), place ^ (2 - core), place ^ 3)
    copies = [
        pltpu.make_async_copy(ref, src.at[spot], sems.at[n])
        for n, (ref, spot) in enumerate(zip((s0, s1, s2, s3), spots))
    ]
    table_copy = pltpu.make_async_copy(table_hbm, table, tsem)
    for copy in copies:
        copy.start()
    table_copy.start()
    for g, ref in enumerate((r0, r1)):
        for w in range(wins):
            for part in range(2):
                both = ref[w, part, 0:12, :]
                rec[g, w, part, 0:12, :] = both
                rec[g, w, part, 12:24, :] = both
    for copy in copies:
        copy.wait()
    upper = lax.broadcasted_iota(jnp.int32, (8, LANES), 0) < 4

    def chunk(c, carry):
        lanes = pl.ds(pl.multiple_of(c * LANES, LANES), LANES)
        receivers = [
            [[rec[g, w, part, :, lanes] for part in range(2)] for w in range(wins)]
            for g in range(groups)
        ]
        for block in range(steps * 12 // 4):
            real_tiles, imag_tiles = [], []
            for pair in range(2):
                numbers = (block * 4 + pair * 2, block * 4 + pair * 2 + 1)
                real = [None] * 3
                imag = [None] * 3
                for g in range(groups):
                    for w in range(wins):
                        spread = []
                        for part in range(2):
                            rows = []
                            for n in numbers:
                                t, s, i = n // 12, (n // 3) % 4, n % 3
                                line = src[
                                    w * 2 + part,
                                    slots[t, s] ^ z,
                                    g,
                                    t,
                                    pl.ds(i * tiles + c, 1),
                                    :,
                                ]
                                rows.append(jnp.broadcast_to(line, (8, LANES)))
                            spread.append((rows[0], jnp.where(upper, rows[0], rows[1]), rows[1]))
                        for k in range(3):
                            rr = receivers[g][w][0][8 * k : 8 * k + 8]
                            ri = receivers[g][w][1][8 * k : 8 * k + 8]
                            sr, si = spread[0][k], spread[1][k]
                            re = sr * rr + si * ri
                            im = si * rr - sr * ri
                            real[k] = re if real[k] is None else real[k] + re
                            imag[k] = im if imag[k] is None else imag[k] + im
                real_tiles += real
                imag_tiles += imag
            at = pl.ds(block * 48, 48)
            base = c * 2 * LANES
            lhs[at, pl.ds(pl.multiple_of(base, LANES), LANES)] = jnp.concatenate(
                real_tiles, axis=0
            ).astype(jnp.bfloat16)
            lhs[at, pl.ds(pl.multiple_of(base + LANES, LANES), LANES)] = jnp.concatenate(
                imag_tiles, axis=0
            ).astype(jnp.bfloat16)
        return carry

    lax.fori_loop(0, tiles, chunk, 0)
    table_copy.wait()
    for n in range(out_ref.shape[2] // 256):
        lags = pl.ds(n * 256, 256)
        result = jnp.dot(lhs[...], table[:, lags], preferred_element_type=jnp.float32)
        for k in range(out_ref.shape[0]):
            out_ref[k, :, lags] = result[4 * k : 4 * k + 4]


def correlate(slots, where, sources, own, other, table):
    steps = sources[0].shape[2]
    bins = own.shape[3]
    rows = steps * 4 * 3 * 12
    lags = table.shape[1]
    vmem = pl.BlockSpec(memory_space=pltpu.VMEM)
    smem = pl.BlockSpec(memory_space=pltpu.SMEM)
    hbm = pl.BlockSpec(memory_space=pltpu.HBM)
    return pl.pallas_call(
        correlate_kernel,
        out_shape=jax.ShapeDtypeStruct((rows // 4, 4, lags), jnp.float32),
        in_specs=[smem, smem] + [vmem] * 6 + [hbm],
        out_specs=vmem,
        scratch_shapes=[
            pltpu.VMEM((4,) + sources[0].shape, jnp.float32),
            pltpu.VMEM((2, 2, 2, 24, bins), jnp.float32),
            pltpu.VMEM(table.shape, jnp.bfloat16),
            pltpu.VMEM((rows, 2 * bins), jnp.bfloat16),
            pltpu.SemaphoreType.DMA((4,)),
            pltpu.SemaphoreType.DMA,
        ],
        compiler_params=pltpu.CompilerParams(vmem_limit_bytes=VMEM),
        name="correlate",
    )(slots, where, *sources, own, other, table)


def join_kernel(core, own, other, out, sems):
    half = own.shape[0]
    copies = []
    for t in range(half):
        copies.append(pltpu.make_async_copy(own.at[t], out.at[2 * t + core[0]], sems.at[2 * t]))
        copies.append(
            pltpu.make_async_copy(other.at[t], out.at[2 * t + 1 - core[0]], sems.at[2 * t + 1])
        )
    for copy in copies:
        copy.start()
    for copy in copies:
        copy.wait()


def join(core, own, other):
    vmem = pl.BlockSpec(memory_space=pltpu.VMEM)
    return pl.pallas_call(
        join_kernel,
        out_shape=jax.ShapeDtypeStruct((2 * own.shape[0],) + own.shape[1:], jnp.float32),
        in_specs=[pl.BlockSpec(memory_space=pltpu.SMEM), vmem, vmem],
        out_specs=pl.BlockSpec(memory_space=pltpu.HBM),
        scratch_shapes=[pltpu.SemaphoreType.DMA((2 * own.shape[0],))],
        name="join",
    )(core, own, other)


def swap(value):
    return lax.ppermute(value, "win", [(0, 1), (1, 0)])


def on_device(spectra, flags, owners, source_slots):
    wins, stas, _, comps, bins = spectra.shape
    steps, sources = source_slots.shape
    place = lax.axis_index("sta") % 4
    z = lax.axis_index("sta") // 4
    core = lax.axis_index("win")
    core_arg = core.astype(jnp.int32)[None]
    blocks = lax.axis_size("sta")
    pieces, own = whiten(spectra, flags)
    other = swap(own)
    got = lax.all_to_all(pieces, "sta", 0, 0)
    keep, send = pick(owners, core_arg, got)
    mine = jnp.stack([keep, swap(send)])

    def partner(bits):
        return [(i, i ^ bits) for i in range(blocks)]

    def by_core(first, second):
        bits = (first, second)
        return [(2 * i + c, 2 * (i ^ bits[c]) + c) for i in range(blocks) for c in range(2)]

    column = jnp.stack([mine] + [lax.ppermute(mine, "sta", partner(4 * k)) for k in (1, 2, 3)])
    near = lax.ppermute(column, ("sta", "win"), by_core(1, 2))
    next_ = lax.ppermute(column, ("sta", "win"), by_core(2, 1))
    far = lax.ppermute(near, ("sta", "win"), by_core(2, 1))
    slots = lax.dynamic_slice(
        source_slots.reshape(steps // 2, 2, sources), (0, core, 0), (steps // 2, 1, sources)
    )[:, 0]
    where = jnp.stack([place, z, core]).astype(jnp.int32)
    table = jnp.asarray(lag_table(bins, NLAG, wins * lax.axis_size("win")))
    half = correlate(slots, where, (column, near, next_, far), own, other, table)
    half = half.reshape(steps // 2, -1, 4, NLAG)
    whole = join(core_arg, half, swap(half))
    return whole.reshape(steps, sources, comps, comps, stas, NLAG).transpose(0, 1, 2, 4, 3, 5)


def spread(value, axis, source):
    kept = jnp.where(lax.axis_index(axis) == source, value, 0).astype(value.dtype)
    return lax.psum(kept, axis)


def cross(picked, receivers, table):
    src_re = picked[:, :, 0][:, :, :, None, None, :]
    src_im = picked[:, :, 1][:, :, :, None, None, :]
    rec_re = receivers[:, :, 0][:, None, None, :, :, :]
    rec_im = receivers[:, :, 1][:, None, None, :, :, :]
    real = jnp.sum(src_re * rec_re + src_im * rec_im, axis=0)
    imag = jnp.sum(src_im * rec_re - src_re * rec_im, axis=0)
    shape = real.shape
    both = jnp.stack(
        [part.reshape(shape[:4] + (shape[4] // LANES, LANES)) for part in (real, imag)], axis=5
    )
    rows = both.reshape(-1, 2 * shape[4]).astype(jnp.bfloat16)
    lagged = jnp.dot(rows, table, preferred_element_type=jnp.float32)
    return lagged.reshape(shape[:4] + (table.shape[1],))


def on_device_general(spectra, flags, owners, source_slots):
    shape = spectra.shape
    blocks = spectra.reshape(shape[:4] + (shape[4] // 64, 64))
    power = jnp.mean(blocks * blocks, axis=(2, 3, 5), keepdims=True)
    whitened = (blocks / jnp.sqrt(power + 1e-06)).reshape(shape)
    weighted = whitened * flags.astype(jnp.float32)[:, :, None, None, None]
    table = jnp.asarray(lag_table(shape[4], NLAG, shape[0] * lax.axis_size("win")))
    outputs = []
    for step in range(source_slots.shape[0]):
        chosen = jnp.take(weighted, source_slots[step], axis=1)
        picked = spread(chosen, "sta", owners[step])
        outputs.append(lax.psum(cross(picked, weighted, table), "win"))
    return jnp.stack(outputs)


def solution(mesh):
    small = mesh.shape["sta"] == 16 and mesh.shape["win"] == 2
    return jax.shard_map(
        on_device if small else on_device_general,
        mesh=mesh,
        in_specs=(P("win", "sta", None, None, None), P("win", "sta"), P(), P()),
        out_specs=P(None, None, None, "sta", None, None),
        check_vma=False,
    )
```

time: 232 us -> 69.5 us (0.30)
  waiting for transfers between devices: 116 us -> 35.5 us
  other arithmetic: 46.3 us -> 0.89 us
  local copies, waits for them, and re-layouts: 37.7 us -> 5.83 us
  between operations: 16.2 us -> 0.08 us
  starting transfers between devices: 0.04 us -> 15 us
  matrix products: 14.4 us -> 0 us
  Pallas kernels: 0 us -> 11.8 us
    psum x2 -> x0, waiting for transfers between devices: 116 us -> none  [the longest x1 94.1 us: spread(): return lax.psum(kept, axis)]
    another operation x2 -> x3, other arithmetic: 25.7 us -> 0.89 us  [the longest x2 0.81 us: on_device(): jnp.stack([mine] + [lax.ppermute(mine, 'sta', partner(4 * k)) for k in (1...]
    ppermute x0 -> x9, waiting for transfers between devices: none -> 24.2 us  [the longest x1 9.13 us: on_device(): near = lax.ppermute(column, ('sta', 'win'), by_core(1, 2))]
    another operation x13 -> x0, local copies, waits for them, and re-layouts: 18.9 us -> none  [the longest x5 9.7 us: on_device(): stacked = jnp.stack(outputs)]
    reduce_sum x3 -> x0, other arithmetic: 15.4 us -> none  [the longest x1 14.1 us: correlate(): real = jnp.sum(src_re * rec_re + src_im * rec_im, axis=0)]
    dot_general x4 -> x0, matrix products: 14.4 us -> none  [correlate(): lagged = jnp.dot(rows, table, preferred_element_type=jnp.float32)]
    pallas_call x0 -> x4, Pallas kernels: none -> 11.8 us  [the longest x1 5.68 us: correlate(): pl.pallas_call(correlate_kernel, out_shape=jax.ShapeDtypeStruct((rows //...]
    all_to_all x0 -> x1, waiting for transfers between devices: none -> 11.3 us  [on_device(): got = lax.all_to_all(pieces, 'sta', 0, 0)]
  transfers between devices with their start and end apart: 2 -> 10, of which waited for: 2 -> 6; matrix products, arithmetic and copies ran while one was open for 10% -> 0% of each run, Pallas kernels for 0% -> 0%
where the time goes in v1:
time: 69.5 us; the launch traced here: 69.1 us
  waiting for transfers between devices  35.5 us (51%)
  starting transfers between devices  15 us (22%)
  Pallas kernels  11.8 us (17%)
  local copies, waits for them, and re-layouts  5.83 us (8%)
  other arithmetic  0.89 us (1%)
    all_to_all x1, waiting for transfers between devices, on_device(): got = lax.all_to_all(pieces, 'sta', 0, 0)  11.3 us
    ppermute x1, waiting for transfers between devices, on_device(): near = lax.ppermute(column, ('sta', 'win'), by_core(1, 2))  9.13 us
    all_to_all x1, starting transfers between devices, on_device(): got = lax.all_to_all(pieces, 'sta', 0, 0)  8.31 us
    ppermute x1, waiting for transfers between devices, on_device(): far = lax.ppermute(near, ('sta', 'win'), by_core(2, 1))  6.18 us
    unnamed x14, local copies, waits for them, and re-layouts  5.83 us
    pallas_call x1, Pallas kernels, correlate(): pl.pallas_call(correlate_kernel, out_shape=jax.ShapeDtypeStruct((rows //...  5.68 us
    ppermute x3, waiting for transfers between devices, on_device(): lax.ppermute(mine, 'sta', partner(4 * k))  5.05 us
    ppermute x3, starting transfers between devices, on_device(): lax.ppermute(mine, 'sta', partner(4 * k))  4.45 us
  transfers between devices with their start and end apart: 10, of which 6 were waited for; matrix products, arithmetic and copies ran while one was open for 0% of the time, Pallas kernels for 0%

profile of v1, /device:TPU:0, one launch (start us, length us, event | category | flops | bytes accessed | tf_op | source)
XLA Modules:
  0.0 69.1 jit_solution(11729519339829328139)
XLA Ops:
  0.0 1.0 %copy-done.3 = f32[2,4,2,3,1664]{4,2,3,1,0:T(2,128)S(1)} copy-done((f32[2,4,2,3,1664]{4,2,3,1,0:T(2,128)S(1)}, f32[2,4,2,3,1664]{4,2,3,1,0:T(2,128)}, u32[]{:S(2)}) %copy-start.3) | copy-done | bytes 319512
  1.0 0.7 copy-done.4
  1.7 1.8 %whiten.1 = (f32[16,40,128]{2,1,0:T(8,128)}, f32[2,2,16,1664]{3,2,1,0:T(8,128)S(1)}) custom-call(s32[2,4]{1,0:T(2,128)S(1)} %copy-done.4, f32[2,4,3,2,1664]{4,3,2,1,0:T(2,128)S(1)} %bitcast.20), custom_call_target="tpu_custom_call" | custom-call | tf_op jit(solution)/shard_map/whiten/pallas_call | solution.py:85
  3.4 8.3 %all-to-all-start = ((f32[16,40,128]{2,1,0:T(8,128)}), f32[16,40,128]{2,1,0:T(8,128)S(1)}, u32[]{:S(2)}, u32[]{:S(2)}) async-start(f32[16,40,128]{2,1,0:T(8,128)} %get-tuple-element.9), calls=%async_computation | async-start | bytes 655360 | tf_op jit(solution)/shard_map/all_to_all | solution.py:275
  11.8 11.3 %all-to-all-done.got_ref = f32[16,40,128]{2,1,0:T(8,128)S(1)} async-done(((f32[16,40,128]{2,1,0:T(8,128)}), f32[16,40,128]{2,1,0:T(8,128)S(1)}, u32[]{:S(2)}, u32[]{:S(2)}) %all-to-all-start) | async-done | bytes 327712 | tf_op jit(solution)/shard_map/all_to_all | solution.py:275
  23.1 0.7 %copy-done.5 = f32[16,40,128]{2,1,0:T(8,128)} copy-done((f32[16,40,128]{2,1,0:T(8,128)}, f32[16,40,128]{2,1,0:T(8,128)S(1)}, u32[]{:S(2)}) %copy-start.5) | copy-done | bytes 327704
  23.8 1.6 %pick.1 = (f32[2,40,128]{2,1,0:T(8,128)}, f32[2,40,128]{2,1,0:T(8,128)}) custom-call(s32[4]{0:T(128)} %owners.1, s32[1]{0:T(128)} %bitcast.core, f32[16,40,128]{2,1,0:T(8,128)} %copy-done.5), custom_call_target="tpu_custom_call" | custom-call | tf_op jit(solution)/shard_map/pick/pallas_call | solution.py:115
  25.4 0.0 collective-permute-start
  25.4 1.4 %collective-permute-done = f32[2,40,128]{2,1,0:T(8,128)S(1)} collective-permute-done((f32[2,40,128]{2,1,0:T(8,128)}, f32[2,40,128]{2,1,0:T(8,128)S(1)}, u32[]{:S(2)}, u32[]{:S(2)}) %collective-permute-start) | collective-permute-done | bytes 40992 | tf_op jit(solution)/shard_map/ppermute | solution.py:262
  26.9 0.8 %fusion = (f32[1,2,2,40,128]{4,3,2,1,0:T(8,128)S(1)}, f32[2,2,40,128]{3,2,1,0:T(8,128)S(1)}) fusion(f32[1,2,40,128]{3,2,1,0:T(8,128)S(1)} %bitcast.26, f32[1,2,40,128]{3,2,1,0:T(8,128)} %bitcast.25), kind=kLoop, calls=%fused_computation.4 | loop fusion | flops 20480 | bytes 245760 | tf_op jit(solution)/shard_map/stack | solution.py:286
  27.7 0.4 collective-permute-start.2
  28.1 1.9 %collective-permute-start.1 = (f32[2,2,40,128]{3,2,1,0:T(8,128)S(1)}, f32[2,2,40,128]{3,2,1,0:T(8,128)S(1)}, u32[]{:S(2)}, u32[]{:S(2)}) collective-permute-start(f32[2,2,40,128]{3,2,1,0:T(8,128)S(1)} %get-tuple-element.14), channel_id=1, source_target_pairs={{0,8},{2,10},{4,12},{6,14},{8,0},{10,2},{12,4},{14,6},{16,24},{18,... | collective-permute-start | bytes 245768 | tf_op jit(solution)/shard_map/ppermute | solution.py:286
  30.0 2.1 %collective-permute-start.3 = (f32[2,2,40,128]{3,2,1,0:T(8,128)S(1)}, f32[2,2,40,128]{3,2,1,0:T(8,128)S(1)}, u32[]{:S(2)}, u32[]{:S(2)}) collective-permute-start(f32[2,2,40,128]{3,2,1,0:T(8,128)S(1)} %get-tuple-element.14), channel_id=1, source_target_pairs={{0,24},{2,26},{4,28},{6,30},{8,16},{10,18},{12,20},{14,22},{16,8},... | collective-permute-start | bytes 245768 | tf_op jit(solution)/shard_map/ppermute | solution.py:286
  32.1 5.0 %collective-permute-done.2 = f32[2,2,40,128]{3,2,1,0:T(8,128)S(1)} collective-permute-done((f32[2,2,40,128]{3,2,1,0:T(8,128)S(1)}, f32[2,2,40,128]{3,2,1,0:T(8,128)S(1)}, u32[]{:S(2)}, u32[]{:S(2)}) %collective-permute-start.2) | collective-permute-done | bytes 81952 | tf_op jit(solution)/shard_map/ppermute | solution.py:286
  37.2 0.0 collective-permute-done.1
  37.2 0.0 collective-permute-done.3
  37.2 0.6 collective-permute-start.4
  37.8 0.0 collective-permute-start.7
  37.8 0.8 %collective-permute-start.5 = (f32[4,2,2,40,128]{4,3,2,1,0:T(8,128)S(1)}, f32[4,2,2,40,128]{4,3,2,1,0:T(8,128)S(1)}, u32[]{:S(2)}, u32[]{:S(2)}) collective-permute-start(f32[4,2,2,40,128]{4,3,2,1,0:T(8,128)S(1)} %pad_maximum_fusion.s0), channel_id=1, source_target_pairs={{0,4},{1,3},{2,6},{3,1},{4,0},{5,7},{6,2},{7,5},{8,12},{9,11},{10,... | collective-permute-start | bytes 983048 | tf_op jit(solution)/shard_map/ppermute | solution.py:288
  38.6 9.1 %collective-permute-done.4.s1 = f32[4,2,2,40,128]{4,3,2,1,0:T(8,128)S(1)} collective-permute-done((f32[4,2,2,40,128]{4,3,2,1,0:T(8,128)S(1)}, f32[4,2,2,40,128]{4,3,2,1,0:T(8,128)S(1)}, u32[]{:S(2)}, u32[]{:S(2)}) %collective-permute-start.4) | collective-permute-done | bytes 327712 | tf_op jit(solution)/shard_map/ppermute | solution.py:287
  47.7 0.8 %collective-permute-start.6 = (f32[4,2,2,40,128]{4,3,2,1,0:T(8,128)S(1)}, f32[4,2,2,40,128]{4,3,2,1,0:T(8,128)S(1)}, u32[]{:S(2)}, u32[]{:S(2)}) collective-permute-start(f32[4,2,2,40,128]{4,3,2,1,0:T(8,128)S(1)} %collective-permute-done.4.s1), channel_id=1, source_target_pairs={{0,4},{1,3},{2,6},{3,1},{4,0},{5,7},{6,2},{7,5},{8,12},{9,11},{10,... | collective-permute-start | bytes 983048 | tf_op jit(solution)/shard_map/ppermute | solution.py:289
  48.5 0.1 pad_add_fusion.where
  48.6 0.0 collective-permute-done.7.r1
  48.6 0.0 collective-permute-done.5.s2
  48.6 6.2 %collective-permute-done.6.s3 = f32[4,2,2,40,128]{4,3,2,1,0:T(8,128)S(1)} collective-permute-done((f32[4,2,2,40,128]{4,3,2,1,0:T(8,128)S(1)}, f32[4,2,2,40,128]{4,3,2,1,0:T(8,128)S(1)}, u32[]{:S(2)}, u32[]{:S(2)}) %collective-permute-start.6) | collective-permute-done | bytes 327712 | tf_op jit(solution)/shard_map/ppermute | solution.py:289
  54.8 2.4 %copy-done.1 = bf16[3328,768]{1,0:T(8,128)(2,1)S(1)} copy-done((bf16[3328,768]{1,0:T(8,128)(2,1)S(1)}, bf16[3328,768]{1,0:T(8,128)(2,1)}, u32[]{:S(2)}) %copy-start.1) | copy-done | bytes 5111832
  57.3 5.7 %correlate.1 = f32[72,4,768]{2,1,0:T(4,128)S(1)} custom-call(s32[2,4]{1,0:T(2,128)S(1)} %bitcast.21, s32[3]{0:T(128)S(1)} %pad_add_fusion.where, f32[4,2,2,40,128]{4,3,2,1,0:T(8,128)S(1)} %pad_maximum_fusion.s0, f32[4,2,2,40,128]{4,3,2,1,0:T(8,128)S(1)} %collective-permute-done.4.s1, f32[4,2,2,40,128]{4,3,2,1,0:T(8,128)S(1)} %collective-permute-done.5.s2, ...), custom_call_target="tpu_custom_call" | custom-call | tf_op jit(solution)/shard_map/correlate/pallas_call | solution.py:217
  63.0 0.0 copy-start.2
  63.0 0.1 collective-permute-start.8
  63.0 2.4 %collective-permute-done.8.other = f32[2,36,4,768]{3,2,1,0:T(4,128)S(1)} collective-permute-done((f32[2,36,4,768]{3,2,1,0:T(4,128)S(1)}, f32[2,36,4,768]{3,2,1,0:T(4,128)S(1)}, u32[]{:S(2)}, u32[]{:S(2)}) %collective-permute-start.8) | collective-permute-done | bytes 884768 | tf_op jit(solution)/shard_map/ppermute | solution.py:262
  65.5 1.0 %copy-done.6 = f32[2,36,4,768]{3,2,1,0:T(4,128)} copy-done((f32[2,36,4,768]{3,2,1,0:T(4,128)}, f32[2,36,4,768]{3,2,1,0:T(4,128)S(1)}, u32[]{:S(2)}) %copy-start.6) | copy-done | bytes 884760
  66.4 2.7 %join.1 = f32[4,36,4,768]{3,2,1,0:T(4,128)} custom-call(s32[1]{0:T(128)} %bitcast.core, f32[2,36,4,768]{3,2,1,0:T(4,128)} %bitcast.19, f32[2,36,4,768]{3,2,1,0:T(4,128)} %copy-done.6), custom_call_target="tpu_custom_call" | custom-call | tf_op jit(solution)/shard_map/join/pallas_call | solution.py:251
  (10 shorter events, 0.0 us)
Async XLA Ops:
  0.0 48.6 %copy-start = (s32[4,4]{1,0:T(4,128)S(1)}, s32[4,4]{1,0:T(4,128)}, u32[]{:S(2)}) copy-start(s32[4,4]{1,0:T(4,128)} %param.8) | copy-start | bytes 196
  0.0 1.0 %copy-start.3 = (f32[2,4,2,3,1664]{4,2,3,1,0:T(2,128)S(1)}, f32[2,4,2,3,1664]{4,2,3,1,0:T(2,128)}, u32[]{:S(2)}) copy-start(f32[2,4,2,3,1664]{4,2,3,1,0:T(2,128)} %param.5) | copy-start | bytes 958468
  1.0 0.7 copy-start.4
  3.4 19.6 %all-to-all-start = ((f32[16,40,128]{2,1,0:T(8,128)}), f32[16,40,128]{2,1,0:T(8,128)S(1)}, u32[]{:S(2)}, u32[]{:S(2)}) async-start(f32[16,40,128]{2,1,0:T(8,128)} %get-tuple-element.9), calls=%async_computation | async-start | bytes 655360 | tf_op jit(solution)/shard_map/all_to_all | solution.py:275
  23.1 0.7 %copy-start.5 = (f32[16,40,128]{2,1,0:T(8,128)}, f32[16,40,128]{2,1,0:T(8,128)S(1)}, u32[]{:S(2)}) copy-start(f32[16,40,128]{2,1,0:T(8,128)S(1)} %all-to-all-done.got_ref) | copy-start | bytes 983044
  25.4 1.4 %collective-permute-start = (f32[2,40,128]{2,1,0:T(8,128)}, f32[2,40,128]{2,1,0:T(8,128)S(1)}, u32[]{:S(2)}, u32[]{:S(2)}) collective-permute-start(f32[2,40,128]{2,1,0:T(8,128)} %get-tuple-element.11), channel_id=1, source_target_pairs={{0,1},{1,0},{2,3},{3,2},{4,5},{5,4},{6,7},{7,6},{8,9},{9,8},{10,11... | collective-permute-start | bytes 122888 | tf_op jit(solution)/shard_map/ppermute | solution.py:262
  27.7 9.5 %collective-permute-start.2 = (f32[2,2,40,128]{3,2,1,0:T(8,128)S(1)}, f32[2,2,40,128]{3,2,1,0:T(8,128)S(1)}, u32[]{:S(2)}, u32[]{:S(2)}) collective-permute-start(f32[2,2,40,128]{3,2,1,0:T(8,128)S(1)} %get-tuple-element.14), channel_id=1, source_target_pairs={{0,16},{2,18},{4,20},{6,22},{8,24},{10,26},{12,28},{14,30},{16,0},... | collective-permute-start | bytes 245768 | tf_op jit(solution)/shard_map/ppermute | solution.py:286
  28.1 9.1 %collective-permute-start.1 = (f32[2,2,40,128]{3,2,1,0:T(8,128)S(1)}, f32[2,2,40,128]{3,2,1,0:T(8,128)S(1)}, u32[]{:S(2)}, u32[]{:S(2)}) collective-permute-start(f32[2,2,40,128]{3,2,1,0:T(8,128)S(1)} %get-tuple-element.14), channel_id=1, source_target_pairs={{0,8},{2,10},{4,12},{6,14},{8,0},{10,2},{12,4},{14,6},{16,24},{18,... | collective-permute-start | bytes 245768 | tf_op jit(solution)/shard_map/ppermute | solution.py:286
  30.0 7.2 %collective-permute-start.3 = (f32[2,2,40,128]{3,2,1,0:T(8,128)S(1)}, f32[2,2,40,128]{3,2,1,0:T(8,128)S(1)}, u32[]{:S(2)}, u32[]{:S(2)}) collective-permute-start(f32[2,2,40,128]{3,2,1,0:T(8,128)S(1)} %get-tuple-element.14), channel_id=1, source_target_pairs={{0,24},{2,26},{4,28},{6,30},{8,16},{10,18},{12,20},{14,22},{16,8},... | collective-permute-start | bytes 245768 | tf_op jit(solution)/shard_map/ppermute | solution.py:286
  37.2 10.5 %collective-permute-start.4 = (f32[4,2,2,40,128]{4,3,2,1,0:T(8,128)S(1)}, f32[4,2,2,40,128]{4,3,2,1,0:T(8,128)S(1)}, u32[]{:S(2)}, u32[]{:S(2)}) collective-permute-start(f32[4,2,2,40,128]{4,3,2,1,0:T(8,128)S(1)} %pad_maximum_fusion.s0), channel_id=1, source_target_pairs={{0,2},{1,5},{2,0},{3,7},{4,6},{5,1},{6,4},{7,3},{8,10},{9,13},{10,... | collective-permute-start | bytes 983048 | tf_op jit(solution)/shard_map/ppermute | solution.py:287
  37.8 10.8 %collective-permute-start.7 = (f32[2,2,16,1664]{3,2,1,0:T(8,128)S(1)}, f32[2,2,16,1664]{3,2,1,0:T(8,128)S(1)}, u32[]{:S(2)}, u32[]{:S(2)}) collective-permute-start(f32[2,2,16,1664]{3,2,1,0:T(8,128)S(1)} %get-tuple-element.12.r0), channel_id=1, source_target_pairs={{0,1},{1,0},{2,3},{3,2},{4,5},{5,4},{6,7},{7,6},{8,9},{9,8},{10,11... | collective-permute-start | bytes 1277960 | tf_op jit(solution)/shard_map/ppermute | solution.py:262
  37.8 10.8 %collective-permute-start.5 = (f32[4,2,2,40,128]{4,3,2,1,0:T(8,128)S(1)}, f32[4,2,2,40,128]{4,3,2,1,0:T(8,128)S(1)}, u32[]{:S(2)}, u32[]{:S(2)}) collective-permute-start(f32[4,2,2,40,128]{4,3,2,1,0:T(8,128)S(1)} %pad_maximum_fusion.s0), channel_id=1, source_target_pairs={{0,4},{1,3},{2,6},{3,1},{4,0},{5,7},{6,2},{7,5},{8,12},{9,11},{10,... | collective-permute-start | bytes 983048 | tf_op jit(solution)/shard_map/ppermute | solution.py:288
  47.7 7.1 %collective-permute-start.6 = (f32[4,2,2,40,128]{4,3,2,1,0:T(8,128)S(1)}, f32[4,2,2,40,128]{4,3,2,1,0:T(8,128)S(1)}, u32[]{:S(2)}, u32[]{:S(2)}) collective-permute-start(f32[4,2,2,40,128]{4,3,2,1,0:T(8,128)S(1)} %collective-permute-done.4.s1), channel_id=1, source_target_pairs={{0,4},{1,3},{2,6},{3,1},{4,0},{5,7},{6,2},{7,5},{8,12},{9,11},{10,... | collective-permute-start | bytes 983048 | tf_op jit(solution)/shard_map/ppermute | solution.py:289
  54.8 2.4 %copy-start.1 = (bf16[3328,768]{1,0:T(8,128)(2,1)S(1)}, bf16[3328,768]{1,0:T(8,128)(2,1)}, u32[]{:S(2)}) copy-start(bf16[3328,768]{1,0:T(8,128)(2,1)} %constant.38.clone.table_hbm) | copy-start | bytes 15335428
  63.0 2.5 %copy-start.2 = (f32[72,4,768]{2,1,0:T(4,128)}, f32[72,4,768]{2,1,0:T(4,128)S(1)}, u32[]{:S(2)}) copy-start(f32[72,4,768]{2,1,0:T(4,128)S(1)} %correlate.1) | copy-start | bytes 2654212
  63.0 2.5 %collective-permute-start.8 = (f32[2,36,4,768]{3,2,1,0:T(4,128)S(1)}, f32[2,36,4,768]{3,2,1,0:T(4,128)S(1)}, u32[]{:S(2)}, u32[]{:S(2)}) collective-permute-start(f32[2,36,4,768]{3,2,1,0:T(4,128)S(1)} %bitcast.18), channel_id=1, source_target_pairs={{0,1},{1,0},{2,3},{3,2},{4,5},{5,4},{6,7},{7,6},{8,9},{9,8},{10,11... | collective-permute-start | bytes 2654216 | tf_op jit(solution)/shard_map/ppermute | solution.py:262
  65.5 1.0 %copy-start.6 = (f32[2,36,4,768]{3,2,1,0:T(4,128)}, f32[2,36,4,768]{3,2,1,0:T(4,128)S(1)}, u32[]{:S(2)}) copy-start(f32[2,36,4,768]{3,2,1,0:T(4,128)S(1)} %collective-permute-done.8.other) | copy-start | bytes 2654212

commit v2 on v1

v2 whole, which is shorter than its diff:
```python
import functools
import math

import jax
import jax.numpy as jnp
import numpy as np
from jax import lax
from jax.experimental import pallas as pl
from jax.experimental.pallas import tpu as pltpu
from jax.sharding import PartitionSpec as P

NLAG = 768
LANES = 128
MIB = 1024 * 1024


def lag_table(bins, lags, windows):
    freq = np.arange(bins, dtype=np.int64) + 360
    shift = np.arange(lags, dtype=np.int64) - lags // 2
    phase = np.mod(freq[:, None] * shift[None, :], 7200).astype(np.float32) * np.float32(
        2.0 * math.pi / 7200.0
    )
    scale = np.float32(1.0 / math.sqrt(windows * bins))
    real = (np.cos(phase) * scale).reshape(bins // LANES, 1, LANES, lags)
    imag = (-np.sin(phase) * scale).reshape(bins // LANES, 1, LANES, lags)
    return np.concatenate([real, imag], axis=1).reshape(2 * bins, lags).astype(jnp.bfloat16)


def whiten_kernel(flags_hbm, x_hbm, pieces_ref, rec_ref, flags, x_ref, sems):
    copies = (
        pltpu.make_async_copy(flags_hbm, flags, sems.at[0]),
        pltpu.make_async_copy(x_hbm, x_ref, sems.at[1]),
    )
    for copy in copies:
        copy.start()
    for copy in copies:
        copy.wait()
    wins, stas, comps, _, bins = x_ref.shape
    core = lax.axis_index("win")
    place = ((0, 1 + core), (2 - core, 3))
    tiles = bins // LANES
    lane = lax.broadcasted_iota(jnp.int32, (wins * stas, LANES), 1)
    left = lane < 64
    sums = []
    for w in range(wins):
        for s in range(stas):
            x = x_ref[w, s]
            sums.append(jnp.sum(jnp.sum(x * x, axis=0), axis=0, keepdims=True))
    power = jnp.concatenate(sums, axis=0)
    weight = jnp.concatenate(
        [
            jnp.full((1, LANES), flags[w, s].astype(jnp.float32), jnp.float32)
            for w in range(wins)
            for s in range(stas)
        ],
        axis=0,
    )
    scales = []
    for c in range(tiles):
        tile = power[:, c * LANES : (c + 1) * LANES]
        low = jnp.sum(jnp.where(left, tile, 0.0), axis=1, keepdims=True)
        high = jnp.sum(jnp.where(left, 0.0, tile), axis=1, keepdims=True)
        mean = jnp.where(left, low, high) * (1.0 / (64 * 2 * comps))
        scales.append(weight / jnp.sqrt(mean + 1e-06))
    scale = jnp.concatenate(scales, axis=1)
    for w in range(wins):
        for s in range(stas):
            k = w * stas + s
            row = scale[k : k + 1]
            for i in range(comps):
                y = x_ref[w, s, i] * row
                for part in range(2):
                    rec_ref[w, part, pl.ds(i * stas + s, 1), :] = y[part : part + 1]
                    for c in range(tiles):
                        pieces_ref[4 * s + place[w][part], pl.ds(i * tiles + c, 1), :] = y[
                            part : part + 1, c * LANES : (c + 1) * LANES
                        ]
    rest = pieces_ref.shape[1] - comps * tiles
    if rest:
        for k in range(wins * stas * 2):
            pieces_ref[k, pl.ds(comps * tiles, rest), :] = jnp.zeros((rest, LANES), jnp.float32)
    spare = rec_ref.shape[2] - comps * stas
    if spare:
        for w in range(wins):
            for part in range(2):
                rec_ref[w, part, pl.ds(comps * stas, spare), :] = jnp.zeros(
                    (spare, bins), jnp.float32
                )


def whiten(spectra, flags):
    wins, stas, _, comps, bins = spectra.shape
    rows = -(-comps * (bins // LANES) // 8) * 8
    recs = -(-comps * stas // 8) * 8
    return pl.pallas_call(
        whiten_kernel,
        out_shape=(
            jax.ShapeDtypeStruct((wins * stas * 2, rows, LANES), jnp.float32),
            jax.ShapeDtypeStruct((wins, 2, recs, bins), jnp.float32),
        ),
        in_specs=[pl.BlockSpec(memory_space=pltpu.HBM)] * 2,
        out_specs=(
            pl.BlockSpec(memory_space=pltpu.VMEM),
            pl.BlockSpec(memory_space=pltpu.VMEM),
        ),
        scratch_shapes=[
            pltpu.SMEM(flags.shape, jnp.int32),
            pltpu.VMEM((wins, stas, comps, 2, bins), jnp.float32),
            pltpu.SemaphoreType.DMA((2,)),
        ],
        compiler_params=pltpu.CompilerParams(vmem_limit_bytes=61 * MIB),
        name="whiten",
    )(flags, jnp.transpose(spectra, (0, 1, 3, 2, 4)))


def pick_kernel(params, got_ref, before, keep_ref, send_ref):
    half = keep_ref.shape[0]
    for t in range(half):
        keep_ref[t] = got_ref[params[3 + t]]
        send_ref[t] = got_ref[params[3 + half + t]]


def pick(params, got, before, steps):
    shape = jax.ShapeDtypeStruct((steps // 2,) + got.shape[1:], jnp.float32)
    smem = pl.BlockSpec(memory_space=pltpu.SMEM)
    vmem = pl.BlockSpec(memory_space=pltpu.VMEM)
    return pl.pallas_call(
        pick_kernel,
        out_shape=(shape, shape),
        in_specs=[smem, vmem, vmem],
        out_specs=(vmem, vmem),
        compiler_params=pltpu.CompilerParams(vmem_limit_bytes=8 * MIB),
        name="pick",
    )(params, got, before)


def pack_kernel(*refs, count):
    for n in range(count):
        refs[-1][n] = refs[n][...]


def pack(values, before):
    vmem = pl.BlockSpec(memory_space=pltpu.VMEM)
    return pl.pallas_call(
        functools.partial(pack_kernel, count=len(values)),
        out_shape=jax.ShapeDtypeStruct((len(values),) + values[0].shape, values[0].dtype),
        in_specs=[vmem] * (len(values) + len(before)),
        out_specs=vmem,
        compiler_params=pltpu.CompilerParams(vmem_limit_bytes=8 * MIB),
        name="pack",
    )(*values, *before)


def load_kernel(table_hbm, after, out_ref, sem):
    copy = pltpu.make_async_copy(table_hbm, out_ref, sem)
    copy.start()
    copy.wait()


def load(table, after):
    vmem = pl.BlockSpec(memory_space=pltpu.VMEM)
    return pl.pallas_call(
        load_kernel,
        out_shape=jax.ShapeDtypeStruct(table.shape, table.dtype),
        in_specs=[pl.BlockSpec(memory_space=pltpu.HBM), vmem],
        out_specs=vmem,
        scratch_shapes=[pltpu.SemaphoreType.DMA],
        compiler_params=pltpu.CompilerParams(vmem_limit_bytes=8 * MIB),
        cost_estimate=pl.CostEstimate(flops=0, bytes_accessed=5 * MIB, transcendentals=0),
        name="load",
    )(table, after)


def correlate_kernel(params, *refs):
    firsts, rests = refs[0:8:2], refs[1:8:2]
    receivers_in, table, out_ref, rec, lhs = refs[8:10], refs[10], refs[11], refs[12], refs[13]
    groups, steps, _, _ = firsts[0].shape
    depth = 1 + rests[0].shape[0]
    tiles = rec.shape[4] // LANES
    window, part = params[1], params[2]
    kinds = ((window, part), (part, window))
    signs = []
    for g, (w, p) in enumerate(kinds):
        signs.append(1.0 - 2.0 * p.astype(jnp.float32))
        for other_w in range(2):
            for other_p in range(2):
                rows = receivers_in[g][w ^ other_w, p ^ other_p, 0:12, :]
                rec[g, other_w, other_p, 0:12, :] = rows
                rec[g, other_w, other_p, 12:24, :] = rows
    spots = (((0, 1), (2, 3)), ((0, 2), (1, 3)))
    upper = lax.broadcasted_iota(jnp.int32, (8, LANES), 0) < 4

    def source(spot, g, n, c):
        t, offset, i = n // (3 * depth), (n // 3) % depth, n % 3
        row = pl.ds(i * tiles + c, 1)
        if offset:
            line = rests[spot][offset - 1, g, t, row, :]
        else:
            line = firsts[spot][g, t, row, :]
        return jnp.broadcast_to(line, (8, LANES))

    def chunk(c, carry):
        lanes = pl.ds(pl.multiple_of(c * LANES, LANES), LANES)
        receivers = [
            [[rec[g, w, p, :, lanes] for p in range(2)] for w in range(2)] for g in range(groups)
        ]
        for block in range(steps * depth * 3 // 4):
            real_tiles, imag_tiles = [], []
            for pair in range(2):
                numbers = (block * 4 + pair * 2, block * 4 + pair * 2 + 1)
                real = [0.0] * 3
                imag = [0.0] * 3
                for g in range(groups):
                    part_imag = [0.0] * 3
                    for w in range(2):
                        spread = []
                        for p in range(2):
                            rows = [source(spots[g][w][p], g, n, c) for n in numbers]
                            spread.append((rows[0], jnp.where(upper, rows[0], rows[1]), rows[1]))
                        for k in range(3):
                            ra = receivers[g][w][0][8 * k : 8 * k + 8]
                            rb = receivers[g][w][1][8 * k : 8 * k + 8]
                            a, b = spread[0][k], spread[1][k]
                            real[k] += a * ra + b * rb
                            part_imag[k] += b * ra - a * rb
                    for k in range(3):
                        imag[k] += signs[g] * part_imag[k]
                real_tiles += real
                imag_tiles += imag
            at = pl.ds(block * 48, 48)
            base = c * 2 * LANES
            lhs[at, pl.ds(pl.multiple_of(base, LANES), LANES)] = jnp.concatenate(
                real_tiles, axis=0
            ).astype(jnp.bfloat16)
            lhs[at, pl.ds(pl.multiple_of(base + LANES, LANES), LANES)] = jnp.concatenate(
                imag_tiles, axis=0
            ).astype(jnp.bfloat16)
        return carry

    lax.fori_loop(0, tiles, chunk, 0)
    for n in range(out_ref.shape[3] // 256):
        lags = pl.ds(n * 256, 256)
        result = jnp.dot(lhs[...], table[:, lags], preferred_element_type=jnp.float32)
        for t in range(steps):
            for offset in range(depth):
                first = params[3 + 2 * steps + depth * t + offset] * 9
                for k in range(9):
                    row = 4 * ((t * depth + offset) * 9 + k)
                    out_ref[t, first + k, :, lags] = result[row : row + 4]


def correlate(params, sources, own, other, table):
    steps = sources[0].shape[1]
    depth = 1 + sources[1].shape[0]
    bins = own.shape[3]
    lags = table.shape[1]
    vmem = pl.BlockSpec(memory_space=pltpu.VMEM)
    return pl.pallas_call(
        correlate_kernel,
        out_shape=jax.ShapeDtypeStruct((steps, depth * 9, 4, lags), jnp.float32),
        in_specs=[pl.BlockSpec(memory_space=pltpu.SMEM)] + [vmem] * 11,
        out_specs=vmem,
        scratch_shapes=[
            pltpu.VMEM((2, 2, 2, 24, bins), jnp.float32),
            pltpu.VMEM((steps * depth * 3 * 12, 2 * bins), jnp.bfloat16),
        ],
        compiler_params=pltpu.CompilerParams(vmem_limit_bytes=20 * MIB),
        name="correlate",
    )(params, *sources, own, other, table)


def write_steps(half, out, core, sems):
    parts = sems.shape[1]
    size = half.shape[1] // parts
    copies = [
        pltpu.make_async_copy(
            half.at[t, pl.ds(n * size, size)],
            out.at[2 * t + core, pl.ds(n * size, size)],
            sems.at[t, n],
        )
        for t in range(half.shape[0])
        for n in range(parts)
    ]
    for copy in copies:
        copy.start()
    for copy in copies:
        copy.wait()


def put_kernel(own, out, sems):
    write_steps(own, out, lax.axis_index("win"), sems)


def put(own):
    return pl.pallas_call(
        put_kernel,
        out_shape=jax.ShapeDtypeStruct((2 * own.shape[0],) + own.shape[1:], own.dtype),
        in_specs=[pl.BlockSpec(memory_space=pltpu.VMEM)],
        out_specs=pl.BlockSpec(memory_space=pltpu.HBM),
        scratch_shapes=[pltpu.SemaphoreType.DMA((own.shape[0], 4))],
        compiler_params=pltpu.CompilerParams(vmem_limit_bytes=8 * MIB),
        name="put",
    )(own)


def join_kernel(other, whole, out, sems):
    write_steps(other, out, 1 - lax.axis_index("win"), sems)


def join(other, whole):
    hbm = pl.BlockSpec(memory_space=pltpu.HBM)
    return pl.pallas_call(
        join_kernel,
        out_shape=jax.ShapeDtypeStruct(whole.shape, whole.dtype),
        in_specs=[pl.BlockSpec(memory_space=pltpu.VMEM), hbm],
        out_specs=hbm,
        scratch_shapes=[pltpu.SemaphoreType.DMA((other.shape[0], 4))],
        input_output_aliases={1: 0},
        compiler_params=pltpu.CompilerParams(vmem_limit_bytes=8 * MIB),
        name="join",
    )(other, whole)


def swap(value):
    return lax.ppermute(value, "win", [(0, 1), (1, 0)])


def on_device(spectra, flags, owners, source_slots):
    wins, stas, _, comps, bins = spectra.shape
    steps, sources = source_slots.shape
    at = lax.axis_index("sta")
    core = lax.axis_index("win")
    blocks = lax.axis_size("sta")
    pairs = owners.reshape(steps // 2, 2)
    slots = source_slots.reshape(steps // 2, 2, sources)
    z, place = at >> 2, at & 3
    high, low = place >> 1, place & 1
    mine = jnp.where(core == 0, slots[:, 0], slots[:, 1])
    held = z ^ jnp.arange(sources, dtype=jnp.int32)
    order = jnp.arange(sources, dtype=jnp.int32)
    found = jnp.sum(
        jnp.where(mine[:, None, :] == held[None, :, None], order[None, None, :], 0), axis=2
    )
    params = jnp.concatenate(
        [
            jnp.stack([core, jnp.where(core == 0, high, low), jnp.where(core == 0, low, high)]),
            jnp.where(core == 0, pairs[:, 0], pairs[:, 1]),
            jnp.where(core == 0, pairs[:, 1], pairs[:, 0]),
            found.reshape(-1),
        ]
    ).astype(jnp.int32)
    pieces, own = whiten(spectra, flags)
    other = swap(own)
    got = lax.all_to_all(pieces, "sta", 0, 0)
    keep, send = pick(params, got, other, steps)
    mine = jnp.stack([keep, swap(send)])

    def partner(bits):
        return [(i, i ^ bits) for i in range(blocks)]

    def by_core(first, second):
        bits = (first, second)
        return [(2 * i + c, 2 * (i ^ bits[c]) + c) for i in range(blocks) for c in range(2)]

    def plane(value):
        near = lax.ppermute(value, ("sta", "win"), by_core(1, 2))
        side = lax.ppermute(value, ("sta", "win"), by_core(2, 1))
        return value, near, side, lax.ppermute(value, "sta", partner(3))

    column = [lax.ppermute(mine, "sta", partner(4 * k)) for k in (1, 2, 3)]
    first = plane(mine)
    rest = plane(pack(column, first[1:]))
    sources_in = [value for spot in zip(first, rest) for value in spot]
    table = jnp.asarray(lag_table(bins, NLAG, wins * lax.axis_size("win")))
    table = load(table, mine)
    half = correlate(params, sources_in, own, other, table)
    whole = join(swap(half), put(half))
    return whole.reshape(steps, sources, comps, comps, stas, NLAG).transpose(0, 1, 2, 4, 3, 5)


def spread(value, axis, source):
    kept = jnp.where(lax.axis_index(axis) == source, value, 0).astype(value.dtype)
    return lax.psum(kept, axis)


def cross(picked, receivers, table):
    src_re = picked[:, :, 0][:, :, :, None, None, :]
    src_im = picked[:, :, 1][:, :, :, None, None, :]
    rec_re = receivers[:, :, 0][:, None, None, :, :, :]
    rec_im = receivers[:, :, 1][:, None, None, :, :, :]
    real = jnp.sum(src_re * rec_re + src_im * rec_im, axis=0)
    imag = jnp.sum(src_im * rec_re - src_re * rec_im, axis=0)
    shape = real.shape
    both = jnp.stack(
        [part.reshape(shape[:4] + (shape[4] // LANES, LANES)) for part in (real, imag)], axis=5
    )
    rows = both.reshape(-1, 2 * shape[4]).astype(jnp.bfloat16)
    lagged = jnp.dot(rows, table, preferred_element_type=jnp.float32)
    return lagged.reshape(shape[:4] + (table.shape[1],))


def on_device_general(spectra, flags, owners, source_slots):
    shape = spectra.shape
    blocks = spectra.reshape(shape[:4] + (shape[4] // 64, 64))
    power = jnp.mean(blocks * blocks, axis=(2, 3, 5), keepdims=True)
    whitened = (blocks / jnp.sqrt(power + 1e-06)).reshape(shape)
    weighted = whitened * flags.astype(jnp.float32)[:, :, None, None, None]
    table = jnp.asarray(lag_table(shape[4], NLAG, shape[0] * lax.axis_size("win")))
    outputs = []
    for step in range(source_slots.shape[0]):
        chosen = jnp.take(weighted, source_slots[step], axis=1)
        picked = spread(chosen, "sta", owners[step])
        outputs.append(lax.psum(cross(picked, weighted, table), "win"))
    return jnp.stack(outputs)


def solution(mesh):
    small = mesh.shape["sta"] == 16 and mesh.shape["win"] == 2
    return jax.shard_map(
        on_device if small else on_device_general,
        mesh=mesh,
        in_specs=(P("win", "sta", None, None, None), P("win", "sta"), P(), P()),
        out_specs=P(None, None, None, "sta", None, None),
        check_vma=False,
    )
```

time: 69.5 us -> 59.2 us (0.85)
  waiting for transfers between devices: 35.5 us -> 24.3 us
  starting transfers between devices: 15 us -> 19.8 us
  local copies, waits for them, and re-layouts: 5.83 us -> 3.35 us
  Pallas kernels: 11.8 us -> 10.2 us
    ppermute x6 -> x9, waiting for transfers between devices: 20.4 us -> 12.5 us  [the longest x3 5.46 us: on_device(): column = [lax.ppermute(mine, 'sta', partner(4 * k)) for k in (1, 2, 3)]]
    ppermute x6 -> x9, starting transfers between devices: 6.65 us -> 11.2 us  [the longest x3 4.16 us: on_device(): column = [lax.ppermute(mine, 'sta', partner(4 * k)) for k in (1, 2, 3)]]
    unnamed x14 -> x4, local copies, waits for them, and re-layouts: 5.83 us -> 2.45 us
    pallas_call x3 -> x6, Pallas kernels: 9.98 us -> 7.79 us  [the longest x1 4.77 us: correlate(): pl.pallas_call(correlate_kernel, out_shape=jax.ShapeDtypeStruct((steps, d...]
    all_to_all x1, waiting for transfers between devices: 11.3 us -> 9.19 us  [on_device(): got = lax.all_to_all(pieces, 'sta', 0, 0)]
    ppermute x3, waiting for transfers between devices: 3.84 us -> 2.62 us  [swap(): return lax.ppermute(value, 'win', [(0, 1), (1, 0)])]
    select_n x0 -> x2, other arithmetic: none -> 0.94 us  [the longest x1 0.76 us: on_device(): mine = jnp.where(core == 0, slots[:, 0], slots[:, 1])]
    another operation x3 -> x1, other arithmetic: 0.89 us -> 0.01 us  [on_device(): mine = jnp.stack([keep, swap(send)])]
  transfers between devices with their start and end apart: 10 -> 13, of which waited for: 6 -> 8; matrix products, arithmetic and copies ran while one was open for 0% -> 3% of each run, Pallas kernels for 0% -> 3%
where the time goes in v2:
time: 59.2 us; the launch traced here: 58.9 us
  waiting for transfers between devices  24.3 us (41%)
  starting transfers between devices  19.8 us (33%)
  Pallas kernels  10.2 us (17%)
  local copies, waits for them, and re-layouts  3.35 us (6%)
  other arithmetic  1.14 us (2%)
    all_to_all x1, waiting for transfers between devices, on_device(): got = lax.all_to_all(pieces, 'sta', 0, 0)  9.19 us
    all_to_all x1, starting transfers between devices, on_device(): got = lax.all_to_all(pieces, 'sta', 0, 0)  8.32 us
    ppermute x3, waiting for transfers between devices, on_device(): column = [lax.ppermute(mine, 'sta', partner(4 * k)) for k in (1, 2, 3)]  5.46 us
    pallas_call x1, Pallas kernels, correlate(): pl.pallas_call(correlate_kernel, out_shape=jax.ShapeDtypeStruct((steps, d...  4.77 us
    ppermute x3, starting transfers between devices, on_device(): column = [lax.ppermute(mine, 'sta', partner(4 * k)) for k in (1, 2, 3)]  4.16 us
    ppermute x2, waiting for transfers between devices, plane(): return (value, near, side, lax.ppermute(value, 'sta', partner(3)))  3.61 us
    ppermute x2, waiting for transfers between devices, plane(): side = lax.ppermute(value, ('sta', 'win'), by_core(2, 1))  3.44 us
    ppermute x2, starting transfers between devices, plane(): near = lax.ppermute(value, ('sta', 'win'), by_core(1, 2))  2.93 us
  transfers between devices with their start and end apart: 13, of which 8 were waited for; matrix products, arithmetic and copies ran while one was open for 3% of the time, Pallas kernels for 3%

profile of v2, /device:TPU:0, one launch (start us, length us, event | category | flops | bytes accessed | tf_op | source)
XLA Modules:
  0.0 58.9 jit_solution(2505038193146084791)
XLA Ops:
  0.0 2.4 %whiten.1 = (f32[16,40,128]{2,1,0:T(8,128)}, f32[2,2,16,1664]{3,2,1,0:T(8,128)}) custom-call(s32[2,4]{1,0:T(2,128)} %flags_hbm.1, f32[2,4,3,2,1664]{4,3,2,1,0:T(2,128)} %bitcast.12), custom_call_target="tpu_custom_call" | custom-call | tf_op jit(solution)/shard_map/whiten/pallas_call | solution.py:95
  2.4 8.3 %all-to-all-start = ((f32[16,40,128]{2,1,0:T(8,128)}), f32[16,40,128]{2,1,0:T(8,128)S(1)}, u32[]{:S(2)}, u32[]{:S(2)}) async-start(f32[16,40,128]{2,1,0:T(8,128)} %get-tuple-element.9), calls=%async_computation | async-start | bytes 655360 | tf_op jit(solution)/shard_map/all_to_all | solution.py:354
  10.8 0.7 %reshape.20 = s32[2,2]{1,0:T(2,128)S(1)} reshape(s32[4]{0:T(128)} %param.7) | data formatting | bytes 32 | tf_op jit(solution)/shard_map/reshape | solution.py:334
  11.6 0.8 %broadcast_select_fusion = s32[2,1,4]{2,1,0:T(1,128)S(1)} fusion(pred[]{:T(512)S(6)} %eq.10, s32[2,2,4]{2,1,0:T(2,128)} %bitcast.15), kind=kLoop, calls=%fused_computation.2 | loop fusion | flops 8 | bytes 97 | tf_op jit(solution)/shard_map/jit(_where)/select_n | solution.py:338
  12.3 0.2 select_reduce_fusion
  12.5 0.1 reshape.22
  12.6 0.2 select_reduce_fusion.1
  12.8 0.1 concatenate.3.params
  12.9 9.2 %all-to-all-done.got_ref = f32[16,40,128]{2,1,0:T(8,128)S(1)} async-done(((f32[16,40,128]{2,1,0:T(8,128)}), f32[16,40,128]{2,1,0:T(8,128)S(1)}, u32[]{:S(2)}, u32[]{:S(2)}) %all-to-all-start) | async-done | bytes 327712 | tf_op jit(solution)/shard_map/all_to_all | solution.py:354
  22.1 0.6 pick.1
  22.7 1.2 %collective-permute-done.1 = f32[2,40,128]{2,1,0:T(8,128)S(1)} collective-permute-done((f32[2,40,128]{2,1,0:T(8,128)S(1)}, f32[2,40,128]{2,1,0:T(8,128)S(1)}, u32[]{:S(2)}, u32[]{:S(2)}) %collective-permute-start.1) | collective-permute-done | bytes 40992 | tf_op jit(solution)/shard_map/ppermute | solution.py:325
  23.9 0.8 %collective-permute-start.7 = (f32[2,2,40,128]{3,2,1,0:T(8,128)S(1)}, f32[2,2,40,128]{3,2,1,0:T(8,128)S(1)}, u32[]{:S(2)}, u32[]{:S(2)}) collective-permute-start(f32[2,2,40,128]{3,2,1,0:T(8,128)S(1)} %pad_maximum_fusion.after.refs_0_), channel_id=1, source_target_pairs={{0,6},{2,4},{4,2},{6,0},{8,14},{10,12},{12,10},{14,8},{16,22},{18,... | collective-permute-start | bytes 245768 | tf_op jit(solution)/shard_map/ppermute | solution.py:368
  24.7 1.2 %collective-permute-start.6 = (f32[2,2,40,128]{3,2,1,0:T(8,128)S(1)}, f32[2,2,40,128]{3,2,1,0:T(8,128)S(1)}, u32[]{:S(2)}, u32[]{:S(2)}) collective-permute-start(f32[2,2,40,128]{3,2,1,0:T(8,128)S(1)} %pad_maximum_fusion.after.refs_0_), channel_id=1, source_target_pairs={{0,4},{1,3},{2,6},{3,1},{4,0},{5,7},{6,2},{7,5},{8,12},{9,11},{10,... | collective-permute-start | bytes 245768 | tf_op jit(solution)/shard_map/ppermute | solution.py:367
  25.9 1.5 %collective-permute-start.5 = (f32[2,2,40,128]{3,2,1,0:T(8,128)S(1)}, f32[2,2,40,128]{3,2,1,0:T(8,128)S(1)}, u32[]{:S(2)}, u32[]{:S(2)}) collective-permute-start(f32[2,2,40,128]{3,2,1,0:T(8,128)S(1)} %pad_maximum_fusion.after.refs_0_), channel_id=1, source_target_pairs={{0,2},{1,5},{2,0},{3,7},{4,6},{5,1},{6,4},{7,3},{8,10},{9,13},{10,... | collective-permute-start | bytes 245768 | tf_op jit(solution)/shard_map/ppermute | solution.py:366
  27.4 1.7 %collective-permute-start.4 = (f32[2,2,40,128]{3,2,1,0:T(8,128)S(1)}, f32[2,2,40,128]{3,2,1,0:T(8,128)S(1)}, u32[]{:S(2)}, u32[]{:S(2)}) collective-permute-start(f32[2,2,40,128]{3,2,1,0:T(8,128)S(1)} %pad_maximum_fusion.after.refs_0_), channel_id=1, source_target_pairs={{0,24},{2,26},{4,28},{6,30},{8,16},{10,18},{12,20},{14,22},{16,8},... | collective-permute-start | bytes 245768 | tf_op jit(solution)/shard_map/ppermute | solution.py:370
  29.1 0.8 %collective-permute-start.3 = (f32[2,2,40,128]{3,2,1,0:T(8,128)S(1)}, f32[2,2,40,128]{3,2,1,0:T(8,128)S(1)}, u32[]{:S(2)}, u32[]{:S(2)}) collective-permute-start(f32[2,2,40,128]{3,2,1,0:T(8,128)S(1)} %pad_maximum_fusion.after.refs_0_), channel_id=1, source_target_pairs={{0,16},{2,18},{4,20},{6,22},{8,24},{10,26},{12,28},{14,30},{16,0},... | collective-permute-start | bytes 245768 | tf_op jit(solution)/shard_map/ppermute | solution.py:370
  29.9 0.2 collective-permute-done.7.refs_5_.refs_6_
  30.1 1.7 %collective-permute-start.2 = (f32[2,2,40,128]{3,2,1,0:T(8,128)S(1)}, f32[2,2,40,128]{3,2,1,0:T(8,128)S(1)}, u32[]{:S(2)}, u32[]{:S(2)}) collective-permute-start(f32[2,2,40,128]{3,2,1,0:T(8,128)S(1)} %pad_maximum_fusion.after.refs_0_), channel_id=1, source_target_pairs={{0,8},{2,10},{4,12},{6,14},{8,0},{10,2},{12,4},{14,6},{16,24},{18,... | collective-permute-start | bytes 245768 | tf_op jit(solution)/shard_map/ppermute | solution.py:370
  31.8 2.8 %collective-permute-done.4.refs_2_ = f32[2,2,40,128]{3,2,1,0:T(8,128)S(1)} collective-permute-done((f32[2,2,40,128]{3,2,1,0:T(8,128)S(1)}, f32[2,2,40,128]{3,2,1,0:T(8,128)S(1)}, u32[]{:S(2)}, u32[]{:S(2)}) %collective-permute-start.4) | collective-permute-done | bytes 81952 | tf_op jit(solution)/shard_map/ppermute | solution.py:370
  34.6 2.7 %collective-permute-done.3.refs_1_ = f32[2,2,40,128]{3,2,1,0:T(8,128)S(1)} collective-permute-done((f32[2,2,40,128]{3,2,1,0:T(8,128)S(1)}, f32[2,2,40,128]{3,2,1,0:T(8,128)S(1)}, u32[]{:S(2)}, u32[]{:S(2)}) %collective-permute-start.3) | collective-permute-done | bytes 81952 | tf_op jit(solution)/shard_map/ppermute | solution.py:370
  37.3 0.8 %collective-permute-start.10 = (f32[3,2,2,40,128]{4,3,2,1,0:T(8,128)S(1)}, f32[3,2,2,40,128]{4,3,2,1,0:T(8,128)S(1)}, u32[]{:S(2)}, u32[]{:S(2)}) collective-permute-start(f32[3,2,2,40,128]{4,3,2,1,0:T(8,128)S(1)} %pack.1.refs_1_), channel_id=1, source_target_pairs={{0,6},{2,4},{4,2},{6,0},{8,14},{10,12},{12,10},{14,8},{16,22},{18,... | collective-permute-start | bytes 737288 | tf_op jit(solution)/shard_map/ppermute | solution.py:368
  38.1 1.2 %collective-permute-start.9 = (f32[3,2,2,40,128]{4,3,2,1,0:T(8,128)S(1)}, f32[3,2,2,40,128]{4,3,2,1,0:T(8,128)S(1)}, u32[]{:S(2)}, u32[]{:S(2)}) collective-permute-start(f32[3,2,2,40,128]{4,3,2,1,0:T(8,128)S(1)} %pack.1.refs_1_), channel_id=1, source_target_pairs={{0,4},{1,3},{2,6},{3,1},{4,0},{5,7},{6,2},{7,5},{8,12},{9,11},{10,... | collective-permute-start | bytes 737288 | tf_op jit(solution)/shard_map/ppermute | solution.py:367
  39.4 1.5 %collective-permute-start.8 = (f32[3,2,2,40,128]{4,3,2,1,0:T(8,128)S(1)}, f32[3,2,2,40,128]{4,3,2,1,0:T(8,128)S(1)}, u32[]{:S(2)}, u32[]{:S(2)}) collective-permute-start(f32[3,2,2,40,128]{4,3,2,1,0:T(8,128)S(1)} %pack.1.refs_1_), channel_id=1, source_target_pairs={{0,2},{1,5},{2,0},{3,7},{4,6},{5,1},{6,4},{7,3},{8,10},{9,13},{10,... | collective-permute-start | bytes 737288 | tf_op jit(solution)/shard_map/ppermute | solution.py:366
  40.8 2.4 %copy-done = bf16[3328,768]{1,0:T(8,128)(2,1)S(1)} copy-done((bf16[3328,768]{1,0:T(8,128)(2,1)S(1)}, bf16[3328,768]{1,0:T(8,128)(2,1)}, u32[]{:S(2)}) %copy-start) | copy-done | bytes 5111832
  43.3 0.5 load.1.refs_10_
  43.8 3.4 %collective-permute-done.10.refs_7_ = f32[3,2,2,40,128]{4,3,2,1,0:T(8,128)S(1)} collective-permute-done((f32[3,2,2,40,128]{4,3,2,1,0:T(8,128)S(1)}, f32[3,2,2,40,128]{4,3,2,1,0:T(8,128)S(1)}, u32[]{:S(2)}, u32[]{:S(2)}) %collective-permute-start.10) | collective-permute-done | bytes 245792 | tf_op jit(solution)/shard_map/ppermute | solution.py:368
  47.2 3.4 %collective-permute-done.9.refs_5_ = f32[3,2,2,40,128]{4,3,2,1,0:T(8,128)S(1)} collective-permute-done((f32[3,2,2,40,128]{4,3,2,1,0:T(8,128)S(1)}, f32[3,2,2,40,128]{4,3,2,1,0:T(8,128)S(1)}, u32[]{:S(2)}, u32[]{:S(2)}) %collective-permute-start.9) | collective-permute-done | bytes 245792 | tf_op jit(solution)/shard_map/ppermute | solution.py:367
  50.6 4.8 %correlate.1.own = f32[2,36,4,768]{3,2,1,0:T(4,128)S(1)} custom-call(s32[15]{0:T(128)S(1)} %concatenate.3.params, f32[2,2,40,128]{3,2,1,0:T(8,128)S(1)} %pad_maximum_fusion.after.refs_0_, f32[3,2,2,40,128]{4,3,2,1,0:T(8,128)S(1)} %pack.1.refs_1_, f32[2,2,40,128]{3,2,1,0:T(8,128)S(1)} %collective-permute-done.5.refs_3_.refs_2_, ...), custom_call_target="tpu_custom_call" | custom-call | tf_op jit(solution)/shard_map/correlate/pallas_call | solution.py:258
  55.4 0.1 collective-permute-start.11
  55.5 1.0 %put.1.whole = f32[4,36,4,768]{3,2,1,0:T(4,128)} custom-call(f32[2,36,4,768]{3,2,1,0:T(4,128)S(1)} %correlate.1.own), custom_call_target="tpu_custom_call" | custom-call | tf_op jit(solution)/shard_map/put/pallas_call | solution.py:295
  56.5 1.4 %collective-permute-done.11.other = f32[2,36,4,768]{3,2,1,0:T(4,128)S(1)} collective-permute-done((f32[2,36,4,768]{3,2,1,0:T(4,128)S(1)}, f32[2,36,4,768]{3,2,1,0:T(4,128)S(1)}, u32[]{:S(2)}, u32[]{:S(2)}) %collective-permute-start.11) | collective-permute-done | bytes 884768 | tf_op jit(solution)/shard_map/ppermute | solution.py:325
  57.9 1.0 %join.1 = f32[4,36,4,768]{3,2,1,0:T(4,128)} custom-call(f32[2,36,4,768]{3,2,1,0:T(4,128)S(1)} %collective-permute-done.11.other, f32[4,36,4,768]{3,2,1,0:T(4,128)} %put.1.whole), custom_call_target="tpu_custom_call", output_to_operand_aliasing={{}: (1, {})} | custom-call | tf_op jit(solution)/shard_map/join/pallas_call | solution.py:312
  (13 shorter events, 0.2 us)
Async XLA Ops:
  2.4 19.6 %all-to-all-start = ((f32[16,40,128]{2,1,0:T(8,128)}), f32[16,40,128]{2,1,0:T(8,128)S(1)}, u32[]{:S(2)}, u32[]{:S(2)}) async-start(f32[16,40,128]{2,1,0:T(8,128)} %get-tuple-element.9), calls=%async_computation | async-start | bytes 655360 | tf_op jit(solution)/shard_map/all_to_all | solution.py:354
  10.7 2.1 %collective-permute-start = (f32[2,2,16,1664]{3,2,1,0:T(8,128)}, f32[2,2,16,1664]{3,2,1,0:T(8,128)S(1)}, u32[]{:S(2)}, u32[]{:S(2)}) collective-permute-start(f32[2,2,16,1664]{3,2,1,0:T(8,128)} %get-tuple-element.10.refs_8_), channel_id=1, source_target_pairs={{0,1},{1,0},{2,3},{3,2},{4,5},{5,4},{6,7},{7,6},{8,9},{9,8},{10,11... | collective-permute-start | bytes 1277960 | tf_op jit(solution)/shard_map/ppermute | solution.py:325
  22.6 1.3 %collective-permute-start.1 = (f32[2,40,128]{2,1,0:T(8,128)S(1)}, f32[2,40,128]{2,1,0:T(8,128)S(1)}, u32[]{:S(2)}, u32[]{:S(2)}) collective-permute-start(f32[2,40,128]{2,1,0:T(8,128)S(1)} %get-tuple-element.12), channel_id=1, source_target_pairs={{0,1},{1,0},{2,3},{3,2},{4,5},{5,4},{6,7},{7,6},{8,9},{9,8},{10,11... | collective-permute-start | bytes 122888 | tf_op jit(solution)/shard_map/ppermute | solution.py:325
  23.9 6.2 %collective-permute-start.7 = (f32[2,2,40,128]{3,2,1,0:T(8,128)S(1)}, f32[2,2,40,128]{3,2,1,0:T(8,128)S(1)}, u32[]{:S(2)}, u32[]{:S(2)}) collective-permute-start(f32[2,2,40,128]{3,2,1,0:T(8,128)S(1)} %pad_maximum_fusion.after.refs_0_), channel_id=1, source_target_pairs={{0,6},{2,4},{4,2},{6,0},{8,14},{10,12},{12,10},{14,8},{16,22},{18,... | collective-permute-start | bytes 245768 | tf_op jit(solution)/shard_map/ppermute | solution.py:368
  24.7 7.1 %collective-permute-start.6 = (f32[2,2,40,128]{3,2,1,0:T(8,128)S(1)}, f32[2,2,40,128]{3,2,1,0:T(8,128)S(1)}, u32[]{:S(2)}, u32[]{:S(2)}) collective-permute-start(f32[2,2,40,128]{3,2,1,0:T(8,128)S(1)} %pad_maximum_fusion.after.refs_0_), channel_id=1, source_target_pairs={{0,4},{1,3},{2,6},{3,1},{4,0},{5,7},{6,2},{7,5},{8,12},{9,11},{10,... | collective-permute-start | bytes 245768 | tf_op jit(solution)/shard_map/ppermute | solution.py:367
  25.9 5.9 %collective-permute-start.5 = (f32[2,2,40,128]{3,2,1,0:T(8,128)S(1)}, f32[2,2,40,128]{3,2,1,0:T(8,128)S(1)}, u32[]{:S(2)}, u32[]{:S(2)}) collective-permute-start(f32[2,2,40,128]{3,2,1,0:T(8,128)S(1)} %pad_maximum_fusion.after.refs_0_), channel_id=1, source_target_pairs={{0,2},{1,5},{2,0},{3,7},{4,6},{5,1},{6,4},{7,3},{8,10},{9,13},{10,... | collective-permute-start | bytes 245768 | tf_op jit(solution)/shard_map/ppermute | solution.py:366
  27.4 7.2 %collective-permute-start.4 = (f32[2,2,40,128]{3,2,1,0:T(8,128)S(1)}, f32[2,2,40,128]{3,2,1,0:T(8,128)S(1)}, u32[]{:S(2)}, u32[]{:S(2)}) collective-permute-start(f32[2,2,40,128]{3,2,1,0:T(8,128)S(1)} %pad_maximum_fusion.after.refs_0_), channel_id=1, source_target_pairs={{0,24},{2,26},{4,28},{6,30},{8,16},{10,18},{12,20},{14,22},{16,8},... | collective-permute-start | bytes 245768 | tf_op jit(solution)/shard_map/ppermute | solution.py:370
  29.1 8.2 %collective-permute-start.3 = (f32[2,2,40,128]{3,2,1,0:T(8,128)S(1)}, f32[2,2,40,128]{3,2,1,0:T(8,128)S(1)}, u32[]{:S(2)}, u32[]{:S(2)}) collective-permute-start(f32[2,2,40,128]{3,2,1,0:T(8,128)S(1)} %pad_maximum_fusion.after.refs_0_), channel_id=1, source_target_pairs={{0,16},{2,18},{4,20},{6,22},{8,24},{10,26},{12,28},{14,30},{16,0},... | collective-permute-start | bytes 245768 | tf_op jit(solution)/shard_map/ppermute | solution.py:370
  30.1 7.2 %collective-permute-start.2 = (f32[2,2,40,128]{3,2,1,0:T(8,128)S(1)}, f32[2,2,40,128]{3,2,1,0:T(8,128)S(1)}, u32[]{:S(2)}, u32[]{:S(2)}) collective-permute-start(f32[2,2,40,128]{3,2,1,0:T(8,128)S(1)} %pad_maximum_fusion.after.refs_0_), channel_id=1, source_target_pairs={{0,8},{2,10},{4,12},{6,14},{8,0},{10,2},{12,4},{14,6},{16,24},{18,... | collective-permute-start | bytes 245768 | tf_op jit(solution)/shard_map/ppermute | solution.py:370
  37.3 13.4 %copy-start.1 = (f32[2,2,16,1664]{3,2,1,0:T(8,128)S(1)}, f32[2,2,16,1664]{3,2,1,0:T(8,128)}, u32[]{:S(2)}) copy-start(f32[2,2,16,1664]{3,2,1,0:T(8,128)} %get-tuple-element.10.refs_8_) | copy-start | bytes 1277956
  37.3 9.9 %collective-permute-start.10 = (f32[3,2,2,40,128]{4,3,2,1,0:T(8,128)S(1)}, f32[3,2,2,40,128]{4,3,2,1,0:T(8,128)S(1)}, u32[]{:S(2)}, u32[]{:S(2)}) collective-permute-start(f32[3,2,2,40,128]{4,3,2,1,0:T(8,128)S(1)} %pack.1.refs_1_), channel_id=1, source_target_pairs={{0,6},{2,4},{4,2},{6,0},{8,14},{10,12},{12,10},{14,8},{16,22},{18,... | collective-permute-start | bytes 737288 | tf_op jit(solution)/shard_map/ppermute | solution.py:368
  38.1 12.5 %collective-permute-start.9 = (f32[3,2,2,40,128]{4,3,2,1,0:T(8,128)S(1)}, f32[3,2,2,40,128]{4,3,2,1,0:T(8,128)S(1)}, u32[]{:S(2)}, u32[]{:S(2)}) collective-permute-start(f32[3,2,2,40,128]{4,3,2,1,0:T(8,128)S(1)} %pack.1.refs_1_), channel_id=1, source_target_pairs={{0,4},{1,3},{2,6},{3,1},{4,0},{5,7},{6,2},{7,5},{8,12},{9,11},{10,... | collective-permute-start | bytes 737288 | tf_op jit(solution)/shard_map/ppermute | solution.py:367
  39.4 11.3 %collective-permute-start.8 = (f32[3,2,2,40,128]{4,3,2,1,0:T(8,128)S(1)}, f32[3,2,2,40,128]{4,3,2,1,0:T(8,128)S(1)}, u32[]{:S(2)}, u32[]{:S(2)}) collective-permute-start(f32[3,2,2,40,128]{4,3,2,1,0:T(8,128)S(1)} %pack.1.refs_1_), channel_id=1, source_target_pairs={{0,2},{1,5},{2,0},{3,7},{4,6},{5,1},{6,4},{7,3},{8,10},{9,13},{10,... | collective-permute-start | bytes 737288 | tf_op jit(solution)/shard_map/ppermute | solution.py:366
  40.8 2.4 %copy-start = (bf16[3328,768]{1,0:T(8,128)(2,1)S(1)}, bf16[3328,768]{1,0:T(8,128)(2,1)}, u32[]{:S(2)}) copy-start(bf16[3328,768]{1,0:T(8,128)(2,1)} %constant.18.clone.table_hbm) | copy-start | bytes 15335428
  55.4 2.5 %collective-permute-start.11 = (f32[2,36,4,768]{3,2,1,0:T(4,128)S(1)}, f32[2,36,4,768]{3,2,1,0:T(4,128)S(1)}, u32[]{:S(2)}, u32[]{:S(2)}) collective-permute-start(f32[2,36,4,768]{3,2,1,0:T(4,128)S(1)} %correlate.1.own), channel_id=1, source_target_pairs={{0,1},{1,0},{2,3},{3,2},{4,5},{5,4},{6,7},{7,6},{8,9},{9,8},{10,11... | collective-permute-start | bytes 2654216 | tf_op jit(solution)/shard_map/ppermute | solution.py:325

commit v3 on v2

--- a/solution.py
+++ b/solution.py
@@ -66,11 +66,13 @@
     for w in range(wins):
         for s in range(stas):
             k = w * stas + s
-            row = scale[k : k + 1]
+            weights = scale[k : k + 1]
             for i in range(comps):
-                y = x_ref[w, s, i] * row
+                y = x_ref[w, s, i] * weights
                 for part in range(2):
-                    rec_ref[w, part, pl.ds(i * stas + s, 1), :] = y[part : part + 1]
+                    for copy in range(2):
+                        row = pl.ds((copy * comps + i) * stas + s, 1)
+                        rec_ref[w, part, row, :] = y[part : part + 1]
                     for c in range(tiles):
                         pieces_ref[4 * s + place[w][part], pl.ds(i * tiles + c, 1), :] = y[
                             part : part + 1, c * LANES : (c + 1) * LANES
@@ -79,24 +81,16 @@
     if rest:
         for k in range(wins * stas * 2):
             pieces_ref[k, pl.ds(comps * tiles, rest), :] = jnp.zeros((rest, LANES), jnp.float32)
-    spare = rec_ref.shape[2] - comps * stas
-    if spare:
-        for w in range(wins):
-            for part in range(2):
-                rec_ref[w, part, pl.ds(comps * stas, spare), :] = jnp.zeros(
-                    (spare, bins), jnp.float32
-                )
 
 
 def whiten(spectra, flags):
     wins, stas, _, comps, bins = spectra.shape
     rows = -(-comps * (bins // LANES) // 8) * 8
-    recs = -(-comps * stas // 8) * 8
     return pl.pallas_call(
         whiten_kernel,
         out_shape=(
             jax.ShapeDtypeStruct((wins * stas * 2, rows, LANES), jnp.float32),
-            jax.ShapeDtypeStruct((wins, 2, recs, bins), jnp.float32),
+            jax.ShapeDtypeStruct((wins, 2, 2 * comps * stas, bins), jnp.float32),
         ),
         in_specs=[pl.BlockSpec(memory_space=pltpu.HBM)] * 2,
         out_specs=(
@@ -116,8 +110,8 @@
 def pick_kernel(params, got_ref, before, keep_ref, send_ref):
     half = keep_ref.shape[0]
     for t in range(half):
-        keep_ref[t] = got_ref[params[3 + t]]
-        send_ref[t] = got_ref[params[3 + half + t]]
+        keep_ref[t] = got_ref[params[t]]
+        send_ref[t] = got_ref[params[half + t]]
 
 
 def pick(params, got, before, steps):
@@ -171,38 +165,31 @@
     )(table, after)
 
 
-def correlate_kernel(params, *refs):
-    firsts, rests = refs[0:8:2], refs[1:8:2]
-    receivers_in, table, out_ref, rec, lhs = refs[8:10], refs[10], refs[11], refs[12], refs[13]
-    groups, steps, _, _ = firsts[0].shape
-    depth = 1 + rests[0].shape[0]
-    tiles = rec.shape[4] // LANES
-    window, part = params[1], params[2]
+def correlate_kernel(params, *refs, count):
+    spots_in = [refs[n * count : (n + 1) * count] for n in range(4)]
+    receivers_in, table, out_ref, lhs = refs[4 * count : 4 * count + 2], *refs[4 * count + 2 :]
+    _, groups, steps, _, _ = spots_in[0][0].shape
+    offsets = [(k, n) for k in range(count) for n in range(spots_in[0][k].shape[0])]
+    depth = len(offsets)
+    tiles = receivers_in[0].shape[3] // LANES
+    place, core = lax.axis_index("sta") & 3, lax.axis_index("win")
+    window, part = (place >> (1 - core)) & 1, (place >> core) & 1
     kinds = ((window, part), (part, window))
-    signs = []
-    for g, (w, p) in enumerate(kinds):
-        signs.append(1.0 - 2.0 * p.astype(jnp.float32))
-        for other_w in range(2):
-            for other_p in range(2):
-                rows = receivers_in[g][w ^ other_w, p ^ other_p, 0:12, :]
-                rec[g, other_w, other_p, 0:12, :] = rows
-                rec[g, other_w, other_p, 12:24, :] = rows
+    signs = [1.0 - 2.0 * p.astype(jnp.float32) for _, p in kinds]
     spots = (((0, 1), (2, 3)), ((0, 2), (1, 3)))
     upper = lax.broadcasted_iota(jnp.int32, (8, LANES), 0) < 4
 
     def source(spot, g, n, c):
-        t, offset, i = n // (3 * depth), (n // 3) % depth, n % 3
-        row = pl.ds(i * tiles + c, 1)
-        if offset:
-            line = rests[spot][offset - 1, g, t, row, :]
-        else:
-            line = firsts[spot][g, t, row, :]
+        t, (k, offset), i = n // (3 * depth), offsets[(n // 3) % depth], n % 3
+        line = spots_in[spot][k][offset, g, t, pl.ds(i * tiles + c, 1), :]
         return jnp.broadcast_to(line, (8, LANES))
 
     def chunk(c, carry):
         lanes = pl.ds(pl.multiple_of(c * LANES, LANES), LANES)
         receivers = [
-            [[rec[g, w, p, :, lanes] for p in range(2)] for w in range(2)] for g in range(groups)
+            [[receivers_in[g][kinds[g][0] ^ w, kinds[g][1] ^ p, :, lanes] for p in range(2)]
+             for w in range(2)]
+            for g in range(groups)
         ]
         for block in range(steps * depth * 3 // 4):
             real_tiles, imag_tiles = [], []
@@ -243,30 +230,32 @@
         result = jnp.dot(lhs[...], table[:, lags], preferred_element_type=jnp.float32)
         for t in range(steps):
             for offset in range(depth):
-                first = params[3 + 2 * steps + depth * t + offset] * 9
+                first = params[2 * steps + depth * t + offset] * 9
                 for k in range(9):
                     row = 4 * ((t * depth + offset) * 9 + k)
                     out_ref[t, first + k, :, lags] = result[row : row + 4]
 
 
 def correlate(params, sources, own, other, table):
-    steps = sources[0].shape[1]
-    depth = 1 + sources[1].shape[0]
+    count = len(sources[0])
+    steps = sources[0][0].shape[2]
+    depth = sum(value.shape[0] for value in sources[0])
     bins = own.shape[3]
     lags = table.shape[1]
+    rows = steps * depth * 3 * 12
     vmem = pl.BlockSpec(memory_space=pltpu.VMEM)
     return pl.pallas_call(
-        correlate_kernel,
+        functools.partial(correlate_kernel, count=count),
         out_shape=jax.ShapeDtypeStruct((steps, depth * 9, 4, lags), jnp.float32),
-        in_specs=[pl.BlockSpec(memory_space=pltpu.SMEM)] + [vmem] * 11,
+        in_specs=[pl.BlockSpec(memory_space=pltpu.SMEM)] + [vmem] * (4 * count + 3),
         out_specs=vmem,
-        scratch_shapes=[
-            pltpu.VMEM((2, 2, 2, 24, bins), jnp.float32),
-            pltpu.VMEM((steps * depth * 3 * 12, 2 * bins), jnp.bfloat16),
-        ],
+        scratch_shapes=[pltpu.VMEM((rows, 2 * bins), jnp.bfloat16)],
         compiler_params=pltpu.CompilerParams(vmem_limit_bytes=20 * MIB),
+        cost_estimate=pl.CostEstimate(
+            flops=4 * rows * bins * lags, bytes_accessed=8 * MIB, transcendentals=0
+        ),
         name="correlate",
-    )(params, *sources, own, other, table)
+    )(params, *[value for spot in sources for value in spot], own, other, table)
 
 
 def write_steps(half, out, core, sems):
@@ -333,8 +322,7 @@
     blocks = lax.axis_size("sta")
     pairs = owners.reshape(steps // 2, 2)
     slots = source_slots.reshape(steps // 2, 2, sources)
-    z, place = at >> 2, at & 3
-    high, low = place >> 1, place & 1
+    z = at >> 2
     mine = jnp.where(core == 0, slots[:, 0], slots[:, 1])
     held = z ^ jnp.arange(sources, dtype=jnp.int32)
     order = jnp.arange(sources, dtype=jnp.int32)
@@ -343,7 +331,6 @@
     )
     params = jnp.concatenate(
         [
-            jnp.stack([core, jnp.where(core == 0, high, low), jnp.where(core == 0, low, high)]),
             jnp.where(core == 0, pairs[:, 0], pairs[:, 1]),
             jnp.where(core == 0, pairs[:, 1], pairs[:, 0]),
             found.reshape(-1),
@@ -367,10 +354,11 @@
         side = lax.ppermute(value, ("sta", "win"), by_core(2, 1))
         return value, near, side, lax.ppermute(value, "sta", partner(3))
 
-    column = [lax.ppermute(mine, "sta", partner(4 * k)) for k in (1, 2, 3)]
+    far, farther = [lax.ppermute(mine, "sta", partner(4 * k)) for k in (2, 3)]
     first = plane(mine)
-    rest = plane(pack(column, first[1:]))
-    sources_in = [value for spot in zip(first, rest) for value in spot]
+    second = [lax.ppermute(value, "sta", partner(4)) for value in first]
+    rest = plane(pack((far, farther), first[1:]))
+    sources_in = [(a[None], b[None], c) for a, b, c in zip(first, second, rest)]
     table = jnp.asarray(lag_table(bins, NLAG, wins * lax.axis_size("win")))
     table = load(table, mine)
     half = correlate(params, sources_in, own, other, table)

time: 59.2 us -> 55.8 us (0.943)
  waiting for transfers between devices: 24.3 us -> 18.4 us
  starting transfers between devices: 19.8 us -> 22.2 us
    ppermute x2, waiting for transfers between devices: 3.61 us -> 0.23 us  [plane(): return (value, near, side, lax.ppermute(value, 'sta', partner(3)))]
    ppermute x2, waiting for transfers between devices: 3.44 us -> 0.89 us  [plane(): side = lax.ppermute(value, ('sta', 'win'), by_core(2, 1))]
    ppermute x3 -> x6, starting transfers between devices: 4.16 us -> 6.52 us  [the longest x4 4.05 us: on_device(): second = [lax.ppermute(value, 'sta', partner(4)) for value in first]]
    ppermute x3 -> x6, waiting for transfers between devices: 5.46 us -> 5.5 us  [the longest x2 5.18 us: on_device(): far, farther = [lax.ppermute(mine, 'sta', partner(4 * k)) for k in (2, 3)]]
  transfers between devices with their start and end apart: 13 -> 16, of which waited for: 8 -> 8; matrix products, arithmetic and copies ran while one was open for 3% -> 4% of each run, Pallas kernels for 3% -> 3%
where the time goes in v3:
time: 55.8 us; the launch traced here: 55.6 us
  starting transfers between devices  22.2 us (40%)
  waiting for transfers between devices  18.4 us (33%)
  Pallas kernels  10.3 us (18%)
  local copies, waits for them, and re-layouts  3.27 us (6%)
  other arithmetic  1.22 us (2%)
    all_to_all x1, waiting for transfers between devices, on_device(): got = lax.all_to_all(pieces, 'sta', 0, 0)  9.19 us
    all_to_all x1, starting transfers between devices, on_device(): got = lax.all_to_all(pieces, 'sta', 0, 0)  8.32 us
    ppermute x2, waiting for transfers between devices, on_device(): far, farther = [lax.ppermute(mine, 'sta', partner(4 * k)) for k in (2, 3)]  5.18 us
    pallas_call x1, Pallas kernels, correlate(): pl.pallas_call(functools.partial(correlate_kernel, count=count), out_shap...  4.8 us
    ppermute x4, starting transfers between devices, on_device(): second = [lax.ppermute(value, 'sta', partner(4)) for value in first]  4.05 us
    ppermute x2, starting transfers between devices, plane(): near = lax.ppermute(value, ('sta', 'win'), by_core(1, 2))  2.93 us
    ppermute x3, waiting for transfers between devices, swap(): return lax.ppermute(value, 'win', [(0, 1), (1, 0)])  2.63 us
    pallas_call x1, Pallas kernels, whiten(): pl.pallas_call(whiten_kernel, out_shape=(jax.ShapeDtypeStruct((wins * sta...  2.5 us
  transfers between devices with their start and end apart: 16, of which 8 were waited for; matrix products, arithmetic and copies ran while one was open for 4% of the time, Pallas kernels for 3%

profile of v3, /device:TPU:0, one launch (start us, length us, event | category | flops | bytes accessed | tf_op | source)
XLA Modules:
  0.0 55.6 jit_solution(9425934090651945243)
XLA Ops:
  0.0 2.5 %whiten.1 = (f32[16,40,128]{2,1,0:T(8,128)}, f32[2,2,24,1664]{3,2,1,0:T(8,128)}) custom-call(s32[2,4]{1,0:T(2,128)} %flags_hbm.1, f32[2,4,3,2,1664]{4,3,2,1,0:T(2,128)} %bitcast.25), custom_call_target="tpu_custom_call" | custom-call | tf_op jit(solution)/shard_map/whiten/pallas_call | solution.py:89
  2.5 8.3 %all-to-all-start = ((f32[16,40,128]{2,1,0:T(8,128)}), f32[16,40,128]{2,1,0:T(8,128)S(1)}, u32[]{:S(2)}, u32[]{:S(2)}) async-start(f32[16,40,128]{2,1,0:T(8,128)} %get-tuple-element.9), calls=%async_computation | async-start | bytes 655360 | tf_op jit(solution)/shard_map/all_to_all | solution.py:341
  10.9 0.7 %reshape.20 = s32[2,2]{1,0:T(2,128)S(1)} reshape(s32[4]{0:T(128)} %param.7) | data formatting | bytes 32 | tf_op jit(solution)/shard_map/reshape | solution.py:323
  11.7 0.8 %broadcast_select_fusion = s32[2,1,4]{2,1,0:T(1,128)S(1)} fusion(pred[]{:T(512)S(6)} %eq.20, s32[2,2,4]{2,1,0:T(2,128)} %bitcast.28), kind=kLoop, calls=%fused_computation.2 | loop fusion | flops 8 | bytes 97 | tf_op jit(solution)/shard_map/jit(_where)/select_n | solution.py:326
  12.4 0.2 select_reduce_fusion
  12.7 0.2 select_reduce_fusion.2
  13.0 9.2 %all-to-all-done.got_ref = f32[16,40,128]{2,1,0:T(8,128)S(1)} async-done(((f32[16,40,128]{2,1,0:T(8,128)}), f32[16,40,128]{2,1,0:T(8,128)S(1)}, u32[]{:S(2)}, u32[]{:S(2)}) %all-to-all-start) | async-done | bytes 327712 | tf_op jit(solution)/shard_map/all_to_all | solution.py:341
  22.2 0.6 pick.1
  22.8 1.2 %collective-permute-done.1 = f32[2,40,128]{2,1,0:T(8,128)S(1)} collective-permute-done((f32[2,40,128]{2,1,0:T(8,128)S(1)}, f32[2,40,128]{2,1,0:T(8,128)S(1)}, u32[]{:S(2)}, u32[]{:S(2)}) %collective-permute-start.1) | collective-permute-done | bytes 40992 | tf_op jit(solution)/shard_map/ppermute | solution.py:314
  24.0 0.8 %collective-permute-start.7 = (f32[2,2,40,128]{3,2,1,0:T(8,128)S(1)}, f32[2,2,40,128]{3,2,1,0:T(8,128)S(1)}, u32[]{:S(2)}, u32[]{:S(2)}) collective-permute-start(f32[2,2,40,128]{3,2,1,0:T(8,128)S(1)} %get-tuple-element.15.after), channel_id=1, source_target_pairs={{0,6},{2,4},{4,2},{6,0},{8,14},{10,12},{12,10},{14,8},{16,22},{18,... | collective-permute-start | bytes 245768 | tf_op jit(solution)/shard_map/ppermute | solution.py:355
  24.9 1.2 %collective-permute-start.6 = (f32[2,2,40,128]{3,2,1,0:T(8,128)S(1)}, f32[2,2,40,128]{3,2,1,0:T(8,128)S(1)}, u32[]{:S(2)}, u32[]{:S(2)}) collective-permute-start(f32[2,2,40,128]{3,2,1,0:T(8,128)S(1)} %get-tuple-element.15.after), channel_id=1, source_target_pairs={{0,4},{1,3},{2,6},{3,1},{4,0},{5,7},{6,2},{7,5},{8,12},{9,11},{10,... | collective-permute-start | bytes 245768 | tf_op jit(solution)/shard_map/ppermute | solution.py:354
  26.1 1.5 %collective-permute-start.5 = (f32[2,2,40,128]{3,2,1,0:T(8,128)S(1)}, f32[2,2,40,128]{3,2,1,0:T(8,128)S(1)}, u32[]{:S(2)}, u32[]{:S(2)}) collective-permute-start(f32[2,2,40,128]{3,2,1,0:T(8,128)S(1)} %get-tuple-element.15.after), channel_id=1, source_target_pairs={{0,2},{1,5},{2,0},{3,7},{4,6},{5,1},{6,4},{7,3},{8,10},{9,13},{10,... | collective-permute-start | bytes 245768 | tf_op jit(solution)/shard_map/ppermute | solution.py:353
  27.6 1.7 %collective-permute-start.4 = (f32[2,2,40,128]{3,2,1,0:T(8,128)S(1)}, f32[2,2,40,128]{3,2,1,0:T(8,128)S(1)}, u32[]{:S(2)}, u32[]{:S(2)}) collective-permute-start(f32[2,2,40,128]{3,2,1,0:T(8,128)S(1)} %get-tuple-element.15.after), channel_id=1, source_target_pairs={{0,24},{2,26},{4,28},{6,30},{8,16},{10,18},{12,20},{14,22},{16,8},... | collective-permute-start | bytes 245768 | tf_op jit(solution)/shard_map/ppermute | solution.py:357
  29.3 0.8 %collective-permute-start.3 = (f32[2,2,40,128]{3,2,1,0:T(8,128)S(1)}, f32[2,2,40,128]{3,2,1,0:T(8,128)S(1)}, u32[]{:S(2)}, u32[]{:S(2)}) collective-permute-start(f32[2,2,40,128]{3,2,1,0:T(8,128)S(1)} %get-tuple-element.15.after), channel_id=1, source_target_pairs={{0,16},{2,18},{4,20},{6,22},{8,24},{10,26},{12,28},{14,30},{16,0},... | collective-permute-start | bytes 245768 | tf_op jit(solution)/shard_map/ppermute | solution.py:357
  30.0 0.2 collective-permute-done.7.refs_4_
  30.3 1.7 %collective-permute-start.2 = (f32[2,2,40,128]{3,2,1,0:T(8,128)S(1)}, f32[2,2,40,128]{3,2,1,0:T(8,128)S(1)}, u32[]{:S(2)}, u32[]{:S(2)}) collective-permute-start(f32[2,2,40,128]{3,2,1,0:T(8,128)S(1)} %get-tuple-element.15.after), channel_id=1, source_target_pairs={{0,8},{2,10},{4,12},{6,14},{8,0},{10,2},{12,4},{14,6},{16,24},{18,... | collective-permute-start | bytes 245768 | tf_op jit(solution)/shard_map/ppermute | solution.py:359
  32.0 0.3 collective-permute-start.12
  32.3 2.5 %collective-permute-done.4.refs_1_ = f32[2,2,40,128]{3,2,1,0:T(8,128)S(1)} collective-permute-done((f32[2,2,40,128]{3,2,1,0:T(8,128)S(1)}, f32[2,2,40,128]{3,2,1,0:T(8,128)S(1)}, u32[]{:S(2)}, u32[]{:S(2)}) %collective-permute-start.4) | collective-permute-done | bytes 81952 | tf_op jit(solution)/shard_map/ppermute | solution.py:357
  34.8 2.7 %collective-permute-done.3.refs_0_ = f32[2,2,40,128]{3,2,1,0:T(8,128)S(1)} collective-permute-done((f32[2,2,40,128]{3,2,1,0:T(8,128)S(1)}, f32[2,2,40,128]{3,2,1,0:T(8,128)S(1)}, u32[]{:S(2)}, u32[]{:S(2)}) %collective-permute-start.3) | collective-permute-done | bytes 81952 | tf_op jit(solution)/shard_map/ppermute | solution.py:357
  37.5 0.8 %collective-permute-start.13 = (f32[2,2,2,40,128]{4,3,2,1,0:T(8,128)S(1)}, f32[2,2,2,40,128]{4,3,2,1,0:T(8,128)S(1)}, u32[]{:S(2)}, u32[]{:S(2)}) collective-permute-start(f32[2,2,2,40,128]{4,3,2,1,0:T(8,128)S(1)} %pack.1.refs_2_), channel_id=1, source_target_pairs={{0,6},{2,4},{4,2},{6,0},{8,14},{10,12},{12,10},{14,8},{16,22},{18,... | collective-permute-start | bytes 491528 | tf_op jit(solution)/shard_map/ppermute | solution.py:355
  38.4 1.2 %collective-permute-start.11 = (f32[2,2,2,40,128]{4,3,2,1,0:T(8,128)S(1)}, f32[2,2,2,40,128]{4,3,2,1,0:T(8,128)S(1)}, u32[]{:S(2)}, u32[]{:S(2)}) collective-permute-start(f32[2,2,2,40,128]{4,3,2,1,0:T(8,128)S(1)} %pack.1.refs_2_), channel_id=1, source_target_pairs={{0,4},{1,3},{2,6},{3,1},{4,0},{5,7},{6,2},{7,5},{8,12},{9,11},{10,... | collective-permute-start | bytes 491528 | tf_op jit(solution)/shard_map/ppermute | solution.py:354
  39.6 1.5 %collective-permute-start.9 = (f32[2,2,2,40,128]{4,3,2,1,0:T(8,128)S(1)}, f32[2,2,2,40,128]{4,3,2,1,0:T(8,128)S(1)}, u32[]{:S(2)}, u32[]{:S(2)}) collective-permute-start(f32[2,2,2,40,128]{4,3,2,1,0:T(8,128)S(1)} %pack.1.refs_2_), channel_id=1, source_target_pairs={{0,2},{1,5},{2,0},{3,7},{4,6},{5,1},{6,4},{7,3},{8,10},{9,13},{10,... | collective-permute-start | bytes 491528 | tf_op jit(solution)/shard_map/ppermute | solution.py:353
  41.1 2.0 %collective-permute-start.8 = (f32[2,2,40,128]{3,2,1,0:T(8,128)S(1)}, f32[2,2,40,128]{3,2,1,0:T(8,128)S(1)}, u32[]{:S(2)}, u32[]{:S(2)}) collective-permute-start(f32[2,2,40,128]{3,2,1,0:T(8,128)S(1)} %collective-permute-done.5.refs_2_), channel_id=1, source_target_pairs={{0,8},{2,10},{4,12},{6,14},{8,0},{10,2},{12,4},{14,6},{16,24},{18,... | collective-permute-start | bytes 245768 | tf_op jit(solution)/shard_map/ppermute | solution.py:359
  43.1 2.4 %copy-done = bf16[3328,768]{1,0:T(8,128)(2,1)S(1)} copy-done((bf16[3328,768]{1,0:T(8,128)(2,1)S(1)}, bf16[3328,768]{1,0:T(8,128)(2,1)}, u32[]{:S(2)}) %copy-start) | copy-done | bytes 5111832
  45.6 0.5 load.1.refs_14_
  46.1 0.3 collective-permute-done.8
  46.4 0.9 %collective-permute-done.11.refs_8_ = f32[2,2,2,40,128]{4,3,2,1,0:T(8,128)S(1)} collective-permute-done((f32[2,2,2,40,128]{4,3,2,1,0:T(8,128)S(1)}, f32[2,2,2,40,128]{4,3,2,1,0:T(8,128)S(1)}, u32[]{:S(2)}, u32[]{:S(2)}) %collective-permute-start.11) | collective-permute-done | bytes 163872 | tf_op jit(solution)/shard_map/ppermute | solution.py:354
  47.3 4.8 %correlate.1.own = f32[2,36,4,768]{3,2,1,0:T(4,128)S(1)} custom-call(s32[12]{0:T(128)S(1)} %pad_add_fusion.params, f32[1,2,2,40,128]{4,3,2,1,0:T(8,128)S(1)} %get-tuple-element.16.refs_0_, f32[1,2,2,40,128]{4,3,2,1,0:T(8,128)S(1)} %bitcast.20, f32[2,2,2,40,128]{4,3,2,1,0:T(8,128)S(1)} %pack.1.refs_2_, f32[1,2,2,40,128]{4,3,2,1,0:T(8,128)S(1)} %bitcast.19, ...), custom_call_target="tpu_custom_call" | custom-call | flops 1472200704 | bytes 8388608 | tf_op jit(solution)/shard_map/correlate/pallas_call | solution.py:247
  52.1 0.1 collective-permute-start.14
  52.2 1.0 %put.1.whole = f32[4,36,4,768]{3,2,1,0:T(4,128)} custom-call(f32[2,36,4,768]{3,2,1,0:T(4,128)S(1)} %correlate.1.own), custom_call_target="tpu_custom_call" | custom-call | tf_op jit(solution)/shard_map/put/pallas_call | solution.py:284
  53.2 1.4 %collective-permute-done.14.other = f32[2,36,4,768]{3,2,1,0:T(4,128)S(1)} collective-permute-done((f32[2,36,4,768]{3,2,1,0:T(4,128)S(1)}, f32[2,36,4,768]{3,2,1,0:T(4,128)S(1)}, u32[]{:S(2)}, u32[]{:S(2)}) %collective-permute-start.14) | collective-permute-done | bytes 884768 | tf_op jit(solution)/shard_map/ppermute | solution.py:314
  54.6 1.0 %join.1 = f32[4,36,4,768]{3,2,1,0:T(4,128)} custom-call(f32[2,36,4,768]{3,2,1,0:T(4,128)S(1)} %collective-permute-done.14.other, f32[4,36,4,768]{3,2,1,0:T(4,128)} %put.1.whole), custom_call_target="tpu_custom_call", output_to_operand_aliasing={{}: (1, {})} | custom-call | tf_op jit(solution)/shard_map/join/pallas_call | solution.py:301
  (19 shorter events, 0.4 us)
Async XLA Ops:
  2.5 19.6 %all-to-all-start = ((f32[16,40,128]{2,1,0:T(8,128)}), f32[16,40,128]{2,1,0:T(8,128)S(1)}, u32[]{:S(2)}, u32[]{:S(2)}) async-start(f32[16,40,128]{2,1,0:T(8,128)} %get-tuple-element.9), calls=%async_computation | async-start | bytes 655360 | tf_op jit(solution)/shard_map/all_to_all | solution.py:341
  10.8 11.3 %collective-permute-start = (f32[2,2,24,1664]{3,2,1,0:T(8,128)}, f32[2,2,24,1664]{3,2,1,0:T(8,128)S(1)}, u32[]{:S(2)}, u32[]{:S(2)}) collective-permute-start(f32[2,2,24,1664]{3,2,1,0:T(8,128)} %get-tuple-element.10.refs_12_), channel_id=1, source_target_pairs={{0,1},{1,0},{2,3},{3,2},{4,5},{5,4},{6,7},{7,6},{8,9},{9,8},{10,11... | collective-permute-start | bytes 1916936 | tf_op jit(solution)/shard_map/ppermute | solution.py:314
  22.7 1.3 %collective-permute-start.1 = (f32[2,40,128]{2,1,0:T(8,128)S(1)}, f32[2,40,128]{2,1,0:T(8,128)S(1)}, u32[]{:S(2)}, u32[]{:S(2)}) collective-permute-start(f32[2,40,128]{2,1,0:T(8,128)S(1)} %get-tuple-element.12), channel_id=1, source_target_pairs={{0,1},{1,0},{2,3},{3,2},{4,5},{5,4},{6,7},{7,6},{8,9},{9,8},{10,11... | collective-permute-start | bytes 122888 | tf_op jit(solution)/shard_map/ppermute | solution.py:314
  24.0 6.3 %collective-permute-start.7 = (f32[2,2,40,128]{3,2,1,0:T(8,128)S(1)}, f32[2,2,40,128]{3,2,1,0:T(8,128)S(1)}, u32[]{:S(2)}, u32[]{:S(2)}) collective-permute-start(f32[2,2,40,128]{3,2,1,0:T(8,128)S(1)} %get-tuple-element.15.after), channel_id=1, source_target_pairs={{0,6},{2,4},{4,2},{6,0},{8,14},{10,12},{12,10},{14,8},{16,22},{18,... | collective-permute-start | bytes 245768 | tf_op jit(solution)/shard_map/ppermute | solution.py:355
  24.9 7.1 %collective-permute-start.6 = (f32[2,2,40,128]{3,2,1,0:T(8,128)S(1)}, f32[2,2,40,128]{3,2,1,0:T(8,128)S(1)}, u32[]{:S(2)}, u32[]{:S(2)}) collective-permute-start(f32[2,2,40,128]{3,2,1,0:T(8,128)S(1)} %get-tuple-element.15.after), channel_id=1, source_target_pairs={{0,4},{1,3},{2,6},{3,1},{4,0},{5,7},{6,2},{7,5},{8,12},{9,11},{10,... | collective-permute-start | bytes 245768 | tf_op jit(solution)/shard_map/ppermute | solution.py:354
  26.1 6.2 %collective-permute-start.5 = (f32[2,2,40,128]{3,2,1,0:T(8,128)S(1)}, f32[2,2,40,128]{3,2,1,0:T(8,128)S(1)}, u32[]{:S(2)}, u32[]{:S(2)}) collective-permute-start(f32[2,2,40,128]{3,2,1,0:T(8,128)S(1)} %get-tuple-element.15.after), channel_id=1, source_target_pairs={{0,2},{1,5},{2,0},{3,7},{4,6},{5,1},{6,4},{7,3},{8,10},{9,13},{10,... | collective-permute-start | bytes 245768 | tf_op jit(solution)/shard_map/ppermute | solution.py:353
  27.6 7.2 %collective-permute-start.4 = (f32[2,2,40,128]{3,2,1,0:T(8,128)S(1)}, f32[2,2,40,128]{3,2,1,0:T(8,128)S(1)}, u32[]{:S(2)}, u32[]{:S(2)}) collective-permute-start(f32[2,2,40,128]{3,2,1,0:T(8,128)S(1)} %get-tuple-element.15.after), channel_id=1, source_target_pairs={{0,24},{2,26},{4,28},{6,30},{8,16},{10,18},{12,20},{14,22},{16,8},... | collective-permute-start | bytes 245768 | tf_op jit(solution)/shard_map/ppermute | solution.py:357
  29.3 8.2 %collective-permute-start.3 = (f32[2,2,40,128]{3,2,1,0:T(8,128)S(1)}, f32[2,2,40,128]{3,2,1,0:T(8,128)S(1)}, u32[]{:S(2)}, u32[]{:S(2)}) collective-permute-start(f32[2,2,40,128]{3,2,1,0:T(8,128)S(1)} %get-tuple-element.15.after), channel_id=1, source_target_pairs={{0,16},{2,18},{4,20},{6,22},{8,24},{10,26},{12,28},{14,30},{16,0},... | collective-permute-start | bytes 245768 | tf_op jit(solution)/shard_map/ppermute | solution.py:357
  30.3 10.8 %collective-permute-start.2 = (f32[2,2,40,128]{3,2,1,0:T(8,128)S(1)}, f32[2,2,40,128]{3,2,1,0:T(8,128)S(1)}, u32[]{:S(2)}, u32[]{:S(2)}) collective-permute-start(f32[2,2,40,128]{3,2,1,0:T(8,128)S(1)} %get-tuple-element.15.after), channel_id=1, source_target_pairs={{0,8},{2,10},{4,12},{6,14},{8,0},{10,2},{12,4},{14,6},{16,24},{18,... | collective-permute-start | bytes 245768 | tf_op jit(solution)/shard_map/ppermute | solution.py:359
  32.0 9.1 %collective-permute-start.12 = (f32[2,2,40,128]{3,2,1,0:T(8,128)S(1)}, f32[2,2,40,128]{3,2,1,0:T(8,128)S(1)}, u32[]{:S(2)}, u32[]{:S(2)}) collective-permute-start(f32[2,2,40,128]{3,2,1,0:T(8,128)S(1)} %collective-permute-done.7.refs_4_), channel_id=1, source_target_pairs={{0,8},{2,10},{4,12},{6,14},{8,0},{10,2},{12,4},{14,6},{16,24},{18,... | collective-permute-start | bytes 245768 | tf_op jit(solution)/shard_map/ppermute | solution.py:359
  37.5 8.9 %collective-permute-start.13 = (f32[2,2,2,40,128]{4,3,2,1,0:T(8,128)S(1)}, f32[2,2,2,40,128]{4,3,2,1,0:T(8,128)S(1)}, u32[]{:S(2)}, u32[]{:S(2)}) collective-permute-start(f32[2,2,2,40,128]{4,3,2,1,0:T(8,128)S(1)} %pack.1.refs_2_), channel_id=1, source_target_pairs={{0,6},{2,4},{4,2},{6,0},{8,14},{10,12},{12,10},{14,8},{16,22},{18,... | collective-permute-start | bytes 491528 | tf_op jit(solution)/shard_map/ppermute | solution.py:355
  38.4 8.9 %collective-permute-start.11 = (f32[2,2,2,40,128]{4,3,2,1,0:T(8,128)S(1)}, f32[2,2,2,40,128]{4,3,2,1,0:T(8,128)S(1)}, u32[]{:S(2)}, u32[]{:S(2)}) collective-permute-start(f32[2,2,2,40,128]{4,3,2,1,0:T(8,128)S(1)} %pack.1.refs_2_), channel_id=1, source_target_pairs={{0,4},{1,3},{2,6},{3,1},{4,0},{5,7},{6,2},{7,5},{8,12},{9,11},{10,... | collective-permute-start | bytes 491528 | tf_op jit(solution)/shard_map/ppermute | solution.py:354
  39.6 7.7 %collective-permute-start.9 = (f32[2,2,2,40,128]{4,3,2,1,0:T(8,128)S(1)}, f32[2,2,2,40,128]{4,3,2,1,0:T(8,128)S(1)}, u32[]{:S(2)}, u32[]{:S(2)}) collective-permute-start(f32[2,2,2,40,128]{4,3,2,1,0:T(8,128)S(1)} %pack.1.refs_2_), channel_id=1, source_target_pairs={{0,2},{1,5},{2,0},{3,7},{4,6},{5,1},{6,4},{7,3},{8,10},{9,13},{10,... | collective-permute-start | bytes 491528 | tf_op jit(solution)/shard_map/ppermute | solution.py:353
  41.1 5.0 %collective-permute-start.10 = (f32[2,2,40,128]{3,2,1,0:T(8,128)S(1)}, f32[2,2,40,128]{3,2,1,0:T(8,128)S(1)}, u32[]{:S(2)}, u32[]{:S(2)}) collective-permute-start(f32[2,2,40,128]{3,2,1,0:T(8,128)S(1)} %collective-permute-done.6.refs_3_), channel_id=1, source_target_pairs={{0,8},{2,10},{4,12},{6,14},{8,0},{10,2},{12,4},{14,6},{16,24},{18,... | collective-permute-start | bytes 245768 | tf_op jit(solution)/shard_map/ppermute | solution.py:359
  41.1 5.3 %collective-permute-start.8 = (f32[2,2,40,128]{3,2,1,0:T(8,128)S(1)}, f32[2,2,40,128]{3,2,1,0:T(8,128)S(1)}, u32[]{:S(2)}, u32[]{:S(2)}) collective-permute-start(f32[2,2,40,128]{3,2,1,0:T(8,128)S(1)} %collective-permute-done.5.refs_2_), channel_id=1, source_target_pairs={{0,8},{2,10},{4,12},{6,14},{8,0},{10,2},{12,4},{14,6},{16,24},{18,... | collective-permute-start | bytes 245768 | tf_op jit(solution)/shard_map/ppermute | solution.py:359
  43.1 2.4 %copy-start = (bf16[3328,768]{1,0:T(8,128)(2,1)S(1)}, bf16[3328,768]{1,0:T(8,128)(2,1)}, u32[]{:S(2)}) copy-start(bf16[3328,768]{1,0:T(8,128)(2,1)} %constant.14.clone.table_hbm) | copy-start | bytes 15335428
  45.6 1.7 %copy-start.1 = (f32[2,2,24,1664]{3,2,1,0:T(8,128)S(1)}, f32[2,2,24,1664]{3,2,1,0:T(8,128)}, u32[]{:S(2)}) copy-start(f32[2,2,24,1664]{3,2,1,0:T(8,128)} %get-tuple-element.10.refs_12_) | copy-start | bytes 1916932
  52.1 2.5 %collective-permute-start.14 = (f32[2,36,4,768]{3,2,1,0:T(4,128)S(1)}, f32[2,36,4,768]{3,2,1,0:T(4,128)S(1)}, u32[]{:S(2)}, u32[]{:S(2)}) collective-permute-start(f32[2,36,4,768]{3,2,1,0:T(4,128)S(1)} %correlate.1.own), channel_id=1, source_target_pairs={{0,1},{1,0},{2,3},{3,2},{4,5},{5,4},{6,7},{7,6},{8,9},{9,8},{10,11... | collective-permute-start | bytes 2654216 | tf_op jit(solution)/shard_map/ppermute | solution.py:314

commit v4 on v3

--- a/solution.py
+++ b/solution.py
@@ -129,8 +129,8 @@
 
 
 def pack_kernel(*refs, count):
-    for n in range(count):
-        refs[-1][n] = refs[n][...]
+    for n, value in enumerate(refs[-1 - count : -1]):
+        refs[-1][n] = value[...]
 
 
 def pack(values, before):
@@ -142,7 +142,7 @@
         out_specs=vmem,
         compiler_params=pltpu.CompilerParams(vmem_limit_bytes=8 * MIB),
         name="pack",
-    )(*values, *before)
+    )(*before, *values)
 
 
 def load_kernel(table_hbm, after, out_ref, sem):
@@ -354,13 +354,12 @@
         side = lax.ppermute(value, ("sta", "win"), by_core(2, 1))
         return value, near, side, lax.ppermute(value, "sta", partner(3))
 
+    first = plane(mine)
     far, farther = [lax.ppermute(mine, "sta", partner(4 * k)) for k in (2, 3)]
-    first = plane(mine)
     second = [lax.ppermute(value, "sta", partner(4)) for value in first]
-    rest = plane(pack((far, farther), first[1:]))
+    table = load(jnp.asarray(lag_table(bins, NLAG, wins * lax.axis_size("win"))), mine)
+    rest = plane(pack((far, farther), (*first[1:], table)))
     sources_in = [(a[None], b[None], c) for a, b, c in zip(first, second, rest)]
-    table = jnp.asarray(lag_table(bins, NLAG, wins * lax.axis_size("win")))
-    table = load(table, mine)
     half = correlate(params, sources_in, own, other, table)
     whole = join(swap(half), put(half))
     return whole.reshape(steps, sources, comps, comps, stas, NLAG).transpose(0, 1, 2, 4, 3, 5)

time: 55.8 us -> 53.5 us (0.959)
  waiting for transfers between devices: 18.4 us -> 15.1 us
  starting transfers between devices: 22.2 us -> 23.1 us
    ppermute x2, waiting for transfers between devices: 5.18 us -> 0.01 us  [on_device(): far, farther = [lax.ppermute(mine, 'sta', partner(4 * k)) for k in (2, 3)]]
    ppermute x4, waiting for transfers between devices: 0.31 us -> 3.29 us  [on_device(): second = [lax.ppermute(value, 'sta', partner(4)) for value in first]]
    ppermute x2, starting transfers between devices: 2.46 us -> 3.43 us  [on_device(): far, farther = [lax.ppermute(mine, 'sta', partner(4 * k)) for k in (2, 3)]]
    ppermute x2, waiting for transfers between devices: 0.89 us -> 0.01 us  [plane(): side = lax.ppermute(value, ('sta', 'win'), by_core(2, 1))]
    ppermute x2, starting transfers between devices: 2.93 us -> 2.07 us  [plane(): near = lax.ppermute(value, ('sta', 'win'), by_core(1, 2))]
    ppermute x2, starting transfers between devices: 2.49 us -> 3.12 us  [plane(): side = lax.ppermute(value, ('sta', 'win'), by_core(2, 1))]
  transfers between devices with their start and end apart: 16 -> 16, of which waited for: 8 -> 5; matrix products, arithmetic and copies ran while one was open for 4% -> 4% of each run, Pallas kernels for 3% -> 3%
where the time goes in v4:
time: 53.5 us; the launch traced here: 53.3 us
  starting transfers between devices  23.1 us (43%)
  waiting for transfers between devices  15.1 us (28%)
  Pallas kernels  10.3 us (19%)
  local copies, waits for them, and re-layouts  3.28 us (6%)
  other arithmetic  1.22 us (2%)
    all_to_all x1, waiting for transfers between devices, on_device(): got = lax.all_to_all(pieces, 'sta', 0, 0)  9.19 us
    all_to_all x1, starting transfers between devices, on_device(): got = lax.all_to_all(pieces, 'sta', 0, 0)  8.32 us
    pallas_call x1, Pallas kernels, correlate(): pl.pallas_call(functools.partial(correlate_kernel, count=count), out_shap...  4.81 us
    ppermute x4, starting transfers between devices, on_device(): second = [lax.ppermute(value, 'sta', partner(4)) for value in first]  4.12 us
    ppermute x2, starting transfers between devices, on_device(): far, farther = [lax.ppermute(mine, 'sta', partner(4 * k)) for k in (2, 3)]  3.43 us
    ppermute x4, waiting for transfers between devices, on_device(): second = [lax.ppermute(value, 'sta', partner(4)) for value in first]  3.29 us
    ppermute x2, starting transfers between devices, plane(): side = lax.ppermute(value, ('sta', 'win'), by_core(2, 1))  3.12 us
    ppermute x3, waiting for transfers between devices, swap(): return lax.ppermute(value, 'win', [(0, 1), (1, 0)])  2.64 us
  transfers between devices with their start and end apart: 16, of which 5 were waited for; matrix products, arithmetic and copies ran while one was open for 4% of the time, Pallas kernels for 3%

profile of v4, /device:TPU:0, one launch (start us, length us, event | category | flops | bytes accessed | tf_op | source)
XLA Modules:
  0.0 53.3 jit_solution(15913409022745222512)
XLA Ops:
  0.0 2.5 %whiten.1 = (f32[16,40,128]{2,1,0:T(8,128)}, f32[2,2,24,1664]{3,2,1,0:T(8,128)}) custom-call(s32[2,4]{1,0:T(2,128)} %flags_hbm.1, f32[2,4,3,2,1664]{4,3,2,1,0:T(2,128)} %bitcast.25), custom_call_target="tpu_custom_call" | custom-call | tf_op jit(solution)/shard_map/whiten/pallas_call | solution.py:89
  2.5 8.3 %all-to-all-start = ((f32[16,40,128]{2,1,0:T(8,128)}), f32[16,40,128]{2,1,0:T(8,128)S(1)}, u32[]{:S(2)}, u32[]{:S(2)}) async-start(f32[16,40,128]{2,1,0:T(8,128)} %get-tuple-element.9), calls=%async_computation | async-start | bytes 655360 | tf_op jit(solution)/shard_map/all_to_all | solution.py:341
  10.9 0.7 %reshape.20 = s32[2,2]{1,0:T(2,128)S(1)} reshape(s32[4]{0:T(128)} %param.7) | data formatting | bytes 32 | tf_op jit(solution)/shard_map/reshape | solution.py:323
  11.7 0.8 %broadcast_select_fusion = s32[2,1,4]{2,1,0:T(1,128)S(1)} fusion(pred[]{:T(512)S(6)} %eq.20, s32[2,2,4]{2,1,0:T(2,128)} %bitcast.28), kind=kLoop, calls=%fused_computation.2 | loop fusion | flops 8 | bytes 97 | tf_op jit(solution)/shard_map/jit(_where)/select_n | solution.py:326
  12.4 0.2 select_reduce_fusion
  12.6 0.1 reshape.22
  12.7 0.2 select_reduce_fusion.2
  12.9 0.1 pad_add_fusion.params
  13.0 9.2 %all-to-all-done.got_ref = f32[16,40,128]{2,1,0:T(8,128)S(1)} async-done(((f32[16,40,128]{2,1,0:T(8,128)}), f32[16,40,128]{2,1,0:T(8,128)S(1)}, u32[]{:S(2)}, u32[]{:S(2)}) %all-to-all-start) | async-done | bytes 327712 | tf_op jit(solution)/shard_map/all_to_all | solution.py:341
  22.2 0.6 %pick.1 = (f32[2,40,128]{2,1,0:T(8,128)S(1)}, f32[2,40,128]{2,1,0:T(8,128)S(1)}) custom-call(s32[12]{0:T(128)S(1)} %pad_add_fusion.params, f32[16,40,128]{2,1,0:T(8,128)S(1)} %all-to-all-done.got_ref, f32[2,2,24,1664]{3,2,1,0:T(8,128)S(1)} %collective-permute-done.before.refs_13_), custom_call_target="tpu_custom_call" | custom-call | tf_op jit(solution)/shard_map/pick/pallas_call | solution.py:121
  22.7 0.1 collective-permute-start.1
  22.8 1.2 %collective-permute-done.1 = f32[2,40,128]{2,1,0:T(8,128)S(1)} collective-permute-done((f32[2,40,128]{2,1,0:T(8,128)S(1)}, f32[2,40,128]{2,1,0:T(8,128)S(1)}, u32[]{:S(2)}, u32[]{:S(2)}) %collective-permute-start.1) | collective-permute-done | bytes 40992 | tf_op jit(solution)/shard_map/ppermute | solution.py:314
  24.0 0.4 collective-permute-start.6
  24.5 1.0 %collective-permute-start.5 = (f32[2,2,40,128]{3,2,1,0:T(8,128)S(1)}, f32[2,2,40,128]{3,2,1,0:T(8,128)S(1)}, u32[]{:S(2)}, u32[]{:S(2)}) collective-permute-start(f32[2,2,40,128]{3,2,1,0:T(8,128)S(1)} %get-tuple-element.15.after), channel_id=1, source_target_pairs={{0,6},{2,4},{4,2},{6,0},{8,14},{10,12},{12,10},{14,8},{16,22},{18,... | collective-permute-start | bytes 245768 | tf_op jit(solution)/shard_map/ppermute | solution.py:355
  25.5 1.9 %collective-permute-start.4 = (f32[2,2,40,128]{3,2,1,0:T(8,128)S(1)}, f32[2,2,40,128]{3,2,1,0:T(8,128)S(1)}, u32[]{:S(2)}, u32[]{:S(2)}) collective-permute-start(f32[2,2,40,128]{3,2,1,0:T(8,128)S(1)} %get-tuple-element.15.after), channel_id=1, source_target_pairs={{0,4},{1,3},{2,6},{3,1},{4,0},{5,7},{6,2},{7,5},{8,12},{9,11},{10,... | collective-permute-start | bytes 245768 | tf_op jit(solution)/shard_map/ppermute | solution.py:354
  27.3 0.6 %collective-permute-start.3 = (f32[2,2,40,128]{3,2,1,0:T(8,128)S(1)}, f32[2,2,40,128]{3,2,1,0:T(8,128)S(1)}, u32[]{:S(2)}, u32[]{:S(2)}) collective-permute-start(f32[2,2,40,128]{3,2,1,0:T(8,128)S(1)} %get-tuple-element.15.after), channel_id=1, source_target_pairs={{0,2},{1,5},{2,0},{3,7},{4,6},{5,1},{6,4},{7,3},{8,10},{9,13},{10,... | collective-permute-start | bytes 245768 | tf_op jit(solution)/shard_map/ppermute | solution.py:353
  27.9 3.0 %collective-permute-start.7 = (f32[2,2,40,128]{3,2,1,0:T(8,128)S(1)}, f32[2,2,40,128]{3,2,1,0:T(8,128)S(1)}, u32[]{:S(2)}, u32[]{:S(2)}) collective-permute-start(f32[2,2,40,128]{3,2,1,0:T(8,128)S(1)} %get-tuple-element.15.after), channel_id=1, source_target_pairs={{0,24},{2,26},{4,28},{6,30},{8,16},{10,18},{12,20},{14,22},{16,8},... | collective-permute-start | bytes 245768 | tf_op jit(solution)/shard_map/ppermute | solution.py:358
  30.9 2.4 %copy-done = bf16[3328,768]{1,0:T(8,128)(2,1)S(1)} copy-done((bf16[3328,768]{1,0:T(8,128)(2,1)S(1)}, bf16[3328,768]{1,0:T(8,128)(2,1)}, u32[]{:S(2)}) %copy-start) | copy-done | bytes 5111832
  33.4 0.5 load.1.refs_3_.refs_14_
  33.9 0.2 collective-permute-start.2
  34.2 1.9 %collective-permute-start.12 = (f32[2,2,40,128]{3,2,1,0:T(8,128)S(1)}, f32[2,2,40,128]{3,2,1,0:T(8,128)S(1)}, u32[]{:S(2)}, u32[]{:S(2)}) collective-permute-start(f32[2,2,40,128]{3,2,1,0:T(8,128)S(1)} %collective-permute-done.5.refs_2_), channel_id=1, source_target_pairs={{0,8},{2,10},{4,12},{6,14},{8,0},{10,2},{12,4},{14,6},{16,24},{18,... | collective-permute-start | bytes 245768 | tf_op jit(solution)/shard_map/ppermute | solution.py:359
  36.1 0.8 %collective-permute-start.13 = (f32[2,2,2,40,128]{4,3,2,1,0:T(8,128)S(1)}, f32[2,2,2,40,128]{4,3,2,1,0:T(8,128)S(1)}, u32[]{:S(2)}, u32[]{:S(2)}) collective-permute-start(f32[2,2,2,40,128]{4,3,2,1,0:T(8,128)S(1)} %pack.1.refs_2_), channel_id=1, source_target_pairs={{0,6},{2,4},{4,2},{6,0},{8,14},{10,12},{12,10},{14,8},{16,22},{18,... | collective-permute-start | bytes 491528 | tf_op jit(solution)/shard_map/ppermute | solution.py:355
  36.9 1.2 %collective-permute-start.11 = (f32[2,2,2,40,128]{4,3,2,1,0:T(8,128)S(1)}, f32[2,2,2,40,128]{4,3,2,1,0:T(8,128)S(1)}, u32[]{:S(2)}, u32[]{:S(2)}) collective-permute-start(f32[2,2,2,40,128]{4,3,2,1,0:T(8,128)S(1)} %pack.1.refs_2_), channel_id=1, source_target_pairs={{0,4},{1,3},{2,6},{3,1},{4,0},{5,7},{6,2},{7,5},{8,12},{9,11},{10,... | collective-permute-start | bytes 491528 | tf_op jit(solution)/shard_map/ppermute | solution.py:354
  38.2 1.5 %collective-permute-start.9 = (f32[2,2,2,40,128]{4,3,2,1,0:T(8,128)S(1)}, f32[2,2,2,40,128]{4,3,2,1,0:T(8,128)S(1)}, u32[]{:S(2)}, u32[]{:S(2)}) collective-permute-start(f32[2,2,2,40,128]{4,3,2,1,0:T(8,128)S(1)} %pack.1.refs_2_), channel_id=1, source_target_pairs={{0,2},{1,5},{2,0},{3,7},{4,6},{5,1},{6,4},{7,3},{8,10},{9,13},{10,... | collective-permute-start | bytes 491528 | tf_op jit(solution)/shard_map/ppermute | solution.py:353
  39.6 0.1 collective-permute-start.10
  39.8 1.9 %collective-permute-start.8 = (f32[2,2,40,128]{3,2,1,0:T(8,128)S(1)}, f32[2,2,40,128]{3,2,1,0:T(8,128)S(1)}, u32[]{:S(2)}, u32[]{:S(2)}) collective-permute-start(f32[2,2,40,128]{3,2,1,0:T(8,128)S(1)} %collective-permute-done.3.refs_0_), channel_id=1, source_target_pairs={{0,8},{2,10},{4,12},{6,14},{8,0},{10,2},{12,4},{14,6},{16,24},{18,... | collective-permute-start | bytes 245768 | tf_op jit(solution)/shard_map/ppermute | solution.py:359
  41.7 2.4 %collective-permute-done.10 = f32[2,2,40,128]{3,2,1,0:T(8,128)S(1)} collective-permute-done((f32[2,2,40,128]{3,2,1,0:T(8,128)S(1)}, f32[2,2,40,128]{3,2,1,0:T(8,128)S(1)}, u32[]{:S(2)}, u32[]{:S(2)}) %collective-permute-start.10) | collective-permute-done | bytes 81952 | tf_op jit(solution)/shard_map/ppermute | solution.py:359
  44.1 0.9 %collective-permute-done.8 = f32[2,2,40,128]{3,2,1,0:T(8,128)S(1)} collective-permute-done((f32[2,2,40,128]{3,2,1,0:T(8,128)S(1)}, f32[2,2,40,128]{3,2,1,0:T(8,128)S(1)}, u32[]{:S(2)}, u32[]{:S(2)}) %collective-permute-start.8) | collective-permute-done | bytes 81952 | tf_op jit(solution)/shard_map/ppermute | solution.py:359
  45.0 4.8 %correlate.1.own = f32[2,36,4,768]{3,2,1,0:T(4,128)S(1)} custom-call(s32[12]{0:T(128)S(1)} %pad_add_fusion.params, f32[1,2,2,40,128]{4,3,2,1,0:T(8,128)S(1)} %get-tuple-element.16.refs_0_, f32[1,2,2,40,128]{4,3,2,1,0:T(8,128)S(1)} %bitcast.20, f32[2,2,2,40,128]{4,3,2,1,0:T(8,128)S(1)} %pack.1.refs_2_, f32[1,2,2,40,128]{4,3,2,1,0:T(8,128)S(1)} %bitcast.19, ...), custom_call_target="tpu_custom_call" | custom-call | flops 1472200704 | bytes 8388608 | tf_op jit(solution)/shard_map/correlate/pallas_call | solution.py:247
  49.9 1.0 %put.1.whole = f32[4,36,4,768]{3,2,1,0:T(4,128)} custom-call(f32[2,36,4,768]{3,2,1,0:T(4,128)S(1)} %correlate.1.own), custom_call_target="tpu_custom_call" | custom-call | tf_op jit(solution)/shard_map/put/pallas_call | solution.py:284
  50.9 1.4 %collective-permute-done.14.other = f32[2,36,4,768]{3,2,1,0:T(4,128)S(1)} collective-permute-done((f32[2,36,4,768]{3,2,1,0:T(4,128)S(1)}, f32[2,36,4,768]{3,2,1,0:T(4,128)S(1)}, u32[]{:S(2)}, u32[]{:S(2)}) %collective-permute-start.14) | collective-permute-done | bytes 884768 | tf_op jit(solution)/shard_map/ppermute | solution.py:314
  52.3 1.0 %join.1 = f32[4,36,4,768]{3,2,1,0:T(4,128)} custom-call(f32[2,36,4,768]{3,2,1,0:T(4,128)S(1)} %collective-permute-done.14.other, f32[4,36,4,768]{3,2,1,0:T(4,128)} %put.1.whole), custom_call_target="tpu_custom_call", output_to_operand_aliasing={{}: (1, {})} | custom-call | tf_op jit(solution)/shard_map/join/pallas_call | solution.py:301
  (19 shorter events, 0.2 us)
Async XLA Ops:
  2.5 19.6 %all-to-all-start = ((f32[16,40,128]{2,1,0:T(8,128)}), f32[16,40,128]{2,1,0:T(8,128)S(1)}, u32[]{:S(2)}, u32[]{:S(2)}) async-start(f32[16,40,128]{2,1,0:T(8,128)} %get-tuple-element.9), calls=%async_computation | async-start | bytes 655360 | tf_op jit(solution)/shard_map/all_to_all | solution.py:341
  10.8 11.3 %collective-permute-start = (f32[2,2,24,1664]{3,2,1,0:T(8,128)}, f32[2,2,24,1664]{3,2,1,0:T(8,128)S(1)}, u32[]{:S(2)}, u32[]{:S(2)}) collective-permute-start(f32[2,2,24,1664]{3,2,1,0:T(8,128)} %get-tuple-element.10.refs_12_), channel_id=1, source_target_pairs={{0,1},{1,0},{2,3},{3,2},{4,5},{5,4},{6,7},{7,6},{8,9},{9,8},{10,11... | collective-permute-start | bytes 1916936 | tf_op jit(solution)/shard_map/ppermute | solution.py:314
  22.7 1.3 %collective-permute-start.1 = (f32[2,40,128]{2,1,0:T(8,128)S(1)}, f32[2,40,128]{2,1,0:T(8,128)S(1)}, u32[]{:S(2)}, u32[]{:S(2)}) collective-permute-start(f32[2,40,128]{2,1,0:T(8,128)S(1)} %get-tuple-element.12), channel_id=1, source_target_pairs={{0,1},{1,0},{2,3},{3,2},{4,5},{5,4},{6,7},{7,6},{8,9},{9,8},{10,11... | collective-permute-start | bytes 122888 | tf_op jit(solution)/shard_map/ppermute | solution.py:314
  24.0 9.9 %collective-permute-start.6 = (f32[2,2,40,128]{3,2,1,0:T(8,128)S(1)}, f32[2,2,40,128]{3,2,1,0:T(8,128)S(1)}, u32[]{:S(2)}, u32[]{:S(2)}) collective-permute-start(f32[2,2,40,128]{3,2,1,0:T(8,128)S(1)} %get-tuple-element.15.after), channel_id=1, source_target_pairs={{0,16},{2,18},{4,20},{6,22},{8,24},{10,26},{12,28},{14,30},{16,0},... | collective-permute-start | bytes 245768 | tf_op jit(solution)/shard_map/ppermute | solution.py:358
  24.5 9.7 %collective-permute-start.5 = (f32[2,2,40,128]{3,2,1,0:T(8,128)S(1)}, f32[2,2,40,128]{3,2,1,0:T(8,128)S(1)}, u32[]{:S(2)}, u32[]{:S(2)}) collective-permute-start(f32[2,2,40,128]{3,2,1,0:T(8,128)S(1)} %get-tuple-element.15.after), channel_id=1, source_target_pairs={{0,6},{2,4},{4,2},{6,0},{8,14},{10,12},{12,10},{14,8},{16,22},{18,... | collective-permute-start | bytes 245768 | tf_op jit(solution)/shard_map/ppermute | solution.py:355
  25.5 10.6 %collective-permute-start.4 = (f32[2,2,40,128]{3,2,1,0:T(8,128)S(1)}, f32[2,2,40,128]{3,2,1,0:T(8,128)S(1)}, u32[]{:S(2)}, u32[]{:S(2)}) collective-permute-start(f32[2,2,40,128]{3,2,1,0:T(8,128)S(1)} %get-tuple-element.15.after), channel_id=1, source_target_pairs={{0,4},{1,3},{2,6},{3,1},{4,0},{5,7},{6,2},{7,5},{8,12},{9,11},{10,... | collective-permute-start | bytes 245768 | tf_op jit(solution)/shard_map/ppermute | solution.py:354
  27.3 8.7 %collective-permute-start.3 = (f32[2,2,40,128]{3,2,1,0:T(8,128)S(1)}, f32[2,2,40,128]{3,2,1,0:T(8,128)S(1)}, u32[]{:S(2)}, u32[]{:S(2)}) collective-permute-start(f32[2,2,40,128]{3,2,1,0:T(8,128)S(1)} %get-tuple-element.15.after), channel_id=1, source_target_pairs={{0,2},{1,5},{2,0},{3,7},{4,6},{5,1},{6,4},{7,3},{8,10},{9,13},{10,... | collective-permute-start | bytes 245768 | tf_op jit(solution)/shard_map/ppermute | solution.py:353
  27.9 8.1 %collective-permute-start.7 = (f32[2,2,40,128]{3,2,1,0:T(8,128)S(1)}, f32[2,2,40,128]{3,2,1,0:T(8,128)S(1)}, u32[]{:S(2)}, u32[]{:S(2)}) collective-permute-start(f32[2,2,40,128]{3,2,1,0:T(8,128)S(1)} %get-tuple-element.15.after), channel_id=1, source_target_pairs={{0,24},{2,26},{4,28},{6,30},{8,16},{10,18},{12,20},{14,22},{16,8},... | collective-permute-start | bytes 245768 | tf_op jit(solution)/shard_map/ppermute | solution.py:358
  30.9 2.4 %copy-start = (bf16[3328,768]{1,0:T(8,128)(2,1)S(1)}, bf16[3328,768]{1,0:T(8,128)(2,1)}, u32[]{:S(2)}) copy-start(bf16[3328,768]{1,0:T(8,128)(2,1)} %constant.14.clone.table_hbm) | copy-start | bytes 15335428
  33.9 11.0 %copy-start.1 = (f32[2,2,24,1664]{3,2,1,0:T(8,128)S(1)}, f32[2,2,24,1664]{3,2,1,0:T(8,128)}, u32[]{:S(2)}) copy-start(f32[2,2,24,1664]{3,2,1,0:T(8,128)} %get-tuple-element.10.refs_12_) | copy-start | bytes 1916932
  33.9 5.7 %collective-permute-start.2 = (f32[2,2,40,128]{3,2,1,0:T(8,128)S(1)}, f32[2,2,40,128]{3,2,1,0:T(8,128)S(1)}, u32[]{:S(2)}, u32[]{:S(2)}) collective-permute-start(f32[2,2,40,128]{3,2,1,0:T(8,128)S(1)} %get-tuple-element.15.after), channel_id=1, source_target_pairs={{0,8},{2,10},{4,12},{6,14},{8,0},{10,2},{12,4},{14,6},{16,24},{18,... | collective-permute-start | bytes 245768 | tf_op jit(solution)/shard_map/ppermute | solution.py:359
  34.2 5.6 %collective-permute-start.12 = (f32[2,2,40,128]{3,2,1,0:T(8,128)S(1)}, f32[2,2,40,128]{3,2,1,0:T(8,128)S(1)}, u32[]{:S(2)}, u32[]{:S(2)}) collective-permute-start(f32[2,2,40,128]{3,2,1,0:T(8,128)S(1)} %collective-permute-done.5.refs_2_), channel_id=1, source_target_pairs={{0,8},{2,10},{4,12},{6,14},{8,0},{10,2},{12,4},{14,6},{16,24},{18,... | collective-permute-start | bytes 245768 | tf_op jit(solution)/shard_map/ppermute | solution.py:359
  36.1 8.9 %collective-permute-start.13 = (f32[2,2,2,40,128]{4,3,2,1,0:T(8,128)S(1)}, f32[2,2,2,40,128]{4,3,2,1,0:T(8,128)S(1)}, u32[]{:S(2)}, u32[]{:S(2)}) collective-permute-start(f32[2,2,2,40,128]{4,3,2,1,0:T(8,128)S(1)} %pack.1.refs_2_), channel_id=1, source_target_pairs={{0,6},{2,4},{4,2},{6,0},{8,14},{10,12},{12,10},{14,8},{16,22},{18,... | collective-permute-start | bytes 491528 | tf_op jit(solution)/shard_map/ppermute | solution.py:355
  36.9 8.0 %collective-permute-start.11 = (f32[2,2,2,40,128]{4,3,2,1,0:T(8,128)S(1)}, f32[2,2,2,40,128]{4,3,2,1,0:T(8,128)S(1)}, u32[]{:S(2)}, u32[]{:S(2)}) collective-permute-start(f32[2,2,2,40,128]{4,3,2,1,0:T(8,128)S(1)} %pack.1.refs_2_), channel_id=1, source_target_pairs={{0,4},{1,3},{2,6},{3,1},{4,0},{5,7},{6,2},{7,5},{8,12},{9,11},{10,... | collective-permute-start | bytes 491528 | tf_op jit(solution)/shard_map/ppermute | solution.py:354
  38.2 6.8 %collective-permute-start.9 = (f32[2,2,2,40,128]{4,3,2,1,0:T(8,128)S(1)}, f32[2,2,2,40,128]{4,3,2,1,0:T(8,128)S(1)}, u32[]{:S(2)}, u32[]{:S(2)}) collective-permute-start(f32[2,2,2,40,128]{4,3,2,1,0:T(8,128)S(1)} %pack.1.refs_2_), channel_id=1, source_target_pairs={{0,2},{1,5},{2,0},{3,7},{4,6},{5,1},{6,4},{7,3},{8,10},{9,13},{10,... | collective-permute-start | bytes 491528 | tf_op jit(solution)/shard_map/ppermute | solution.py:353
  39.6 4.4 %collective-permute-start.10 = (f32[2,2,40,128]{3,2,1,0:T(8,128)S(1)}, f32[2,2,40,128]{3,2,1,0:T(8,128)S(1)}, u32[]{:S(2)}, u32[]{:S(2)}) collective-permute-start(f32[2,2,40,128]{3,2,1,0:T(8,128)S(1)} %collective-permute-done.4.refs_1_), channel_id=1, source_target_pairs={{0,8},{2,10},{4,12},{6,14},{8,0},{10,2},{12,4},{14,6},{16,24},{18,... | collective-permute-start | bytes 245768 | tf_op jit(solution)/shard_map/ppermute | solution.py:359
  39.8 5.2 %collective-permute-start.8 = (f32[2,2,40,128]{3,2,1,0:T(8,128)S(1)}, f32[2,2,40,128]{3,2,1,0:T(8,128)S(1)}, u32[]{:S(2)}, u32[]{:S(2)}) collective-permute-start(f32[2,2,40,128]{3,2,1,0:T(8,128)S(1)} %collective-permute-done.3.refs_0_), channel_id=1, source_target_pairs={{0,8},{2,10},{4,12},{6,14},{8,0},{10,2},{12,4},{14,6},{16,24},{18,... | collective-permute-start | bytes 245768 | tf_op jit(solution)/shard_map/ppermute | solution.py:359
  49.8 2.5 %collective-permute-start.14 = (f32[2,36,4,768]{3,2,1,0:T(4,128)S(1)}, f32[2,36,4,768]{3,2,1,0:T(4,128)S(1)}, u32[]{:S(2)}, u32[]{:S(2)}) collective-permute-start(f32[2,36,4,768]{3,2,1,0:T(4,128)S(1)} %correlate.1.own), channel_id=1, source_target_pairs={{0,1},{1,0},{2,3},{3,2},{4,5},{5,4},{6,7},{7,6},{8,9},{9,8},{10,11... | collective-permute-start | bytes 2654216 | tf_op jit(solution)/shard_map/ppermute | solution.py:314

commit v5 on v4

--- a/solution.py
+++ b/solution.py
@@ -70,9 +70,7 @@
             for i in range(comps):
                 y = x_ref[w, s, i] * weights
                 for part in range(2):
-                    for copy in range(2):
-                        row = pl.ds((copy * comps + i) * stas + s, 1)
-                        rec_ref[w, part, row, :] = y[part : part + 1]
+                    rec_ref[w, part, pl.ds(i * stas + s, 1), :] = y[part : part + 1]
                     for c in range(tiles):
                         pieces_ref[4 * s + place[w][part], pl.ds(i * tiles + c, 1), :] = y[
                             part : part + 1, c * LANES : (c + 1) * LANES
@@ -81,16 +79,24 @@
     if rest:
         for k in range(wins * stas * 2):
             pieces_ref[k, pl.ds(comps * tiles, rest), :] = jnp.zeros((rest, LANES), jnp.float32)
+    spare = rec_ref.shape[2] - comps * stas
+    if spare:
+        for w in range(wins):
+            for part in range(2):
+                rec_ref[w, part, pl.ds(comps * stas, spare), :] = jnp.zeros(
+                    (spare, bins), jnp.float32
+                )
 
 
 def whiten(spectra, flags):
     wins, stas, _, comps, bins = spectra.shape
     rows = -(-comps * (bins // LANES) // 8) * 8
+    recs = -(-comps * stas // 8) * 8
     return pl.pallas_call(
         whiten_kernel,
         out_shape=(
             jax.ShapeDtypeStruct((wins * stas * 2, rows, LANES), jnp.float32),
-            jax.ShapeDtypeStruct((wins, 2, 2 * comps * stas, bins), jnp.float32),
+            jax.ShapeDtypeStruct((wins, 2, recs, bins), jnp.float32),
         ),
         in_specs=[pl.BlockSpec(memory_space=pltpu.HBM)] * 2,
         out_specs=(
@@ -167,7 +173,10 @@
 
 def correlate_kernel(params, *refs, count):
     spots_in = [refs[n * count : (n + 1) * count] for n in range(4)]
-    receivers_in, table, out_ref, lhs = refs[4 * count : 4 * count + 2], *refs[4 * count + 2 :]
+    receivers_in, table, out_ref, lhs, rec = (
+        refs[4 * count : 4 * count + 2],
+        *refs[4 * count + 2 :],
+    )
     _, groups, steps, _, _ = spots_in[0][0].shape
     offsets = [(k, n) for k in range(count) for n in range(spots_in[0][k].shape[0])]
     depth = len(offsets)
@@ -176,6 +185,12 @@
     window, part = (place >> (1 - core)) & 1, (place >> core) & 1
     kinds = ((window, part), (part, window))
     signs = [1.0 - 2.0 * p.astype(jnp.float32) for _, p in kinds]
+    for g in range(groups):
+        for w in range(2):
+            for p in range(2):
+                rows = receivers_in[g][kinds[g][0] ^ w, kinds[g][1] ^ p, 0:12, :]
+                rec[g, w, p, 0:12, :] = rows
+                rec[g, w, p, 12:24, :] = rows
     spots = (((0, 1), (2, 3)), ((0, 2), (1, 3)))
     upper = lax.broadcasted_iota(jnp.int32, (8, LANES), 0) < 4
 
@@ -187,9 +202,7 @@
     def chunk(c, carry):
         lanes = pl.ds(pl.multiple_of(c * LANES, LANES), LANES)
         receivers = [
-            [[receivers_in[g][kinds[g][0] ^ w, kinds[g][1] ^ p, :, lanes] for p in range(2)]
-             for w in range(2)]
-            for g in range(groups)
+            [[rec[g, w, p, :, lanes] for p in range(2)] for w in range(2)] for g in range(groups)
         ]
         for block in range(steps * depth * 3 // 4):
             real_tiles, imag_tiles = [], []
@@ -224,7 +237,7 @@
             ).astype(jnp.bfloat16)
         return carry
 
-    lax.fori_loop(0, tiles, chunk, 0)
+    lax.fori_loop(0, tiles, chunk, 0, unroll=True)
     for n in range(out_ref.shape[3] // 256):
         lags = pl.ds(n * 256, 256)
         result = jnp.dot(lhs[...], table[:, lags], preferred_element_type=jnp.float32)
@@ -249,7 +262,10 @@
         out_shape=jax.ShapeDtypeStruct((steps, depth * 9, 4, lags), jnp.float32),
         in_specs=[pl.BlockSpec(memory_space=pltpu.SMEM)] + [vmem] * (4 * count + 3),
         out_specs=vmem,
-        scratch_shapes=[pltpu.VMEM((rows, 2 * bins), jnp.bfloat16)],
+        scratch_shapes=[
+            pltpu.VMEM((rows, 2 * bins), jnp.bfloat16),
+            pltpu.VMEM((2, 2, 2, 24, bins), jnp.float32),
+        ],
         compiler_params=pltpu.CompilerParams(vmem_limit_bytes=20 * MIB),
         cost_estimate=pl.CostEstimate(
             flops=4 * rows * bins * lags, bytes_accessed=8 * MIB, transcendentals=0
@@ -357,8 +373,9 @@
     first = plane(mine)
     far, farther = [lax.ppermute(mine, "sta", partner(4 * k)) for k in (2, 3)]
     second = [lax.ppermute(value, "sta", partner(4)) for value in first]
-    table = load(jnp.asarray(lag_table(bins, NLAG, wins * lax.axis_size("win"))), mine)
-    rest = plane(pack((far, farther), (*first[1:], table)))
+    packed = pack((far, farther), first[1:])
+    rest = plane(packed)
+    table = load(jnp.asarray(lag_table(bins, NLAG, wins * lax.axis_size("win"))), packed)
     sources_in = [(a[None], b[None], c) for a, b, c in zip(first, second, rest)]
     half = correlate(params, sources_in, own, other, table)
     whole = join(swap(half), put(half))

time: 53.5 us -> 52.1 us (0.974)
  waiting for transfers between devices: 15.1 us -> 14.1 us
    ppermute x4, waiting for transfers between devices: 3.29 us -> 0.31 us  [on_device(): second = [lax.ppermute(value, 'sta', partner(4)) for value in first]]
    ppermute x2, waiting for transfers between devices: 0.01 us -> 1.98 us  [on_device(): far, farther = [lax.ppermute(mine, 'sta', partner(4 * k)) for k in (2, 3)]]
  transfers between devices with their start and end apart: 16 -> 16, of which waited for: 5 -> 6; matrix products, arithmetic and copies ran while one was open for 4% -> 4% of each run, Pallas kernels for 3% -> 3%
where the time goes in v5:
time: 52.1 us; the launch traced here: 51.8 us
  starting transfers between devices  23.1 us (44%)
  waiting for transfers between devices  14.1 us (27%)
  Pallas kernels  9.96 us (19%)
  local copies, waits for them, and re-layouts  3.27 us (6%)
  other arithmetic  1.22 us (2%)
    all_to_all x1, waiting for transfers between devices, on_device(): got = lax.all_to_all(pieces, 'sta', 0, 0)  9.19 us
    all_to_all x1, starting transfers between devices, on_device(): got = lax.all_to_all(pieces, 'sta', 0, 0)  8.32 us
    pallas_call x1, Pallas kernels, correlate(): pl.pallas_call(functools.partial(correlate_kernel, count=count), out_shap...  4.54 us
    ppermute x4, starting transfers between devices, on_device(): second = [lax.ppermute(value, 'sta', partner(4)) for value in first]  4.05 us
    ppermute x2, starting transfers between devices, on_device(): far, farther = [lax.ppermute(mine, 'sta', partner(4 * k)) for k in (2, 3)]  3.43 us
    ppermute x2, starting transfers between devices, plane(): side = lax.ppermute(value, ('sta', 'win'), by_core(2, 1))  3.41 us
    ppermute x3, waiting for transfers between devices, swap(): return lax.ppermute(value, 'win', [(0, 1), (1, 0)])  2.64 us
    unnamed x4, local copies, waits for them, and re-layouts  2.45 us
  transfers between devices with their start and end apart: 16, of which 6 were waited for; matrix products, arithmetic and copies ran while one was open for 4% of the time, Pallas kernels for 3%

profile of v5, /device:TPU:0, one launch (start us, length us, event | category | flops | bytes accessed | tf_op | source)
XLA Modules:
  0.0 51.8 jit_solution(17287950042333098581)
XLA Ops:
  0.0 2.4 %whiten.1 = (f32[16,40,128]{2,1,0:T(8,128)}, f32[2,2,16,1664]{3,2,1,0:T(8,128)}) custom-call(s32[2,4]{1,0:T(2,128)} %flags_hbm.1, f32[2,4,3,2,1664]{4,3,2,1,0:T(2,128)} %bitcast.25), custom_call_target="tpu_custom_call" | custom-call | tf_op jit(solution)/shard_map/whiten/pallas_call | solution.py:95
  2.4 8.3 %all-to-all-start = ((f32[16,40,128]{2,1,0:T(8,128)}), f32[16,40,128]{2,1,0:T(8,128)S(1)}, u32[]{:S(2)}, u32[]{:S(2)}) async-start(f32[16,40,128]{2,1,0:T(8,128)} %get-tuple-element.9), calls=%async_computation | async-start | bytes 655360 | tf_op jit(solution)/shard_map/all_to_all | solution.py:357
  10.8 0.7 %reshape.20 = s32[2,2]{1,0:T(2,128)S(1)} reshape(s32[4]{0:T(128)} %param.7) | data formatting | bytes 32 | tf_op jit(solution)/shard_map/reshape | solution.py:339
  11.6 0.8 %broadcast_select_fusion = s32[2,1,4]{2,1,0:T(1,128)S(1)} fusion(pred[]{:T(512)S(6)} %eq.20, s32[2,2,4]{2,1,0:T(2,128)} %bitcast.28), kind=kLoop, calls=%fused_computation.2 | loop fusion | flops 8 | bytes 97 | tf_op jit(solution)/shard_map/jit(_where)/select_n | solution.py:342
  12.3 0.2 select_reduce_fusion
  12.5 0.1 reshape.22
  12.6 0.2 select_reduce_fusion.2
  12.8 0.1 pad_add_fusion.params
  12.9 9.2 %all-to-all-done.got_ref = f32[16,40,128]{2,1,0:T(8,128)S(1)} async-done(((f32[16,40,128]{2,1,0:T(8,128)}), f32[16,40,128]{2,1,0:T(8,128)S(1)}, u32[]{:S(2)}, u32[]{:S(2)}) %all-to-all-start) | async-done | bytes 327712 | tf_op jit(solution)/shard_map/all_to_all | solution.py:357
  22.1 0.6 %pick.1 = (f32[2,40,128]{2,1,0:T(8,128)S(1)}, f32[2,40,128]{2,1,0:T(8,128)S(1)}) custom-call(s32[12]{0:T(128)S(1)} %pad_add_fusion.params, f32[16,40,128]{2,1,0:T(8,128)S(1)} %all-to-all-done.got_ref, f32[2,2,16,1664]{3,2,1,0:T(8,128)S(1)} %collective-permute-done.before.refs_13_), custom_call_target="tpu_custom_call" | custom-call | tf_op jit(solution)/shard_map/pick/pallas_call | solution.py:127
  22.6 0.1 collective-permute-start.1
  22.7 1.2 %collective-permute-done.1 = f32[2,40,128]{2,1,0:T(8,128)S(1)} collective-permute-done((f32[2,40,128]{2,1,0:T(8,128)S(1)}, f32[2,40,128]{2,1,0:T(8,128)S(1)}, u32[]{:S(2)}, u32[]{:S(2)}) %collective-permute-start.1) | collective-permute-done | bytes 40992 | tf_op jit(solution)/shard_map/ppermute | solution.py:330
  23.9 0.4 collective-permute-start.6
  24.3 1.0 %collective-permute-start.5 = (f32[2,2,40,128]{3,2,1,0:T(8,128)S(1)}, f32[2,2,40,128]{3,2,1,0:T(8,128)S(1)}, u32[]{:S(2)}, u32[]{:S(2)}) collective-permute-start(f32[2,2,40,128]{3,2,1,0:T(8,128)S(1)} %get-tuple-element.15), channel_id=1, source_target_pairs={{0,6},{2,4},{4,2},{6,0},{8,14},{10,12},{12,10},{14,8},{16,22},{18,... | collective-permute-start | bytes 245768 | tf_op jit(solution)/shard_map/ppermute | solution.py:371
  25.3 1.9 %collective-permute-start.4 = (f32[2,2,40,128]{3,2,1,0:T(8,128)S(1)}, f32[2,2,40,128]{3,2,1,0:T(8,128)S(1)}, u32[]{:S(2)}, u32[]{:S(2)}) collective-permute-start(f32[2,2,40,128]{3,2,1,0:T(8,128)S(1)} %get-tuple-element.15), channel_id=1, source_target_pairs={{0,4},{1,3},{2,6},{3,1},{4,0},{5,7},{6,2},{7,5},{8,12},{9,11},{10,... | collective-permute-start | bytes 245768 | tf_op jit(solution)/shard_map/ppermute | solution.py:370
  27.2 0.6 %collective-permute-start.3 = (f32[2,2,40,128]{3,2,1,0:T(8,128)S(1)}, f32[2,2,40,128]{3,2,1,0:T(8,128)S(1)}, u32[]{:S(2)}, u32[]{:S(2)}) collective-permute-start(f32[2,2,40,128]{3,2,1,0:T(8,128)S(1)} %get-tuple-element.15), channel_id=1, source_target_pairs={{0,2},{1,5},{2,0},{3,7},{4,6},{5,1},{6,4},{7,3},{8,10},{9,13},{10,... | collective-permute-start | bytes 245768 | tf_op jit(solution)/shard_map/ppermute | solution.py:369
  27.8 3.0 %collective-permute-start.7 = (f32[2,2,40,128]{3,2,1,0:T(8,128)S(1)}, f32[2,2,40,128]{3,2,1,0:T(8,128)S(1)}, u32[]{:S(2)}, u32[]{:S(2)}) collective-permute-start(f32[2,2,40,128]{3,2,1,0:T(8,128)S(1)} %get-tuple-element.15), channel_id=1, source_target_pairs={{0,24},{2,26},{4,28},{6,30},{8,16},{10,18},{12,20},{14,22},{16,8},... | collective-permute-start | bytes 245768 | tf_op jit(solution)/shard_map/ppermute | solution.py:374
  30.8 1.5 %collective-permute-done.6.refs_3_ = f32[2,2,40,128]{3,2,1,0:T(8,128)S(1)} collective-permute-done((f32[2,2,40,128]{3,2,1,0:T(8,128)S(1)}, f32[2,2,40,128]{3,2,1,0:T(8,128)S(1)}, u32[]{:S(2)}, u32[]{:S(2)}) %collective-permute-start.6) | collective-permute-done | bytes 81952 | tf_op jit(solution)/shard_map/ppermute | solution.py:374
  32.3 2.0 %collective-permute-start.12 = (f32[2,2,40,128]{3,2,1,0:T(8,128)S(1)}, f32[2,2,40,128]{3,2,1,0:T(8,128)S(1)}, u32[]{:S(2)}, u32[]{:S(2)}) collective-permute-start(f32[2,2,40,128]{3,2,1,0:T(8,128)S(1)} %collective-permute-done.5.refs_2_), channel_id=1, source_target_pairs={{0,8},{2,10},{4,12},{6,14},{8,0},{10,2},{12,4},{14,6},{16,24},{18,... | collective-permute-start | bytes 245768 | tf_op jit(solution)/shard_map/ppermute | solution.py:375
  34.4 0.5 collective-permute-done.7.refs_4_
  34.9 1.1 %collective-permute-start.13 = (f32[2,2,2,40,128]{4,3,2,1,0:T(8,128)S(1)}, f32[2,2,2,40,128]{4,3,2,1,0:T(8,128)S(1)}, u32[]{:S(2)}, u32[]{:S(2)}) collective-permute-start(f32[2,2,2,40,128]{4,3,2,1,0:T(8,128)S(1)} %pack.1.after.refs_2_), channel_id=1, source_target_pairs={{0,6},{2,4},{4,2},{6,0},{8,14},{10,12},{12,10},{14,8},{16,22},{18,... | collective-permute-start | bytes 491528 | tf_op jit(solution)/shard_map/ppermute | solution.py:371
  35.9 1.5 %collective-permute-start.11 = (f32[2,2,2,40,128]{4,3,2,1,0:T(8,128)S(1)}, f32[2,2,2,40,128]{4,3,2,1,0:T(8,128)S(1)}, u32[]{:S(2)}, u32[]{:S(2)}) collective-permute-start(f32[2,2,2,40,128]{4,3,2,1,0:T(8,128)S(1)} %pack.1.after.refs_2_), channel_id=1, source_target_pairs={{0,4},{1,3},{2,6},{3,1},{4,0},{5,7},{6,2},{7,5},{8,12},{9,11},{10,... | collective-permute-start | bytes 491528 | tf_op jit(solution)/shard_map/ppermute | solution.py:370
  37.5 0.9 %collective-permute-start.9 = (f32[2,2,2,40,128]{4,3,2,1,0:T(8,128)S(1)}, f32[2,2,2,40,128]{4,3,2,1,0:T(8,128)S(1)}, u32[]{:S(2)}, u32[]{:S(2)}) collective-permute-start(f32[2,2,2,40,128]{4,3,2,1,0:T(8,128)S(1)} %pack.1.after.refs_2_), channel_id=1, source_target_pairs={{0,2},{1,5},{2,0},{3,7},{4,6},{5,1},{6,4},{7,3},{8,10},{9,13},{10,... | collective-permute-start | bytes 491528 | tf_op jit(solution)/shard_map/ppermute | solution.py:369
  38.4 0.2 collective-permute-start.10
  38.6 1.9 %collective-permute-start.8 = (f32[2,2,40,128]{3,2,1,0:T(8,128)S(1)}, f32[2,2,40,128]{3,2,1,0:T(8,128)S(1)}, u32[]{:S(2)}, u32[]{:S(2)}) collective-permute-start(f32[2,2,40,128]{3,2,1,0:T(8,128)S(1)} %collective-permute-done.3.refs_0_), channel_id=1, source_target_pairs={{0,8},{2,10},{4,12},{6,14},{8,0},{10,2},{12,4},{14,6},{16,24},{18,... | collective-permute-start | bytes 245768 | tf_op jit(solution)/shard_map/ppermute | solution.py:375
  40.5 2.4 %copy-done = bf16[3328,768]{1,0:T(8,128)(2,1)S(1)} copy-done((bf16[3328,768]{1,0:T(8,128)(2,1)S(1)}, bf16[3328,768]{1,0:T(8,128)(2,1)}, u32[]{:S(2)}) %copy-start) | copy-done | bytes 5111832
  42.9 0.5 load.1.refs_14_
  43.4 0.3 collective-permute-done.8
  43.8 4.5 %correlate.1.own = f32[2,36,4,768]{3,2,1,0:T(4,128)S(1)} custom-call(s32[12]{0:T(128)S(1)} %pad_add_fusion.params, f32[1,2,2,40,128]{4,3,2,1,0:T(8,128)S(1)} %get-tuple-element.16.refs_0_, f32[1,2,2,40,128]{4,3,2,1,0:T(8,128)S(1)} %bitcast.20, f32[2,2,2,40,128]{4,3,2,1,0:T(8,128)S(1)} %pack.1.after.refs_2_, f32[1,2,2,40,128]{4,3,2,1,0:T(8,128)S(1)} %bitcast.19, ...), custom_call_target="tpu_custom_call" | custom-call | flops 1472200704 | bytes 8388608 | tf_op jit(solution)/shard_map/correlate/pallas_call | solution.py:260
  48.4 1.0 %put.1.whole = f32[4,36,4,768]{3,2,1,0:T(4,128)} custom-call(f32[2,36,4,768]{3,2,1,0:T(4,128)S(1)} %correlate.1.own), custom_call_target="tpu_custom_call" | custom-call | tf_op jit(solution)/shard_map/put/pallas_call | solution.py:300
  49.4 1.4 %collective-permute-done.14.other = f32[2,36,4,768]{3,2,1,0:T(4,128)S(1)} collective-permute-done((f32[2,36,4,768]{3,2,1,0:T(4,128)S(1)}, f32[2,36,4,768]{3,2,1,0:T(4,128)S(1)}, u32[]{:S(2)}, u32[]{:S(2)}) %collective-permute-start.14) | collective-permute-done | bytes 884768 | tf_op jit(solution)/shard_map/ppermute | solution.py:330
  50.8 1.0 %join.1 = f32[4,36,4,768]{3,2,1,0:T(4,128)} custom-call(f32[2,36,4,768]{3,2,1,0:T(4,128)S(1)} %collective-permute-done.14.other, f32[4,36,4,768]{3,2,1,0:T(4,128)} %put.1.whole), custom_call_target="tpu_custom_call", output_to_operand_aliasing={{}: (1, {})} | custom-call | tf_op jit(solution)/shard_map/join/pallas_call | solution.py:317
  (19 shorter events, 0.2 us)
Async XLA Ops:
  2.4 19.6 %all-to-all-start = ((f32[16,40,128]{2,1,0:T(8,128)}), f32[16,40,128]{2,1,0:T(8,128)S(1)}, u32[]{:S(2)}, u32[]{:S(2)}) async-start(f32[16,40,128]{2,1,0:T(8,128)} %get-tuple-element.9), calls=%async_computation | async-start | bytes 655360 | tf_op jit(solution)/shard_map/all_to_all | solution.py:357
  10.7 2.1 %collective-permute-start = (f32[2,2,16,1664]{3,2,1,0:T(8,128)}, f32[2,2,16,1664]{3,2,1,0:T(8,128)S(1)}, u32[]{:S(2)}, u32[]{:S(2)}) collective-permute-start(f32[2,2,16,1664]{3,2,1,0:T(8,128)} %get-tuple-element.10.refs_12_), channel_id=1, source_target_pairs={{0,1},{1,0},{2,3},{3,2},{4,5},{5,4},{6,7},{7,6},{8,9},{9,8},{10,11... | collective-permute-start | bytes 1277960 | tf_op jit(solution)/shard_map/ppermute | solution.py:330
  22.6 1.3 %collective-permute-start.1 = (f32[2,40,128]{2,1,0:T(8,128)S(1)}, f32[2,40,128]{2,1,0:T(8,128)S(1)}, u32[]{:S(2)}, u32[]{:S(2)}) collective-permute-start(f32[2,40,128]{2,1,0:T(8,128)S(1)} %get-tuple-element.12), channel_id=1, source_target_pairs={{0,1},{1,0},{2,3},{3,2},{4,5},{5,4},{6,7},{7,6},{8,9},{9,8},{10,11... | collective-permute-start | bytes 122888 | tf_op jit(solution)/shard_map/ppermute | solution.py:330
  23.9 8.4 %collective-permute-start.6 = (f32[2,2,40,128]{3,2,1,0:T(8,128)S(1)}, f32[2,2,40,128]{3,2,1,0:T(8,128)S(1)}, u32[]{:S(2)}, u32[]{:S(2)}) collective-permute-start(f32[2,2,40,128]{3,2,1,0:T(8,128)S(1)} %get-tuple-element.15), channel_id=1, source_target_pairs={{0,16},{2,18},{4,20},{6,22},{8,24},{10,26},{12,28},{14,30},{16,0},... | collective-permute-start | bytes 245768 | tf_op jit(solution)/shard_map/ppermute | solution.py:374
  24.3 8.0 %collective-permute-start.5 = (f32[2,2,40,128]{3,2,1,0:T(8,128)S(1)}, f32[2,2,40,128]{3,2,1,0:T(8,128)S(1)}, u32[]{:S(2)}, u32[]{:S(2)}) collective-permute-start(f32[2,2,40,128]{3,2,1,0:T(8,128)S(1)} %get-tuple-element.15), channel_id=1, source_target_pairs={{0,6},{2,4},{4,2},{6,0},{8,14},{10,12},{12,10},{14,8},{16,22},{18,... | collective-permute-start | bytes 245768 | tf_op jit(solution)/shard_map/ppermute | solution.py:371
  25.3 9.0 %collective-permute-start.4 = (f32[2,2,40,128]{3,2,1,0:T(8,128)S(1)}, f32[2,2,40,128]{3,2,1,0:T(8,128)S(1)}, u32[]{:S(2)}, u32[]{:S(2)}) collective-permute-start(f32[2,2,40,128]{3,2,1,0:T(8,128)S(1)} %get-tuple-element.15), channel_id=1, source_target_pairs={{0,4},{1,3},{2,6},{3,1},{4,0},{5,7},{6,2},{7,5},{8,12},{9,11},{10,... | collective-permute-start | bytes 245768 | tf_op jit(solution)/shard_map/ppermute | solution.py:370
  27.2 7.1 %collective-permute-start.3 = (f32[2,2,40,128]{3,2,1,0:T(8,128)S(1)}, f32[2,2,40,128]{3,2,1,0:T(8,128)S(1)}, u32[]{:S(2)}, u32[]{:S(2)}) collective-permute-start(f32[2,2,40,128]{3,2,1,0:T(8,128)S(1)} %get-tuple-element.15), channel_id=1, source_target_pairs={{0,2},{1,5},{2,0},{3,7},{4,6},{5,1},{6,4},{7,3},{8,10},{9,13},{10,... | collective-permute-start | bytes 245768 | tf_op jit(solution)/shard_map/ppermute | solution.py:369
  27.8 7.0 %collective-permute-start.7 = (f32[2,2,40,128]{3,2,1,0:T(8,128)S(1)}, f32[2,2,40,128]{3,2,1,0:T(8,128)S(1)}, u32[]{:S(2)}, u32[]{:S(2)}) collective-permute-start(f32[2,2,40,128]{3,2,1,0:T(8,128)S(1)} %get-tuple-element.15), channel_id=1, source_target_pairs={{0,24},{2,26},{4,28},{6,30},{8,16},{10,18},{12,20},{14,22},{16,8},... | collective-permute-start | bytes 245768 | tf_op jit(solution)/shard_map/ppermute | solution.py:374
  32.3 6.1 %collective-permute-start.2 = (f32[2,2,40,128]{3,2,1,0:T(8,128)S(1)}, f32[2,2,40,128]{3,2,1,0:T(8,128)S(1)}, u32[]{:S(2)}, u32[]{:S(2)}) collective-permute-start(f32[2,2,40,128]{3,2,1,0:T(8,128)S(1)} %get-tuple-element.15), channel_id=1, source_target_pairs={{0,8},{2,10},{4,12},{6,14},{8,0},{10,2},{12,4},{14,6},{16,24},{18,... | collective-permute-start | bytes 245768 | tf_op jit(solution)/shard_map/ppermute | solution.py:375
  32.3 6.3 %collective-permute-start.12 = (f32[2,2,40,128]{3,2,1,0:T(8,128)S(1)}, f32[2,2,40,128]{3,2,1,0:T(8,128)S(1)}, u32[]{:S(2)}, u32[]{:S(2)}) collective-permute-start(f32[2,2,40,128]{3,2,1,0:T(8,128)S(1)} %collective-permute-done.5.refs_2_), channel_id=1, source_target_pairs={{0,8},{2,10},{4,12},{6,14},{8,0},{10,2},{12,4},{14,6},{16,24},{18,... | collective-permute-start | bytes 245768 | tf_op jit(solution)/shard_map/ppermute | solution.py:375
  34.8 8.9 %copy-start.1 = (f32[2,2,16,1664]{3,2,1,0:T(8,128)S(1)}, f32[2,2,16,1664]{3,2,1,0:T(8,128)}, u32[]{:S(2)}) copy-start(f32[2,2,16,1664]{3,2,1,0:T(8,128)} %get-tuple-element.10.refs_12_) | copy-start | bytes 1277956
  34.9 8.9 %collective-permute-start.13 = (f32[2,2,2,40,128]{4,3,2,1,0:T(8,128)S(1)}, f32[2,2,2,40,128]{4,3,2,1,0:T(8,128)S(1)}, u32[]{:S(2)}, u32[]{:S(2)}) collective-permute-start(f32[2,2,2,40,128]{4,3,2,1,0:T(8,128)S(1)} %pack.1.after.refs_2_), channel_id=1, source_target_pairs={{0,6},{2,4},{4,2},{6,0},{8,14},{10,12},{12,10},{14,8},{16,22},{18,... | collective-permute-start | bytes 491528 | tf_op jit(solution)/shard_map/ppermute | solution.py:371
  35.9 7.8 %collective-permute-start.11 = (f32[2,2,2,40,128]{4,3,2,1,0:T(8,128)S(1)}, f32[2,2,2,40,128]{4,3,2,1,0:T(8,128)S(1)}, u32[]{:S(2)}, u32[]{:S(2)}) collective-permute-start(f32[2,2,2,40,128]{4,3,2,1,0:T(8,128)S(1)} %pack.1.after.refs_2_), channel_id=1, source_target_pairs={{0,4},{1,3},{2,6},{3,1},{4,0},{5,7},{6,2},{7,5},{8,12},{9,11},{10,... | collective-permute-start | bytes 491528 | tf_op jit(solution)/shard_map/ppermute | solution.py:370
  37.5 6.3 %collective-permute-start.9 = (f32[2,2,2,40,128]{4,3,2,1,0:T(8,128)S(1)}, f32[2,2,2,40,128]{4,3,2,1,0:T(8,128)S(1)}, u32[]{:S(2)}, u32[]{:S(2)}) collective-permute-start(f32[2,2,2,40,128]{4,3,2,1,0:T(8,128)S(1)} %pack.1.after.refs_2_), channel_id=1, source_target_pairs={{0,2},{1,5},{2,0},{3,7},{4,6},{5,1},{6,4},{7,3},{8,10},{9,13},{10,... | collective-permute-start | bytes 491528 | tf_op jit(solution)/shard_map/ppermute | solution.py:369
  38.4 5.0 %collective-permute-start.10 = (f32[2,2,40,128]{3,2,1,0:T(8,128)S(1)}, f32[2,2,40,128]{3,2,1,0:T(8,128)S(1)}, u32[]{:S(2)}, u32[]{:S(2)}) collective-permute-start(f32[2,2,40,128]{3,2,1,0:T(8,128)S(1)} %collective-permute-done.4.refs_1_), channel_id=1, source_target_pairs={{0,8},{2,10},{4,12},{6,14},{8,0},{10,2},{12,4},{14,6},{16,24},{18,... | collective-permute-start | bytes 245768 | tf_op jit(solution)/shard_map/ppermute | solution.py:375
  38.6 5.1 %collective-permute-start.8 = (f32[2,2,40,128]{3,2,1,0:T(8,128)S(1)}, f32[2,2,40,128]{3,2,1,0:T(8,128)S(1)}, u32[]{:S(2)}, u32[]{:S(2)}) collective-permute-start(f32[2,2,40,128]{3,2,1,0:T(8,128)S(1)} %collective-permute-done.3.refs_0_), channel_id=1, source_target_pairs={{0,8},{2,10},{4,12},{6,14},{8,0},{10,2},{12,4},{14,6},{16,24},{18,... | collective-permute-start | bytes 245768 | tf_op jit(solution)/shard_map/ppermute | solution.py:375
  40.5 2.4 %copy-start = (bf16[3328,768]{1,0:T(8,128)(2,1)S(1)}, bf16[3328,768]{1,0:T(8,128)(2,1)}, u32[]{:S(2)}) copy-start(bf16[3328,768]{1,0:T(8,128)(2,1)} %constant.14.clone.table_hbm) | copy-start | bytes 15335428
  48.3 2.5 %collective-permute-start.14 = (f32[2,36,4,768]{3,2,1,0:T(4,128)S(1)}, f32[2,36,4,768]{3,2,1,0:T(4,128)S(1)}, u32[]{:S(2)}, u32[]{:S(2)}) collective-permute-start(f32[2,36,4,768]{3,2,1,0:T(4,128)S(1)} %correlate.1.own), channel_id=1, source_target_pairs={{0,1},{1,0},{2,3},{3,2},{4,5},{5,4},{6,7},{7,6},{8,9},{9,8},{10,11... | collective-permute-start | bytes 2654216 | tf_op jit(solution)/shard_map/ppermute | solution.py:330

commit v6 on v5

--- a/solution.py
+++ b/solution.py
@@ -147,6 +147,7 @@
         in_specs=[vmem] * (len(values) + len(before)),
         out_specs=vmem,
         compiler_params=pltpu.CompilerParams(vmem_limit_bytes=8 * MIB),
+        cost_estimate=pl.CostEstimate(flops=0, bytes_accessed=20 * MIB, transcendentals=0),
         name="pack",
     )(*before, *values)
 
@@ -308,14 +309,14 @@
     )(own)
 
 
-def join_kernel(other, whole, out, sems):
-    write_steps(other, out, 1 - lax.axis_index("win"), sems)
-
-
-def join(other, whole):
+def join_kernel(other, whole, out, sems, first):
+    write_steps(other, out, 2 * first + 1 - lax.axis_index("win"), sems)
+
+
+def join(other, whole, first):
     hbm = pl.BlockSpec(memory_space=pltpu.HBM)
     return pl.pallas_call(
-        join_kernel,
+        functools.partial(join_kernel, first=first),
         out_shape=jax.ShapeDtypeStruct(whole.shape, whole.dtype),
         in_specs=[pl.BlockSpec(memory_space=pltpu.VMEM), hbm],
         out_specs=hbm,
@@ -378,7 +379,9 @@
     table = load(jnp.asarray(lag_table(bins, NLAG, wins * lax.axis_size("win"))), packed)
     sources_in = [(a[None], b[None], c) for a, b, c in zip(first, second, rest)]
     half = correlate(params, sources_in, own, other, table)
-    whole = join(swap(half), put(half))
+    whole = put(half)
+    for step in range(half.shape[0]):
+        whole = join(swap(half[step : step + 1]), whole, step)
     return whole.reshape(steps, sources, comps, comps, stas, NLAG).transpose(0, 1, 2, 4, 3, 5)
 
 

time: 52.1 us -> 52.1 us (level)
  waiting for transfers between devices: 14.1 us -> 13 us
  Pallas kernels: 9.96 us -> 10.6 us
    ppermute x3 -> x4, waiting for transfers between devices: 2.64 us -> 1.52 us  [swap(): return lax.ppermute(value, 'win', [(0, 1), (1, 0)])]
    pallas_call x1 -> x2, Pallas kernels: 0.97 us -> 1.59 us  [join(): pl.pallas_call(functools.partial(join_kernel, first=first), out_shape=jax...]
  transfers between devices with their start and end apart: 16 -> 17, of which waited for: 6 -> 6; matrix products, arithmetic and copies ran while one was open for 4% -> 4% of each run, Pallas kernels for 3% -> 4%
where the time goes in v6:
time: 52.1 us; the launch traced here: 51.8 us
  starting transfers between devices  23.6 us (45%)
  waiting for transfers between devices  13 us (25%)
  Pallas kernels  10.6 us (20%)
  local copies, waits for them, and re-layouts  3.33 us (6%)
  other arithmetic  1.22 us (2%)
    all_to_all x1, waiting for transfers between devices, on_device(): got = lax.all_to_all(pieces, 'sta', 0, 0)  9.19 us
    all_to_all x1, starting transfers between devices, on_device(): got = lax.all_to_all(pieces, 'sta', 0, 0)  8.32 us
    pallas_call x1, Pallas kernels, correlate(): pl.pallas_call(functools.partial(correlate_kernel, count=count), out_shap...  4.54 us
    ppermute x4, starting transfers between devices, on_device(): second = [lax.ppermute(value, 'sta', partner(4)) for value in first]  4.05 us
    ppermute x2, starting transfers between devices, on_device(): far, farther = [lax.ppermute(mine, 'sta', partner(4 * k)) for k in (2, 3)]  3.43 us
    ppermute x2, starting transfers between devices, plane(): side = lax.ppermute(value, ('sta', 'win'), by_core(2, 1))  3.41 us
    unnamed x4, local copies, waits for them, and re-layouts  2.45 us
    pallas_call x1, Pallas kernels, whiten(): pl.pallas_call(whiten_kernel, out_shape=(jax.ShapeDtypeStruct((wins * sta...  2.4 us
  transfers between devices with their start and end apart: 17, of which 6 were waited for; matrix products, arithmetic and copies ran while one was open for 4% of the time, Pallas kernels for 4%

profile of v6, /device:TPU:0, one launch (start us, length us, event | category | flops | bytes accessed | tf_op | source)
XLA Modules:
  0.0 51.8 jit_solution(14614314770325684163)
XLA Ops:
  0.0 2.4 %whiten.1 = (f32[16,40,128]{2,1,0:T(8,128)}, f32[2,2,16,1664]{3,2,1,0:T(8,128)}) custom-call(s32[2,4]{1,0:T(2,128)} %flags_hbm.1, f32[2,4,3,2,1664]{4,3,2,1,0:T(2,128)} %bitcast.25), custom_call_target="tpu_custom_call" | custom-call | tf_op jit(solution)/shard_map/whiten/pallas_call | solution.py:95
  2.4 8.3 %all-to-all-start = ((f32[16,40,128]{2,1,0:T(8,128)}), f32[16,40,128]{2,1,0:T(8,128)S(1)}, u32[]{:S(2)}, u32[]{:S(2)}) async-start(f32[16,40,128]{2,1,0:T(8,128)} %get-tuple-element.9), calls=%async_computation | async-start | bytes 655360 | tf_op jit(solution)/shard_map/all_to_all | solution.py:358
  10.8 0.7 %reshape.20 = s32[2,2]{1,0:T(2,128)S(1)} reshape(s32[4]{0:T(128)} %param.7) | data formatting | bytes 32 | tf_op jit(solution)/shard_map/reshape | solution.py:340
  11.6 0.8 %broadcast_select_fusion = s32[2,1,4]{2,1,0:T(1,128)S(1)} fusion(pred[]{:T(512)S(6)} %eq.20, s32[2,2,4]{2,1,0:T(2,128)} %bitcast.28), kind=kLoop, calls=%fused_computation.2 | loop fusion | flops 8 | bytes 97 | tf_op jit(solution)/shard_map/jit(_where)/select_n | solution.py:343
  12.3 0.2 select_reduce_fusion
  12.5 0.1 reshape.22
  12.6 0.2 select_reduce_fusion.2
  12.9 9.2 %all-to-all-done.got_ref = f32[16,40,128]{2,1,0:T(8,128)S(1)} async-done(((f32[16,40,128]{2,1,0:T(8,128)}), f32[16,40,128]{2,1,0:T(8,128)S(1)}, u32[]{:S(2)}, u32[]{:S(2)}) %all-to-all-start) | async-done | bytes 327712 | tf_op jit(solution)/shard_map/all_to_all | solution.py:358
  22.1 0.6 %pick.1 = (f32[2,40,128]{2,1,0:T(8,128)S(1)}, f32[2,40,128]{2,1,0:T(8,128)S(1)}) custom-call(s32[12]{0:T(128)S(1)} %pad_add_fusion.params, f32[16,40,128]{2,1,0:T(8,128)S(1)} %all-to-all-done.got_ref, f32[2,2,16,1664]{3,2,1,0:T(8,128)S(1)} %collective-permute-done.before.refs_13_), custom_call_target="tpu_custom_call" | custom-call | tf_op jit(solution)/shard_map/pick/pallas_call | solution.py:127
  22.7 1.2 %collective-permute-done.1 = f32[2,40,128]{2,1,0:T(8,128)S(1)} collective-permute-done((f32[2,40,128]{2,1,0:T(8,128)S(1)}, f32[2,40,128]{2,1,0:T(8,128)S(1)}, u32[]{:S(2)}, u32[]{:S(2)}) %collective-permute-start.1) | collective-permute-done | bytes 40992 | tf_op jit(solution)/shard_map/ppermute | solution.py:331
  23.9 0.4 collective-permute-start.6
  24.3 1.0 %collective-permute-start.5 = (f32[2,2,40,128]{3,2,1,0:T(8,128)S(1)}, f32[2,2,40,128]{3,2,1,0:T(8,128)S(1)}, u32[]{:S(2)}, u32[]{:S(2)}) collective-permute-start(f32[2,2,40,128]{3,2,1,0:T(8,128)S(1)} %get-tuple-element.17), channel_id=1, source_target_pairs={{0,6},{2,4},{4,2},{6,0},{8,14},{10,12},{12,10},{14,8},{16,22},{18,... | collective-permute-start | bytes 245768 | tf_op jit(solution)/shard_map/ppermute | solution.py:372
  25.3 1.9 %collective-permute-start.4 = (f32[2,2,40,128]{3,2,1,0:T(8,128)S(1)}, f32[2,2,40,128]{3,2,1,0:T(8,128)S(1)}, u32[]{:S(2)}, u32[]{:S(2)}) collective-permute-start(f32[2,2,40,128]{3,2,1,0:T(8,128)S(1)} %get-tuple-element.17), channel_id=1, source_target_pairs={{0,4},{1,3},{2,6},{3,1},{4,0},{5,7},{6,2},{7,5},{8,12},{9,11},{10,... | collective-permute-start | bytes 245768 | tf_op jit(solution)/shard_map/ppermute | solution.py:371
  27.2 0.6 %collective-permute-start.3 = (f32[2,2,40,128]{3,2,1,0:T(8,128)S(1)}, f32[2,2,40,128]{3,2,1,0:T(8,128)S(1)}, u32[]{:S(2)}, u32[]{:S(2)}) collective-permute-start(f32[2,2,40,128]{3,2,1,0:T(8,128)S(1)} %get-tuple-element.17), channel_id=1, source_target_pairs={{0,2},{1,5},{2,0},{3,7},{4,6},{5,1},{6,4},{7,3},{8,10},{9,13},{10,... | collective-permute-start | bytes 245768 | tf_op jit(solution)/shard_map/ppermute | solution.py:370
  27.8 3.0 %collective-permute-start.7 = (f32[2,2,40,128]{3,2,1,0:T(8,128)S(1)}, f32[2,2,40,128]{3,2,1,0:T(8,128)S(1)}, u32[]{:S(2)}, u32[]{:S(2)}) collective-permute-start(f32[2,2,40,128]{3,2,1,0:T(8,128)S(1)} %get-tuple-element.17), channel_id=1, source_target_pairs={{0,24},{2,26},{4,28},{6,30},{8,16},{10,18},{12,20},{14,22},{16,8},... | collective-permute-start | bytes 245768 | tf_op jit(solution)/shard_map/ppermute | solution.py:375
  30.8 1.5 %collective-permute-done.6.refs_3_ = f32[2,2,40,128]{3,2,1,0:T(8,128)S(1)} collective-permute-done((f32[2,2,40,128]{3,2,1,0:T(8,128)S(1)}, f32[2,2,40,128]{3,2,1,0:T(8,128)S(1)}, u32[]{:S(2)}, u32[]{:S(2)}) %collective-permute-start.6) | collective-permute-done | bytes 81952 | tf_op jit(solution)/shard_map/ppermute | solution.py:375
  32.3 2.0 %collective-permute-start.12 = (f32[2,2,40,128]{3,2,1,0:T(8,128)S(1)}, f32[2,2,40,128]{3,2,1,0:T(8,128)S(1)}, u32[]{:S(2)}, u32[]{:S(2)}) collective-permute-start(f32[2,2,40,128]{3,2,1,0:T(8,128)S(1)} %collective-permute-done.5.refs_2_), channel_id=1, source_target_pairs={{0,8},{2,10},{4,12},{6,14},{8,0},{10,2},{12,4},{14,6},{16,24},{18,... | collective-permute-start | bytes 245768 | tf_op jit(solution)/shard_map/ppermute | solution.py:376
  34.4 0.5 collective-permute-done.7.refs_4_
  34.9 1.1 %collective-permute-start.13 = (f32[2,2,2,40,128]{4,3,2,1,0:T(8,128)S(1)}, f32[2,2,2,40,128]{4,3,2,1,0:T(8,128)S(1)}, u32[]{:S(2)}, u32[]{:S(2)}) collective-permute-start(f32[2,2,2,40,128]{4,3,2,1,0:T(8,128)S(1)} %pack.1.after.refs_2_), channel_id=1, source_target_pairs={{0,6},{2,4},{4,2},{6,0},{8,14},{10,12},{12,10},{14,8},{16,22},{18,... | collective-permute-start | bytes 491528 | tf_op jit(solution)/shard_map/ppermute | solution.py:372
  35.9 1.5 %collective-permute-start.11 = (f32[2,2,2,40,128]{4,3,2,1,0:T(8,128)S(1)}, f32[2,2,2,40,128]{4,3,2,1,0:T(8,128)S(1)}, u32[]{:S(2)}, u32[]{:S(2)}) collective-permute-start(f32[2,2,2,40,128]{4,3,2,1,0:T(8,128)S(1)} %pack.1.after.refs_2_), channel_id=1, source_target_pairs={{0,4},{1,3},{2,6},{3,1},{4,0},{5,7},{6,2},{7,5},{8,12},{9,11},{10,... | collective-permute-start | bytes 491528 | tf_op jit(solution)/shard_map/ppermute | solution.py:371
  37.5 0.9 %collective-permute-start.9 = (f32[2,2,2,40,128]{4,3,2,1,0:T(8,128)S(1)}, f32[2,2,2,40,128]{4,3,2,1,0:T(8,128)S(1)}, u32[]{:S(2)}, u32[]{:S(2)}) collective-permute-start(f32[2,2,2,40,128]{4,3,2,1,0:T(8,128)S(1)} %pack.1.after.refs_2_), channel_id=1, source_target_pairs={{0,2},{1,5},{2,0},{3,7},{4,6},{5,1},{6,4},{7,3},{8,10},{9,13},{10,... | collective-permute-start | bytes 491528 | tf_op jit(solution)/shard_map/ppermute | solution.py:370
  38.4 0.2 collective-permute-start.10
  38.6 1.9 %collective-permute-start.8 = (f32[2,2,40,128]{3,2,1,0:T(8,128)S(1)}, f32[2,2,40,128]{3,2,1,0:T(8,128)S(1)}, u32[]{:S(2)}, u32[]{:S(2)}) collective-permute-start(f32[2,2,40,128]{3,2,1,0:T(8,128)S(1)} %collective-permute-done.3.refs_0_), channel_id=1, source_target_pairs={{0,8},{2,10},{4,12},{6,14},{8,0},{10,2},{12,4},{14,6},{16,24},{18,... | collective-permute-start | bytes 245768 | tf_op jit(solution)/shard_map/ppermute | solution.py:376
  40.5 2.4 %copy-done = bf16[3328,768]{1,0:T(8,128)(2,1)S(1)} copy-done((bf16[3328,768]{1,0:T(8,128)(2,1)S(1)}, bf16[3328,768]{1,0:T(8,128)(2,1)}, u32[]{:S(2)}) %copy-start) | copy-done | bytes 5111832
  42.9 0.5 load.1.refs_14_
  43.4 0.3 collective-permute-done.8
  43.8 4.5 %correlate.1.own = f32[2,36,4,768]{3,2,1,0:T(4,128)S(1)} custom-call(s32[12]{0:T(128)S(1)} %pad_add_fusion.params, f32[1,2,2,40,128]{4,3,2,1,0:T(8,128)S(1)} %get-tuple-element.18.refs_0_, f32[1,2,2,40,128]{4,3,2,1,0:T(8,128)S(1)} %bitcast.20, f32[2,2,2,40,128]{4,3,2,1,0:T(8,128)S(1)} %pack.1.after.refs_2_, f32[1,2,2,40,128]{4,3,2,1,0:T(8,128)S(1)} %bitcast.19, ...), custom_call_target="tpu_custom_call" | custom-call | flops 1472200704 | bytes 8388608 | tf_op jit(solution)/shard_map/correlate/pallas_call | solution.py:261
  48.5 0.5 collective-permute-start.14
  49.0 1.0 %put.1.whole = f32[4,36,4,768]{3,2,1,0:T(4,128)} custom-call(f32[2,36,4,768]{3,2,1,0:T(4,128)S(1)} %correlate.1.own), custom_call_target="tpu_custom_call" | custom-call | tf_op jit(solution)/shard_map/put/pallas_call | solution.py:301
  49.9 0.3 collective-permute-done.15.other
  50.2 0.8 %join.2.whole = f32[4,36,4,768]{3,2,1,0:T(4,128)} custom-call(f32[1,36,4,768]{3,2,1,0:T(4,128)S(1)} %collective-permute-done.15.other, f32[4,36,4,768]{3,2,1,0:T(4,128)} %put.1.whole), custom_call_target="tpu_custom_call", output_to_operand_aliasing={{}: (1, {})} | custom-call | tf_op jit(solution)/shard_map/join/pallas_call | solution.py:318
  51.0 0.8 %join.3 = f32[4,36,4,768]{3,2,1,0:T(4,128)} custom-call(f32[1,36,4,768]{3,2,1,0:T(4,128)S(1)} %collective-permute-done.14.other, f32[4,36,4,768]{3,2,1,0:T(4,128)} %join.2.whole), custom_call_target="tpu_custom_call", output_to_operand_aliasing={{}: (1, {})} | custom-call | tf_op jit(solution)/shard_map/join/pallas_call | solution.py:318
  (23 shorter events, 0.4 us)
Async XLA Ops:
  2.4 19.6 %all-to-all-start = ((f32[16,40,128]{2,1,0:T(8,128)}), f32[16,40,128]{2,1,0:T(8,128)S(1)}, u32[]{:S(2)}, u32[]{:S(2)}) async-start(f32[16,40,128]{2,1,0:T(8,128)} %get-tuple-element.9), calls=%async_computation | async-start | bytes 655360 | tf_op jit(solution)/shard_map/all_to_all | solution.py:358
  10.7 2.1 %collective-permute-start = (f32[2,2,16,1664]{3,2,1,0:T(8,128)}, f32[2,2,16,1664]{3,2,1,0:T(8,128)S(1)}, u32[]{:S(2)}, u32[]{:S(2)}) collective-permute-start(f32[2,2,16,1664]{3,2,1,0:T(8,128)} %get-tuple-element.10.refs_12_), channel_id=1, source_target_pairs={{0,1},{1,0},{2,3},{3,2},{4,5},{5,4},{6,7},{7,6},{8,9},{9,8},{10,11... | collective-permute-start | bytes 1277960 | tf_op jit(solution)/shard_map/ppermute | solution.py:331
  22.6 1.3 %collective-permute-start.1 = (f32[2,40,128]{2,1,0:T(8,128)S(1)}, f32[2,40,128]{2,1,0:T(8,128)S(1)}, u32[]{:S(2)}, u32[]{:S(2)}) collective-permute-start(f32[2,40,128]{2,1,0:T(8,128)S(1)} %get-tuple-element.12), channel_id=1, source_target_pairs={{0,1},{1,0},{2,3},{3,2},{4,5},{5,4},{6,7},{7,6},{8,9},{9,8},{10,11... | collective-permute-start | bytes 122888 | tf_op jit(solution)/shard_map/ppermute | solution.py:331
  23.9 8.4 %collective-permute-start.6 = (f32[2,2,40,128]{3,2,1,0:T(8,128)S(1)}, f32[2,2,40,128]{3,2,1,0:T(8,128)S(1)}, u32[]{:S(2)}, u32[]{:S(2)}) collective-permute-start(f32[2,2,40,128]{3,2,1,0:T(8,128)S(1)} %get-tuple-element.17), channel_id=1, source_target_pairs={{0,16},{2,18},{4,20},{6,22},{8,24},{10,26},{12,28},{14,30},{16,0},... | collective-permute-start | bytes 245768 | tf_op jit(solution)/shard_map/ppermute | solution.py:375
  24.3 8.0 %collective-permute-start.5 = (f32[2,2,40,128]{3,2,1,0:T(8,128)S(1)}, f32[2,2,40,128]{3,2,1,0:T(8,128)S(1)}, u32[]{:S(2)}, u32[]{:S(2)}) collective-permute-start(f32[2,2,40,128]{3,2,1,0:T(8,128)S(1)} %get-tuple-element.17), channel_id=1, source_target_pairs={{0,6},{2,4},{4,2},{6,0},{8,14},{10,12},{12,10},{14,8},{16,22},{18,... | collective-permute-start | bytes 245768 | tf_op jit(solution)/shard_map/ppermute | solution.py:372
  25.3 9.0 %collective-permute-start.4 = (f32[2,2,40,128]{3,2,1,0:T(8,128)S(1)}, f32[2,2,40,128]{3,2,1,0:T(8,128)S(1)}, u32[]{:S(2)}, u32[]{:S(2)}) collective-permute-start(f32[2,2,40,128]{3,2,1,0:T(8,128)S(1)} %get-tuple-element.17), channel_id=1, source_target_pairs={{0,4},{1,3},{2,6},{3,1},{4,0},{5,7},{6,2},{7,5},{8,12},{9,11},{10,... | collective-permute-start | bytes 245768 | tf_op jit(solution)/shard_map/ppermute | solution.py:371
  27.2 7.1 %collective-permute-start.3 = (f32[2,2,40,128]{3,2,1,0:T(8,128)S(1)}, f32[2,2,40,128]{3,2,1,0:T(8,128)S(1)}, u32[]{:S(2)}, u32[]{:S(2)}) collective-permute-start(f32[2,2,40,128]{3,2,1,0:T(8,128)S(1)} %get-tuple-element.17), channel_id=1, source_target_pairs={{0,2},{1,5},{2,0},{3,7},{4,6},{5,1},{6,4},{7,3},{8,10},{9,13},{10,... | collective-permute-start | bytes 245768 | tf_op jit(solution)/shard_map/ppermute | solution.py:370
  27.8 7.0 %collective-permute-start.7 = (f32[2,2,40,128]{3,2,1,0:T(8,128)S(1)}, f32[2,2,40,128]{3,2,1,0:T(8,128)S(1)}, u32[]{:S(2)}, u32[]{:S(2)}) collective-permute-start(f32[2,2,40,128]{3,2,1,0:T(8,128)S(1)} %get-tuple-element.17), channel_id=1, source_target_pairs={{0,24},{2,26},{4,28},{6,30},{8,16},{10,18},{12,20},{14,22},{16,8},... | collective-permute-start | bytes 245768 | tf_op jit(solution)/shard_map/ppermute | solution.py:375
  32.3 6.1 %collective-permute-start.2 = (f32[2,2,40,128]{3,2,1,0:T(8,128)S(1)}, f32[2,2,40,128]{3,2,1,0:T(8,128)S(1)}, u32[]{:S(2)}, u32[]{:S(2)}) collective-permute-start(f32[2,2,40,128]{3,2,1,0:T(8,128)S(1)} %get-tuple-element.17), channel_id=1, source_target_pairs={{0,8},{2,10},{4,12},{6,14},{8,0},{10,2},{12,4},{14,6},{16,24},{18,... | collective-permute-start | bytes 245768 | tf_op jit(solution)/shard_map/ppermute | solution.py:376
  32.3 6.3 %collective-permute-start.12 = (f32[2,2,40,128]{3,2,1,0:T(8,128)S(1)}, f32[2,2,40,128]{3,2,1,0:T(8,128)S(1)}, u32[]{:S(2)}, u32[]{:S(2)}) collective-permute-start(f32[2,2,40,128]{3,2,1,0:T(8,128)S(1)} %collective-permute-done.5.refs_2_), channel_id=1, source_target_pairs={{0,8},{2,10},{4,12},{6,14},{8,0},{10,2},{12,4},{14,6},{16,24},{18,... | collective-permute-start | bytes 245768 | tf_op jit(solution)/shard_map/ppermute | solution.py:376
  34.8 8.9 %copy-start.1 = (f32[2,2,16,1664]{3,2,1,0:T(8,128)S(1)}, f32[2,2,16,1664]{3,2,1,0:T(8,128)}, u32[]{:S(2)}) copy-start(f32[2,2,16,1664]{3,2,1,0:T(8,128)} %get-tuple-element.10.refs_12_) | copy-start | bytes 1277956
  34.9 8.9 %collective-permute-start.13 = (f32[2,2,2,40,128]{4,3,2,1,0:T(8,128)S(1)}, f32[2,2,2,40,128]{4,3,2,1,0:T(8,128)S(1)}, u32[]{:S(2)}, u32[]{:S(2)}) collective-permute-start(f32[2,2,2,40,128]{4,3,2,1,0:T(8,128)S(1)} %pack.1.after.refs_2_), channel_id=1, source_target_pairs={{0,6},{2,4},{4,2},{6,0},{8,14},{10,12},{12,10},{14,8},{16,22},{18,... | collective-permute-start | bytes 491528 | tf_op jit(solution)/shard_map/ppermute | solution.py:372
  35.9 7.8 %collective-permute-start.11 = (f32[2,2,2,40,128]{4,3,2,1,0:T(8,128)S(1)}, f32[2,2,2,40,128]{4,3,2,1,0:T(8,128)S(1)}, u32[]{:S(2)}, u32[]{:S(2)}) collective-permute-start(f32[2,2,2,40,128]{4,3,2,1,0:T(8,128)S(1)} %pack.1.after.refs_2_), channel_id=1, source_target_pairs={{0,4},{1,3},{2,6},{3,1},{4,0},{5,7},{6,2},{7,5},{8,12},{9,11},{10,... | collective-permute-start | bytes 491528 | tf_op jit(solution)/shard_map/ppermute | solution.py:371
  37.5 6.3 %collective-permute-start.9 = (f32[2,2,2,40,128]{4,3,2,1,0:T(8,128)S(1)}, f32[2,2,2,40,128]{4,3,2,1,0:T(8,128)S(1)}, u32[]{:S(2)}, u32[]{:S(2)}) collective-permute-start(f32[2,2,2,40,128]{4,3,2,1,0:T(8,128)S(1)} %pack.1.after.refs_2_), channel_id=1, source_target_pairs={{0,2},{1,5},{2,0},{3,7},{4,6},{5,1},{6,4},{7,3},{8,10},{9,13},{10,... | collective-permute-start | bytes 491528 | tf_op jit(solution)/shard_map/ppermute | solution.py:370
  38.4 5.0 %collective-permute-start.10 = (f32[2,2,40,128]{3,2,1,0:T(8,128)S(1)}, f32[2,2,40,128]{3,2,1,0:T(8,128)S(1)}, u32[]{:S(2)}, u32[]{:S(2)}) collective-permute-start(f32[2,2,40,128]{3,2,1,0:T(8,128)S(1)} %collective-permute-done.4.refs_1_), channel_id=1, source_target_pairs={{0,8},{2,10},{4,12},{6,14},{8,0},{10,2},{12,4},{14,6},{16,24},{18,... | collective-permute-start | bytes 245768 | tf_op jit(solution)/shard_map/ppermute | solution.py:376
  38.6 5.1 %collective-permute-start.8 = (f32[2,2,40,128]{3,2,1,0:T(8,128)S(1)}, f32[2,2,40,128]{3,2,1,0:T(8,128)S(1)}, u32[]{:S(2)}, u32[]{:S(2)}) collective-permute-start(f32[2,2,40,128]{3,2,1,0:T(8,128)S(1)} %collective-permute-done.3.refs_0_), channel_id=1, source_target_pairs={{0,8},{2,10},{4,12},{6,14},{8,0},{10,2},{12,4},{14,6},{16,24},{18,... | collective-permute-start | bytes 245768 | tf_op jit(solution)/shard_map/ppermute | solution.py:376
  40.5 2.4 %copy-start = (bf16[3328,768]{1,0:T(8,128)(2,1)S(1)}, bf16[3328,768]{1,0:T(8,128)(2,1)}, u32[]{:S(2)}) copy-start(bf16[3328,768]{1,0:T(8,128)(2,1)} %constant.14.clone.table_hbm) | copy-start | bytes 15335428
  48.4 1.9 %collective-permute-start.15 = (f32[1,36,4,768]{3,2,1,0:T(4,128)S(1)}, f32[1,36,4,768]{3,2,1,0:T(4,128)S(1)}, u32[]{:S(2)}, u32[]{:S(2)}) collective-permute-start(f32[1,36,4,768]{3,2,1,0:T(4,128)S(1)} %get-tuple-element.15), channel_id=1, source_target_pairs={{0,1},{1,0},{2,3},{3,2},{4,5},{5,4},{6,7},{7,6},{8,9},{9,8},{10,11... | collective-permute-start | bytes 1327112 | tf_op jit(solution)/shard_map/ppermute | solution.py:331
  48.5 2.6 %collective-permute-start.14 = (f32[1,36,4,768]{3,2,1,0:T(4,128)S(1)}, f32[1,36,4,768]{3,2,1,0:T(4,128)S(1)}, u32[]{:S(2)}, u32[]{:S(2)}) collective-permute-start(f32[1,36,4,768]{3,2,1,0:T(4,128)S(1)} %get-tuple-element.16), channel_id=1, source_target_pairs={{0,1},{1,0},{2,3},{3,2},{4,5},{5,4},{6,7},{7,6},{8,9},{9,8},{10,11... | collective-permute-start | bytes 1327112 | tf_op jit(solution)/shard_map/ppermute | solution.py:331

commit v7 on v6

--- a/solution.py
+++ b/solution.py
@@ -185,7 +185,8 @@
     place, core = lax.axis_index("sta") & 3, lax.axis_index("win")
     window, part = (place >> (1 - core)) & 1, (place >> core) & 1
     kinds = ((window, part), (part, window))
-    signs = [1.0 - 2.0 * p.astype(jnp.float32) for _, p in kinds]
+    turn = 1.0 - 2.0 * (window ^ part).astype(jnp.float32)
+    sign = 1.0 - 2.0 * part.astype(jnp.float32)
     for g in range(groups):
         for w in range(2):
             for p in range(2):
@@ -225,7 +226,7 @@
                             real[k] += a * ra + b * rb
                             part_imag[k] += b * ra - a * rb
                     for k in range(3):
-                        imag[k] += signs[g] * part_imag[k]
+                        imag[k] += part_imag[k] if g == 0 else turn * part_imag[k]
                 real_tiles += real
                 imag_tiles += imag
             at = pl.ds(block * 48, 48)
@@ -233,8 +234,8 @@
             lhs[at, pl.ds(pl.multiple_of(base, LANES), LANES)] = jnp.concatenate(
                 real_tiles, axis=0
             ).astype(jnp.bfloat16)
-            lhs[at, pl.ds(pl.multiple_of(base + LANES, LANES), LANES)] = jnp.concatenate(
-                imag_tiles, axis=0
+            lhs[at, pl.ds(pl.multiple_of(base + LANES, LANES), LANES)] = (
+                jnp.concatenate(imag_tiles, axis=0) * sign
             ).astype(jnp.bfloat16)
         return carry
 

time: 52.1 us -> 52.2 us (level)
  no operation moved by 1% of the time
where the time goes in v7:
time: 52.2 us; the launch traced here: 51.9 us
  starting transfers between devices  23.6 us (45%)
  waiting for transfers between devices  13 us (25%)
  Pallas kernels  10.6 us (20%)
  local copies, waits for them, and re-layouts  3.33 us (6%)
  other arithmetic  1.22 us (2%)
    all_to_all x1, waiting for transfers between devices, on_device(): got = lax.all_to_all(pieces, 'sta', 0, 0)  9.19 us
    all_to_all x1, starting transfers between devices, on_device(): got = lax.all_to_all(pieces, 'sta', 0, 0)  8.32 us
    pallas_call x1, Pallas kernels, correlate(): pl.pallas_call(functools.partial(correlate_kernel, count=count), out_shap...  4.55 us
    ppermute x4, starting transfers between devices, on_device(): second = [lax.ppermute(value, 'sta', partner(4)) for value in first]  4.05 us
    ppermute x2, starting transfers between devices, on_device(): far, farther = [lax.ppermute(mine, 'sta', partner(4 * k)) for k in (2, 3)]  3.43 us
    ppermute x2, starting transfers between devices, plane(): side = lax.ppermute(value, ('sta', 'win'), by_core(2, 1))  3.41 us
    unnamed x4, local copies, waits for them, and re-layouts  2.45 us
    pallas_call x1, Pallas kernels, whiten(): pl.pallas_call(whiten_kernel, out_shape=(jax.ShapeDtypeStruct((wins * sta...  2.4 us
  transfers between devices with their start and end apart: 17, of which 6 were waited for; matrix products, arithmetic and copies ran while one was open for 4% of the time, Pallas kernels for 4%

profile of v7, /device:TPU:0, one launch (start us, length us, event | category | flops | bytes accessed | tf_op | source)
XLA Modules:
  0.0 51.9 jit_solution(6912364955912215924)
XLA Ops:
  0.0 2.4 %whiten.1 = (f32[16,40,128]{2,1,0:T(8,128)}, f32[2,2,16,1664]{3,2,1,0:T(8,128)}) custom-call(s32[2,4]{1,0:T(2,128)} %flags_hbm.1, f32[2,4,3,2,1664]{4,3,2,1,0:T(2,128)} %bitcast.25), custom_call_target="tpu_custom_call" | custom-call | tf_op jit(solution)/shard_map/whiten/pallas_call | solution.py:95
  2.4 8.3 %all-to-all-start = ((f32[16,40,128]{2,1,0:T(8,128)}), f32[16,40,128]{2,1,0:T(8,128)S(1)}, u32[]{:S(2)}, u32[]{:S(2)}) async-start(f32[16,40,128]{2,1,0:T(8,128)} %get-tuple-element.9), calls=%async_computation | async-start | bytes 655360 | tf_op jit(solution)/shard_map/all_to_all | solution.py:359
  10.8 0.7 %reshape.20 = s32[2,2]{1,0:T(2,128)S(1)} reshape(s32[4]{0:T(128)} %param.7) | data formatting | bytes 32 | tf_op jit(solution)/shard_map/reshape | solution.py:341
  11.6 0.8 %broadcast_select_fusion = s32[2,1,4]{2,1,0:T(1,128)S(1)} fusion(pred[]{:T(512)S(6)} %eq.20, s32[2,2,4]{2,1,0:T(2,128)} %bitcast.28), kind=kLoop, calls=%fused_computation.2 | loop fusion | flops 8 | bytes 97 | tf_op jit(solution)/shard_map/jit(_where)/select_n | solution.py:344
  12.3 0.2 select_reduce_fusion
  12.5 0.1 reshape.22
  12.6 0.2 select_reduce_fusion.2
  12.9 9.2 %all-to-all-done.got_ref = f32[16,40,128]{2,1,0:T(8,128)S(1)} async-done(((f32[16,40,128]{2,1,0:T(8,128)}), f32[16,40,128]{2,1,0:T(8,128)S(1)}, u32[]{:S(2)}, u32[]{:S(2)}) %all-to-all-start) | async-done | bytes 327712 | tf_op jit(solution)/shard_map/all_to_all | solution.py:359
  22.1 0.6 %pick.1 = (f32[2,40,128]{2,1,0:T(8,128)S(1)}, f32[2,40,128]{2,1,0:T(8,128)S(1)}) custom-call(s32[12]{0:T(128)S(1)} %pad_add_fusion.params, f32[16,40,128]{2,1,0:T(8,128)S(1)} %all-to-all-done.got_ref, f32[2,2,16,1664]{3,2,1,0:T(8,128)S(1)} %collective-permute-done.before.refs_13_), custom_call_target="tpu_custom_call" | custom-call | tf_op jit(solution)/shard_map/pick/pallas_call | solution.py:127
  22.7 1.2 %collective-permute-done.1 = f32[2,40,128]{2,1,0:T(8,128)S(1)} collective-permute-done((f32[2,40,128]{2,1,0:T(8,128)S(1)}, f32[2,40,128]{2,1,0:T(8,128)S(1)}, u32[]{:S(2)}, u32[]{:S(2)}) %collective-permute-start.1) | collective-permute-done | bytes 40992 | tf_op jit(solution)/shard_map/ppermute | solution.py:332
  23.9 0.4 collective-permute-start.6
  24.3 1.0 %collective-permute-start.5 = (f32[2,2,40,128]{3,2,1,0:T(8,128)S(1)}, f32[2,2,40,128]{3,2,1,0:T(8,128)S(1)}, u32[]{:S(2)}, u32[]{:S(2)}) collective-permute-start(f32[2,2,40,128]{3,2,1,0:T(8,128)S(1)} %get-tuple-element.17), channel_id=1, source_target_pairs={{0,6},{2,4},{4,2},{6,0},{8,14},{10,12},{12,10},{14,8},{16,22},{18,... | collective-permute-start | bytes 245768 | tf_op jit(solution)/shard_map/ppermute | solution.py:373
  25.3 1.9 %collective-permute-start.4 = (f32[2,2,40,128]{3,2,1,0:T(8,128)S(1)}, f32[2,2,40,128]{3,2,1,0:T(8,128)S(1)}, u32[]{:S(2)}, u32[]{:S(2)}) collective-permute-start(f32[2,2,40,128]{3,2,1,0:T(8,128)S(1)} %get-tuple-element.17), channel_id=1, source_target_pairs={{0,4},{1,3},{2,6},{3,1},{4,0},{5,7},{6,2},{7,5},{8,12},{9,11},{10,... | collective-permute-start | bytes 245768 | tf_op jit(solution)/shard_map/ppermute | solution.py:372
  27.2 0.6 %collective-permute-start.3 = (f32[2,2,40,128]{3,2,1,0:T(8,128)S(1)}, f32[2,2,40,128]{3,2,1,0:T(8,128)S(1)}, u32[]{:S(2)}, u32[]{:S(2)}) collective-permute-start(f32[2,2,40,128]{3,2,1,0:T(8,128)S(1)} %get-tuple-element.17), channel_id=1, source_target_pairs={{0,2},{1,5},{2,0},{3,7},{4,6},{5,1},{6,4},{7,3},{8,10},{9,13},{10,... | collective-permute-start | bytes 245768 | tf_op jit(solution)/shard_map/ppermute | solution.py:371
  27.8 3.0 %collective-permute-start.7 = (f32[2,2,40,128]{3,2,1,0:T(8,128)S(1)}, f32[2,2,40,128]{3,2,1,0:T(8,128)S(1)}, u32[]{:S(2)}, u32[]{:S(2)}) collective-permute-start(f32[2,2,40,128]{3,2,1,0:T(8,128)S(1)} %get-tuple-element.17), channel_id=1, source_target_pairs={{0,24},{2,26},{4,28},{6,30},{8,16},{10,18},{12,20},{14,22},{16,8},... | collective-permute-start | bytes 245768 | tf_op jit(solution)/shard_map/ppermute | solution.py:376
  30.8 1.5 %collective-permute-done.6.refs_3_ = f32[2,2,40,128]{3,2,1,0:T(8,128)S(1)} collective-permute-done((f32[2,2,40,128]{3,2,1,0:T(8,128)S(1)}, f32[2,2,40,128]{3,2,1,0:T(8,128)S(1)}, u32[]{:S(2)}, u32[]{:S(2)}) %collective-permute-start.6) | collective-permute-done | bytes 81952 | tf_op jit(solution)/shard_map/ppermute | solution.py:376
  32.3 2.0 %collective-permute-start.12 = (f32[2,2,40,128]{3,2,1,0:T(8,128)S(1)}, f32[2,2,40,128]{3,2,1,0:T(8,128)S(1)}, u32[]{:S(2)}, u32[]{:S(2)}) collective-permute-start(f32[2,2,40,128]{3,2,1,0:T(8,128)S(1)} %collective-permute-done.5.refs_2_), channel_id=1, source_target_pairs={{0,8},{2,10},{4,12},{6,14},{8,0},{10,2},{12,4},{14,6},{16,24},{18,... | collective-permute-start | bytes 245768 | tf_op jit(solution)/shard_map/ppermute | solution.py:377
  34.4 0.5 collective-permute-done.7.refs_4_
  34.9 1.1 %collective-permute-start.13 = (f32[2,2,2,40,128]{4,3,2,1,0:T(8,128)S(1)}, f32[2,2,2,40,128]{4,3,2,1,0:T(8,128)S(1)}, u32[]{:S(2)}, u32[]{:S(2)}) collective-permute-start(f32[2,2,2,40,128]{4,3,2,1,0:T(8,128)S(1)} %pack.1.after.refs_2_), channel_id=1, source_target_pairs={{0,6},{2,4},{4,2},{6,0},{8,14},{10,12},{12,10},{14,8},{16,22},{18,... | collective-permute-start | bytes 491528 | tf_op jit(solution)/shard_map/ppermute | solution.py:373
  35.9 1.5 %collective-permute-start.11 = (f32[2,2,2,40,128]{4,3,2,1,0:T(8,128)S(1)}, f32[2,2,2,40,128]{4,3,2,1,0:T(8,128)S(1)}, u32[]{:S(2)}, u32[]{:S(2)}) collective-permute-start(f32[2,2,2,40,128]{4,3,2,1,0:T(8,128)S(1)} %pack.1.after.refs_2_), channel_id=1, source_target_pairs={{0,4},{1,3},{2,6},{3,1},{4,0},{5,7},{6,2},{7,5},{8,12},{9,11},{10,... | collective-permute-start | bytes 491528 | tf_op jit(solution)/shard_map/ppermute | solution.py:372
  37.5 0.9 %collective-permute-start.9 = (f32[2,2,2,40,128]{4,3,2,1,0:T(8,128)S(1)}, f32[2,2,2,40,128]{4,3,2,1,0:T(8,128)S(1)}, u32[]{:S(2)}, u32[]{:S(2)}) collective-permute-start(f32[2,2,2,40,128]{4,3,2,1,0:T(8,128)S(1)} %pack.1.after.refs_2_), channel_id=1, source_target_pairs={{0,2},{1,5},{2,0},{3,7},{4,6},{5,1},{6,4},{7,3},{8,10},{9,13},{10,... | collective-permute-start | bytes 491528 | tf_op jit(solution)/shard_map/ppermute | solution.py:371
  38.4 0.2 collective-permute-start.10
  38.6 1.9 %collective-permute-start.8 = (f32[2,2,40,128]{3,2,1,0:T(8,128)S(1)}, f32[2,2,40,128]{3,2,1,0:T(8,128)S(1)}, u32[]{:S(2)}, u32[]{:S(2)}) collective-permute-start(f32[2,2,40,128]{3,2,1,0:T(8,128)S(1)} %collective-permute-done.3.refs_0_), channel_id=1, source_target_pairs={{0,8},{2,10},{4,12},{6,14},{8,0},{10,2},{12,4},{14,6},{16,24},{18,... | collective-permute-start | bytes 245768 | tf_op jit(solution)/shard_map/ppermute | solution.py:377
  40.5 2.4 %copy-done = bf16[3328,768]{1,0:T(8,128)(2,1)S(1)} copy-done((bf16[3328,768]{1,0:T(8,128)(2,1)S(1)}, bf16[3328,768]{1,0:T(8,128)(2,1)}, u32[]{:S(2)}) %copy-start) | copy-done | bytes 5111832
  42.9 0.5 load.1.refs_14_
  43.4 0.3 collective-permute-done.8
  43.8 4.5 %correlate.1.own = f32[2,36,4,768]{3,2,1,0:T(4,128)S(1)} custom-call(s32[12]{0:T(128)S(1)} %pad_add_fusion.params, f32[1,2,2,40,128]{4,3,2,1,0:T(8,128)S(1)} %get-tuple-element.18.refs_0_, f32[1,2,2,40,128]{4,3,2,1,0:T(8,128)S(1)} %bitcast.20, f32[2,2,2,40,128]{4,3,2,1,0:T(8,128)S(1)} %pack.1.after.refs_2_, f32[1,2,2,40,128]{4,3,2,1,0:T(8,128)S(1)} %bitcast.19, ...), custom_call_target="tpu_custom_call" | custom-call | flops 1472200704 | bytes 8388608 | tf_op jit(solution)/shard_map/correlate/pallas_call | solution.py:262
  48.5 0.5 collective-permute-start.14
  49.0 1.0 %put.1.whole = f32[4,36,4,768]{3,2,1,0:T(4,128)} custom-call(f32[2,36,4,768]{3,2,1,0:T(4,128)S(1)} %correlate.1.own), custom_call_target="tpu_custom_call" | custom-call | tf_op jit(solution)/shard_map/put/pallas_call | solution.py:302
  49.9 0.3 collective-permute-done.15.other
  50.3 0.8 %join.2.whole = f32[4,36,4,768]{3,2,1,0:T(4,128)} custom-call(f32[1,36,4,768]{3,2,1,0:T(4,128)S(1)} %collective-permute-done.15.other, f32[4,36,4,768]{3,2,1,0:T(4,128)} %put.1.whole), custom_call_target="tpu_custom_call", output_to_operand_aliasing={{}: (1, {})} | custom-call | tf_op jit(solution)/shard_map/join/pallas_call | solution.py:319
  51.1 0.8 %join.3 = f32[4,36,4,768]{3,2,1,0:T(4,128)} custom-call(f32[1,36,4,768]{3,2,1,0:T(4,128)S(1)} %collective-permute-done.14.other, f32[4,36,4,768]{3,2,1,0:T(4,128)} %join.2.whole), custom_call_target="tpu_custom_call", output_to_operand_aliasing={{}: (1, {})} | custom-call | tf_op jit(solution)/shard_map/join/pallas_call | solution.py:319
  (23 shorter events, 0.4 us)
Async XLA Ops:
  2.4 19.6 %all-to-all-start = ((f32[16,40,128]{2,1,0:T(8,128)}), f32[16,40,128]{2,1,0:T(8,128)S(1)}, u32[]{:S(2)}, u32[]{:S(2)}) async-start(f32[16,40,128]{2,1,0:T(8,128)} %get-tuple-element.9), calls=%async_computation | async-start | bytes 655360 | tf_op jit(solution)/shard_map/all_to_all | solution.py:359
  10.7 2.1 %collective-permute-start = (f32[2,2,16,1664]{3,2,1,0:T(8,128)}, f32[2,2,16,1664]{3,2,1,0:T(8,128)S(1)}, u32[]{:S(2)}, u32[]{:S(2)}) collective-permute-start(f32[2,2,16,1664]{3,2,1,0:T(8,128)} %get-tuple-element.10.refs_12_), channel_id=1, source_target_pairs={{0,1},{1,0},{2,3},{3,2},{4,5},{5,4},{6,7},{7,6},{8,9},{9,8},{10,11... | collective-permute-start | bytes 1277960 | tf_op jit(solution)/shard_map/ppermute | solution.py:332
  22.6 1.3 %collective-permute-start.1 = (f32[2,40,128]{2,1,0:T(8,128)S(1)}, f32[2,40,128]{2,1,0:T(8,128)S(1)}, u32[]{:S(2)}, u32[]{:S(2)}) collective-permute-start(f32[2,40,128]{2,1,0:T(8,128)S(1)} %get-tuple-element.12), channel_id=1, source_target_pairs={{0,1},{1,0},{2,3},{3,2},{4,5},{5,4},{6,7},{7,6},{8,9},{9,8},{10,11... | collective-permute-start | bytes 122888 | tf_op jit(solution)/shard_map/ppermute | solution.py:332
  23.9 8.4 %collective-permute-start.6 = (f32[2,2,40,128]{3,2,1,0:T(8,128)S(1)}, f32[2,2,40,128]{3,2,1,0:T(8,128)S(1)}, u32[]{:S(2)}, u32[]{:S(2)}) collective-permute-start(f32[2,2,40,128]{3,2,1,0:T(8,128)S(1)} %get-tuple-element.17), channel_id=1, source_target_pairs={{0,16},{2,18},{4,20},{6,22},{8,24},{10,26},{12,28},{14,30},{16,0},... | collective-permute-start | bytes 245768 | tf_op jit(solution)/shard_map/ppermute | solution.py:376
  24.3 8.0 %collective-permute-start.5 = (f32[2,2,40,128]{3,2,1,0:T(8,128)S(1)}, f32[2,2,40,128]{3,2,1,0:T(8,128)S(1)}, u32[]{:S(2)}, u32[]{:S(2)}) collective-permute-start(f32[2,2,40,128]{3,2,1,0:T(8,128)S(1)} %get-tuple-element.17), channel_id=1, source_target_pairs={{0,6},{2,4},{4,2},{6,0},{8,14},{10,12},{12,10},{14,8},{16,22},{18,... | collective-permute-start | bytes 245768 | tf_op jit(solution)/shard_map/ppermute | solution.py:373
  25.3 9.0 %collective-permute-start.4 = (f32[2,2,40,128]{3,2,1,0:T(8,128)S(1)}, f32[2,2,40,128]{3,2,1,0:T(8,128)S(1)}, u32[]{:S(2)}, u32[]{:S(2)}) collective-permute-start(f32[2,2,40,128]{3,2,1,0:T(8,128)S(1)} %get-tuple-element.17), channel_id=1, source_target_pairs={{0,4},{1,3},{2,6},{3,1},{4,0},{5,7},{6,2},{7,5},{8,12},{9,11},{10,... | collective-permute-start | bytes 245768 | tf_op jit(solution)/shard_map/ppermute | solution.py:372
  27.2 7.1 %collective-permute-start.3 = (f32[2,2,40,128]{3,2,1,0:T(8,128)S(1)}, f32[2,2,40,128]{3,2,1,0:T(8,128)S(1)}, u32[]{:S(2)}, u32[]{:S(2)}) collective-permute-start(f32[2,2,40,128]{3,2,1,0:T(8,128)S(1)} %get-tuple-element.17), channel_id=1, source_target_pairs={{0,2},{1,5},{2,0},{3,7},{4,6},{5,1},{6,4},{7,3},{8,10},{9,13},{10,... | collective-permute-start | bytes 245768 | tf_op jit(solution)/shard_map/ppermute | solution.py:371
  27.8 7.0 %collective-permute-start.7 = (f32[2,2,40,128]{3,2,1,0:T(8,128)S(1)}, f32[2,2,40,128]{3,2,1,0:T(8,128)S(1)}, u32[]{:S(2)}, u32[]{:S(2)}) collective-permute-start(f32[2,2,40,128]{3,2,1,0:T(8,128)S(1)} %get-tuple-element.17), channel_id=1, source_target_pairs={{0,24},{2,26},{4,28},{6,30},{8,16},{10,18},{12,20},{14,22},{16,8},... | collective-permute-start | bytes 245768 | tf_op jit(solution)/shard_map/ppermute | solution.py:376
  32.3 6.1 %collective-permute-start.2 = (f32[2,2,40,128]{3,2,1,0:T(8,128)S(1)}, f32[2,2,40,128]{3,2,1,0:T(8,128)S(1)}, u32[]{:S(2)}, u32[]{:S(2)}) collective-permute-start(f32[2,2,40,128]{3,2,1,0:T(8,128)S(1)} %get-tuple-element.17), channel_id=1, source_target_pairs={{0,8},{2,10},{4,12},{6,14},{8,0},{10,2},{12,4},{14,6},{16,24},{18,... | collective-permute-start | bytes 245768 | tf_op jit(solution)/shard_map/ppermute | solution.py:377
  32.3 6.3 %collective-permute-start.12 = (f32[2,2,40,128]{3,2,1,0:T(8,128)S(1)}, f32[2,2,40,128]{3,2,1,0:T(8,128)S(1)}, u32[]{:S(2)}, u32[]{:S(2)}) collective-permute-start(f32[2,2,40,128]{3,2,1,0:T(8,128)S(1)} %collective-permute-done.5.refs_2_), channel_id=1, source_target_pairs={{0,8},{2,10},{4,12},{6,14},{8,0},{10,2},{12,4},{14,6},{16,24},{18,... | collective-permute-start | bytes 245768 | tf_op jit(solution)/shard_map/ppermute | solution.py:377
  34.8 8.9 %copy-start.1 = (f32[2,2,16,1664]{3,2,1,0:T(8,128)S(1)}, f32[2,2,16,1664]{3,2,1,0:T(8,128)}, u32[]{:S(2)}) copy-start(f32[2,2,16,1664]{3,2,1,0:T(8,128)} %get-tuple-element.10.refs_12_) | copy-start | bytes 1277956
  34.9 8.9 %collective-permute-start.13 = (f32[2,2,2,40,128]{4,3,2,1,0:T(8,128)S(1)}, f32[2,2,2,40,128]{4,3,2,1,0:T(8,128)S(1)}, u32[]{:S(2)}, u32[]{:S(2)}) collective-permute-start(f32[2,2,2,40,128]{4,3,2,1,0:T(8,128)S(1)} %pack.1.after.refs_2_), channel_id=1, source_target_pairs={{0,6},{2,4},{4,2},{6,0},{8,14},{10,12},{12,10},{14,8},{16,22},{18,... | collective-permute-start | bytes 491528 | tf_op jit(solution)/shard_map/ppermute | solution.py:373
  35.9 7.8 %collective-permute-start.11 = (f32[2,2,2,40,128]{4,3,2,1,0:T(8,128)S(1)}, f32[2,2,2,40,128]{4,3,2,1,0:T(8,128)S(1)}, u32[]{:S(2)}, u32[]{:S(2)}) collective-permute-start(f32[2,2,2,40,128]{4,3,2,1,0:T(8,128)S(1)} %pack.1.after.refs_2_), channel_id=1, source_target_pairs={{0,4},{1,3},{2,6},{3,1},{4,0},{5,7},{6,2},{7,5},{8,12},{9,11},{10,... | collective-permute-start | bytes 491528 | tf_op jit(solution)/shard_map/ppermute | solution.py:372
  37.5 6.3 %collective-permute-start.9 = (f32[2,2,2,40,128]{4,3,2,1,0:T(8,128)S(1)}, f32[2,2,2,40,128]{4,3,2,1,0:T(8,128)S(1)}, u32[]{:S(2)}, u32[]{:S(2)}) collective-permute-start(f32[2,2,2,40,128]{4,3,2,1,0:T(8,128)S(1)} %pack.1.after.refs_2_), channel_id=1, source_target_pairs={{0,2},{1,5},{2,0},{3,7},{4,6},{5,1},{6,4},{7,3},{8,10},{9,13},{10,... | collective-permute-start | bytes 491528 | tf_op jit(solution)/shard_map/ppermute | solution.py:371
  38.4 5.0 %collective-permute-start.10 = (f32[2,2,40,128]{3,2,1,0:T(8,128)S(1)}, f32[2,2,40,128]{3,2,1,0:T(8,128)S(1)}, u32[]{:S(2)}, u32[]{:S(2)}) collective-permute-start(f32[2,2,40,128]{3,2,1,0:T(8,128)S(1)} %collective-permute-done.4.refs_1_), channel_id=1, source_target_pairs={{0,8},{2,10},{4,12},{6,14},{8,0},{10,2},{12,4},{14,6},{16,24},{18,... | collective-permute-start | bytes 245768 | tf_op jit(solution)/shard_map/ppermute | solution.py:377
  38.6 5.1 %collective-permute-start.8 = (f32[2,2,40,128]{3,2,1,0:T(8,128)S(1)}, f32[2,2,40,128]{3,2,1,0:T(8,128)S(1)}, u32[]{:S(2)}, u32[]{:S(2)}) collective-permute-start(f32[2,2,40,128]{3,2,1,0:T(8,128)S(1)} %collective-permute-done.3.refs_0_), channel_id=1, source_target_pairs={{0,8},{2,10},{4,12},{6,14},{8,0},{10,2},{12,4},{14,6},{16,24},{18,... | collective-permute-start | bytes 245768 | tf_op jit(solution)/shard_map/ppermute | solution.py:377
  40.5 2.4 %copy-start = (bf16[3328,768]{1,0:T(8,128)(2,1)S(1)}, bf16[3328,768]{1,0:T(8,128)(2,1)}, u32[]{:S(2)}) copy-start(bf16[3328,768]{1,0:T(8,128)(2,1)} %constant.14.clone.table_hbm) | copy-start | bytes 15335428
  48.4 1.9 %collective-permute-start.15 = (f32[1,36,4,768]{3,2,1,0:T(4,128)S(1)}, f32[1,36,4,768]{3,2,1,0:T(4,128)S(1)}, u32[]{:S(2)}, u32[]{:S(2)}) collective-permute-start(f32[1,36,4,768]{3,2,1,0:T(4,128)S(1)} %get-tuple-element.15), channel_id=1, source_target_pairs={{0,1},{1,0},{2,3},{3,2},{4,5},{5,4},{6,7},{7,6},{8,9},{9,8},{10,11... | collective-permute-start | bytes 1327112 | tf_op jit(solution)/shard_map/ppermute | solution.py:332
  48.5 2.6 %collective-permute-start.14 = (f32[1,36,4,768]{3,2,1,0:T(4,128)S(1)}, f32[1,36,4,768]{3,2,1,0:T(4,128)S(1)}, u32[]{:S(2)}, u32[]{:S(2)}) collective-permute-start(f32[1,36,4,768]{3,2,1,0:T(4,128)S(1)} %get-tuple-element.16), channel_id=1, source_target_pairs={{0,1},{1,0},{2,3},{3,2},{4,5},{5,4},{6,7},{7,6},{8,9},{9,8},{10,11... | collective-permute-start | bytes 1327112 | tf_op jit(solution)/shard_map/ppermute | solution.py:332
